TPU v7x, 256 devices: a whole 4x4x8 slice. The times are simulated.
256 devices in a mesh: seq: 16 (over y, x), sec: 2 (over z_hi), mp: 8 (over z_lo, core).
Axes of the slice: x: 4, y: 4, z: 8 (z_hi: 2, z_lo: 4; z = z_hi * 4 + z_lo), core: 2. Of those that a mesh axis runs over, the one named last changes fastest.
Arguments:
- mantissas: bfloat16 [2, 4096, 4096], P('sec', 'seq', 'mp'), may hold values from -6 to 6
- exponents: int32 [2, 4096, 32], P('sec', 'seq', 'mp'), may hold values from -2 to 1
- source_lengths: int32 [3], replicated, may hold values from 1 to 3072, 4096 in all
- target_lengths: int32 [3], replicated, may hold values from 1 to 3072, 4096 in all
- norm_gains: float32 [2, 2, 4096], P('sec'), may hold values from 0.1 to 1.9
- self_weights: bfloat16 [2, 3, 4096, 2048], P('sec', None, None, 'mp'), may hold values from -3.125 to 3.125
- self_output: bfloat16 [2, 2048, 4096], P('sec', 'mp'), may hold values from -1 to 1
- cross_weights: bfloat16 [2, 2, 4096, 2048], P('sec', None, None, 'mp'), may hold values from -3.125 to 3.125
Outputs:
- layer_out: float32 [2, 4096, 4096], P('sec', 'seq', 'mp')
Inputs may be any that keep to these rules, and one draw needn't show every extreme that they name: `source_lengths`: 3 positive lengths summing to 4096; the longest is exactly 3072. `target_lengths`: 3 positive lengths summing to 4096; the longest is exactly 3072.
All inputs are finite; a program needn't handle non-finite values.
Results may differ from a plain program's by a relative error of at most 0.025.
Values may be sent and summed in bfloat16 or wider, within the bound.
A program may use at most 128 MiB of HBM per device.

v0:
```python
import math

import jax
import jax.numpy as jnp
from jax import lax
from jax.sharding import PartitionSpec as P

HD = 64
EXP_BLOCK = 128


epsilon = 1e-06


def shifted(value, axis, steps):
    count = lax.axis_size(axis)
    initial, last = (max(0, -steps), min(count, count - steps))
    return lax.ppermute(value, axis, [(source, source + steps) for source in range(initial, last)])


def sylvester(order):
    matrix = jnp.ones((1, 1), jnp.float32)
    base = jnp.array([[1.0, 1.0], [1.0, -1.0]], jnp.float32)
    while matrix.shape[0] < order:
        matrix = jnp.kron(matrix, base)
    return matrix / math.sqrt(order)


def decode_blocks(mantissa, exponent):
    row_count = mantissa.shape[0]
    width = mantissa.shape[1]
    scaling = jnp.exp2(exponent.astype(jnp.float32))
    blocked = mantissa.astype(jnp.float32).reshape(row_count, width // EXP_BLOCK, EXP_BLOCK)
    return (blocked * scaling[:, :, None]).reshape(row_count, width)


def rms_norm(values, gain):
    power = jnp.mean(values * values, axis=-1, keepdims=True)
    return (values * lax.rsqrt(power + epsilon) * gain).astype(jnp.bfloat16)


def rotate(values, rotation):
    heads_count = values.shape[-1] // HD
    pieces = values.reshape(values.shape[:-1] + (heads_count, HD))
    turned = jnp.einsum("...hd,de->...he", pieces, rotation, precision=lax.Precision.HIGHEST)
    return turned.reshape(values.shape).astype(jnp.bfloat16)


def document_of(position, lengths):
    bounds = jnp.cumsum(lengths)
    return jnp.sum((position[:, None] >= bounds[None, :]).astype(jnp.int32), axis=1)


def empty_state(queries):
    row_count = queries.shape[0]
    heads_count = queries.shape[1] // HD
    return (
        jnp.full((heads_count, row_count), -jnp.inf, jnp.float32),
        jnp.zeros((heads_count, row_count), jnp.float32),
        jnp.zeros((heads_count, row_count, HD), jnp.float32),
    )


def make_fold(queries, query_rows, query_docs, key_lengths, causal, masked):
    row_count = queries.shape[0]
    heads_count = queries.shape[1] // HD
    split_queries = queries.reshape(row_count, heads_count, HD)

    def accumulate(carried, incoming, first_key):
        top_score, denominator, numerator = carried
        key_block, value_block = incoming
        key_count = key_block.shape[0]
        if masked:
            key_rows = jnp.arange(key_count, dtype=jnp.int32)
            key_docs = document_of(key_rows, key_lengths)
            allowed = query_docs[:, None] == key_docs[None, :]
            allowed = allowed & (
                jnp.logical_not(causal) | (key_rows[None, :] <= query_rows[:, None])
            )
        else:
            allowed = jnp.ones((row_count, key_count), bool)
        scores = jnp.einsum(
            "rhd,khd->hrk",
            split_queries,
            key_block.reshape(key_count, heads_count, HD),
            preferred_element_type=jnp.float32,
        ) * HD ** (-0.5)
        scores = jnp.where(allowed[None], scores, -jnp.inf)
        new_top = jnp.max(scores, axis=2)
        anchor = jnp.where(new_top == -jnp.inf, 0.0, new_top)
        weights = jnp.where(allowed[None], jnp.exp(scores - anchor[:, :, None]), 0.0)
        rescale = jnp.exp(top_score - anchor)
        denominator = denominator * rescale + jnp.sum(weights, axis=2)
        numerator = numerator * rescale[:, :, None] + jnp.einsum(
            "hrk,khd->hrd",
            weights.astype(jnp.bfloat16),
            value_block.reshape(key_count, heads_count, HD),
            preferred_element_type=jnp.float32,
        )
        return (new_top, denominator, numerator)

    return accumulate


def finish(carried, rotation):
    top_score, denominator, numerator = carried
    mixed = numerator / denominator[:, :, None]
    turned = jnp.einsum("hrd,de->rhe", mixed, rotation, precision=lax.Precision.HIGHEST)
    return turned.reshape(turned.shape[0], -1).astype(jnp.bfloat16)


def body(
    mantissas,
    exponents,
    source_lengths,
    target_lengths,
    norm_gains,
    self_weights,
    self_output,
    cross_weights,
):
    rotation = sylvester(HD)
    is_decoder = lax.axis_index("sec") == 1
    row_count = mantissas.shape[1]
    first_row = lax.axis_index("seq") * row_count
    own_rows = first_row + jnp.arange(row_count, dtype=jnp.int32)
    mant_full, exp_full = (
        lax.all_gather(mantissas[0], "mp", axis=1, tiled=True),
        lax.all_gather(exponents[0], "mp", axis=1, tiled=True),
    )
    inputs = decode_blocks(mant_full, exp_full)
    local_inputs = decode_blocks(mantissas[0], exponents[0])
    normed = rms_norm(inputs, norm_gains[0, 0])
    projected = jnp.einsum(
        "rd,kdc->krc", normed, self_weights[0], preferred_element_type=jnp.float32
    )
    rotated = rotate(projected, rotation)
    queries = rotated[0]
    own_lengths = jnp.where(is_decoder, target_lengths, source_lengths)
    own_docs = document_of(own_rows, own_lengths)
    self_fold = make_fold(queries, own_rows, own_docs, own_lengths, is_decoder, True)
    carried = self_fold(
        empty_state(queries),
        (
            lax.all_gather(rotated[1], "seq", axis=0, tiled=True),
            lax.all_gather(rotated[2], "seq", axis=0, tiled=True),
        ),
        jnp.int32(0),
    )
    self_mixed = finish(carried, rotation)
    self_terms = jnp.dot(self_mixed, self_output[0], preferred_element_type=jnp.float32)
    shares = lax.psum_scatter(self_terms, "mp", scatter_dimension=1, tiled=True)
    local_rows = local_inputs + shares
    layer_rows = lax.all_gather(local_rows, "mp", axis=1, tiled=True)
    cross_normed = rms_norm(layer_rows, norm_gains[0, 1])
    first_product = rotate(
        jnp.dot(cross_normed, cross_weights[0, 0], preferred_element_type=jnp.float32), rotation
    )

    def second_projection(source):
        return rotate(
            jnp.dot(source, cross_weights[0, 1], preferred_element_type=jnp.float32), rotation
        )

    def skipped_projection(source):
        return jnp.zeros((row_count, cross_weights.shape[3]), jnp.bfloat16)

    second_product = lax.cond(is_decoder, skipped_projection, second_projection, cross_normed)
    pairs = jnp.stack([first_product, second_product])
    arrived = shifted(pairs, "sec", 1)
    cross_fold = make_fold(first_product, None, None, None, None, False)
    carried = cross_fold(
        empty_state(first_product),
        (
            lax.all_gather(arrived[0], "seq", axis=0, tiled=True),
            lax.all_gather(arrived[1], "seq", axis=0, tiled=True),
        ),
        jnp.int32(0),
    )
    cross_mixed = finish(carried, rotation)

    def cross_output(mixed):
        return lax.dot_general(
            mixed, cross_weights[0, 1], (((1,), (1,)), ((), ())), preferred_element_type=jnp.float32
        )

    def empty_output(mixed):
        return jnp.zeros((row_count, cross_weights.shape[2]), jnp.float32)

    cross_terms = lax.cond(is_decoder, cross_output, empty_output, cross_mixed)
    cross_shares = lax.psum_scatter(cross_terms, "mp", scatter_dimension=1, tiled=True)
    decoded = local_rows + cross_shares
    result = jnp.where(is_decoder, decoded, local_rows)
    return result[None]


def solution(mesh):
    in_specs = (
        P("sec", "seq", "mp"),
        P("sec", "seq", "mp"),
        P(),
        P(),
        P("sec", None, None),
        P("sec", None, None, "mp"),
        P("sec", "mp", None),
        P("sec", None, None, "mp"),
    )
    out_specs = P("sec", "seq", "mp")
    return jax.shard_map(body, mesh=mesh, in_specs=in_specs, out_specs=out_specs, check_vma=False)
```

profile of v0, /device:TPU:129, one launch (start us, length us, event | category | flops | bytes accessed | tf_op | source)
XLA Modules:
  0.0 503.4 jit_solution(10908247503762912736)
XLA Ops:
  8.0 14.5 %all-gather.1 = s32[1,256,32]{1,0,2:T(1,128)S(1)} all-gather(s32[1,256,4]{1,0,2:T(1,128)S(1)} %copy.40), channel_id=3, replica_groups=mesh['seq'=16,'sec'=2,'mp'=8] {'mp'}, dimensions={2}, use_global_device_ids=true | all-gather | bytes 36864 | tf_op jit(solution)/shard_map/all_gather | solution.py:129
  22.6 0.8 broadcast_multiply_fusion.3
  26.1 0.9 multiply_multiply_fusion
  27.0 1.3 div.32
  28.3 0.9 fusion.58
  29.2 17.2 %all-gather.17.cloned.1.call-done = bf16[1,256,4096]{2,1,0:T(8,128)(2,1)} async-done(((bf16[1,256,512]{2,1,0:T(8,128)(2,1)}), bf16[1,256,4096]{2,1,0:T(8,128)(2,1)}) %all-gather.17.cloned.1.call-update) | async-done | bytes 2097168 | tf_op jit(solution)/shard_map/all_gather | solution.py:128
  46.4 1.1 mul.252
  48.0 2.4 multiply_reduce_fusion.2
  50.4 6.9 %fusion.16 = f32[256,3,256]{0,2,1:T(8,128)S(1)} fusion(bf16[1,3,4096,256]{3,2,1,0:T(8,128)(2,1)} %param.18, f32[32,8,32,128]{3,2,1,0:T(8,128)S(1)} %bitcast.121, bf16[1,256,4096]{2,1,0:T(8,128)(2,1)S(1)} %copy-done.5, f32[4096]{0:T(1024)S(1)} %bitcast.136, f32[256]{0:T(256)S(1)} %add_rsqrt_fusion.1), kind=kOutput, calls=%fused_computation.19 | convolution fusion | flops 1615855616 | bytes 13386752 | tf_op jit(solution)/shard_map/rd,kdc->krc/dot_general | solution.py:134
  60.3 1.4 fusion.19
  61.6 52.2 %all-gather.11.cloned.1.call-done = bf16[4096,256]{0,1:T(8,128)(2,1)} async-done(((bf16[256,256]{0,1:T(8,128)(2,1)}), bf16[4096,256]{0,1:T(8,128)(2,1)}) %all-gather.11.cloned.1.call-update) | async-done | bytes 2097168 | tf_op jit(solution)/shard_map/all_gather | solution.py:145
  113.8 4.6 fusion.6
  118.4 5.0 fusion.9
  124.1 44.2 %all-gather.13.cloned.1.call-done = bf16[4096,256]{0,1:T(8,128)(2,1)} async-done(((bf16[256,256]{0,1:T(8,128)(2,1)}), bf16[4096,256]{0,1:T(8,128)(2,1)}) %all-gather.13.cloned.1.call-update) | async-done | bytes 2097168 | tf_op jit(solution)/shard_map/all_gather | solution.py:146
  168.3 8.7 %fusion.36 = f32[4,256,64]{1,2,0:T(8,128)S(1)} fusion(bf16[4096,4,64]{0,2,1:T(8,128)(2,1)} %bitcast.139, f32[4,256,4096]{2,1,0:T(8,128)} %copy-done.2, f32[4,256]{1,0:T(4,128)S(1)} %compare_select_fusion.1, pred[256,4096]{1,0:T(8,128)(4,1)S(1)} %fusion.19, f32[4,256]{1,0:T(4,128)S(1)} %get-tuple-element.48, f32[4,256]{1,0:T(4,128)S(1)} %get-tuple-element.47), kind=kOutput, calls=%fused_computation.44 | convolution fusion | flops 557973504 | bytes 20197376 | tf_op jit(solution)/shard_map/hrk,khd->hrd/dot_general | solution.py:94
  177.5 2.7 fusion.25
  180.5 53.3 %reduce-scatter.3.cloned.1.call-done = f32[256,512]{1,0:T(8,128)} async-done(((f32[256,4096]{1,0:T(8,128)}), f32[256,512]{1,0:T(8,128)}) %reduce-scatter.3.cloned.1.call-update) | async-done | bytes 524304 | tf_op jit(solution)/shard_map/reduce_scatter | solution.py:152
  234.1 2.0 fusion.43
  236.2 3.0 copy.62
  239.2 50.4 %all-gather.15.cloned.1.call-done = f32[256,4096]{1,0:T(8,128)} async-done(((f32[256,512]{1,0:T(8,128)}), f32[256,4096]{1,0:T(8,128)}) %all-gather.15.cloned.1.call-update) | async-done | bytes 4194320 | tf_op jit(solution)/shard_map/all_gather | solution.py:154
  289.6 2.7 multiply_reduce_fusion.1
  295.3 1.3 collective-permute-start
  296.6 14.9 %collective-permute-done = bf16[2,256,256]{1,2,0:T(8,128)(2,1)S(1)} collective-permute-done((bf16[2,256,256]{1,2,0:T(8,128)(2,1)S(1)}, bf16[2,256,256]{1,2,0:T(8,128)(2,1)S(1)}, u32[]{:S(2)}, u32[]{:S(2)}) %collective-permute-start) | collective-permute-done | bytes 262176 | tf_op jit(solution)/shard_map/ppermute | solution.py:18
  313.3 60.2 %all-gather.19.cloned.1.call-done = bf16[1,4096,256]{1,2,0:T(8,128)(2,1)} async-done(((bf16[1,256,256]{1,2,0:T(8,128)(2,1)}), bf16[1,4096,256]{1,2,0:T(8,128)(2,1)}) %all-gather.19.cloned.1.call-update) | async-done | bytes 2097168 | tf_op jit(solution)/shard_map/all_gather | solution.py:175
  373.5 9.7 %multiply_reduce_fusion = (f32[4,256]{1,0:T(4,128)S(1)}, f32[4,256,4096]{2,1,0:T(8,128)}) fusion(bf16[256,4,64]{0,2,1:T(8,128)(2,1)S(1)} %convolution_convert_fusion.3, bf16[4096,4,64]{0,2,1:T(8,128)(2,1)} %bitcast.126), kind=kOutput, calls=%fused_computation.10 | convolution fusion | flops 545258496 | bytes 19009536 | tf_op jit(solution)/shard_map/rhd,khd->hrk/dot_general | solution.py:82
  383.2 8.7 %fusion.7 = f32[4,256]{1,0:T(4,128)S(1)} fusion(f32[4,256,4096]{2,1,0:T(8,128)} %get-tuple-element.52, f32[4,256]{1,0:T(4,128)S(1)} %compare_select_fusion), kind=kLoop, calls=%fused_computation.12 | loop fusion | flops 12581888 | bytes 16785408 | tf_op jit(solution)/shard_map/reduce_sum | solution.py:93
  391.9 36.2 %all-gather.21.cloned.1.call-done = bf16[1,4096,256]{1,2,0:T(8,128)(2,1)} async-done(((bf16[1,256,256]{1,2,0:T(8,128)(2,1)}), bf16[1,4096,256]{1,2,0:T(8,128)(2,1)}) %all-gather.21.cloned.1.call-update) | async-done | bytes 2097168 | tf_op jit(solution)/shard_map/all_gather | solution.py:176
  428.1 8.3 %fusion.39 = f32[4,256,64]{1,2,0:T(8,128)S(1)} fusion(bf16[4096,4,64]{0,2,1:T(8,128)(2,1)} %bitcast.140, f32[4,256,4096]{2,1,0:T(8,128)} %get-tuple-element.52, f32[4,256]{1,0:T(4,128)S(1)} %compare_select_fusion, f32[4,256]{1,0:T(4,128)S(1)} %get-tuple-element.46, f32[4,256]{1,0:T(4,128)S(1)} %get-tuple-element.45), kind=kOutput, calls=%fused_computation.45 | convolution fusion | flops 549584896 | bytes 19148800 | tf_op jit(solution)/shard_map/hrk,khd->hrd/dot_general | solution.py:94
  436.8 4.3 conditional.3
  436.8 4.3 fusion.3
  441.1 53.5 %reduce-scatter.5.cloned.1.call-done = f32[256,512]{1,0:T(8,128)} async-done(((f32[256,4096]{1,0:T(8,128)}), f32[256,512]{1,0:T(8,128)}) %reduce-scatter.5.cloned.1.call-update) | async-done | bytes 524304 | tf_op jit(solution)/shard_map/reduce_scatter | solution.py:191
  494.6 1.9 fusion.42
  (79 shorter events, 14.6 us)
Async XLA Ops:
  6.5 171.0 %copy-start = (bf16[1,256,4096]{2,1,0:T(8,128)(2,1)S(1)}, bf16[1,256,4096]{2,1,0:T(8,128)(2,1)}, u32[]{:S(2)}) copy-start(bf16[1,256,4096]{2,1,0:T(8,128)(2,1)} %param.19) | copy-start | bytes 6291460
  6.5 39.8 %all-gather.17.cloned.1.call-start = ((), (), s32[]{:S(2)}) async-start(), calls=%async_computation.7 | async-start | bytes 2359296 | tf_op jit(solution)/shard_map/all_gather | solution.py:128
  7.3 106.5 %all-gather.11.cloned.1.call-start = ((), (), s32[]{:S(2)}) async-start(), calls=%async_computation.2 | async-start | bytes 2228224 | tf_op jit(solution)/shard_map/all_gather | solution.py:145
  46.4 1.6 copy-start.5
  50.3 7.0 %copy-start.9 = (f32[64,64]{1,0:T(8,128)S(1)}, f32[64,64]{1,0:T(8,128)}, u32[]{:S(2)}) copy-start(f32[64,64]{1,0:T(8,128)} %div.32) | copy-start | bytes 49156
  50.3 9.5 %copy-start.13 = (s32[3]{0:T(128)S(1)}, s32[3]{0:T(128)}, u32[]{:S(2)}) copy-start(s32[3]{0:T(128)} %param.16) | copy-start | bytes 40
  50.3 9.5 %copy-start.14 = (s32[3]{0:T(128)S(1)}, s32[3]{0:T(128)}, u32[]{:S(2)}) copy-start(s32[3]{0:T(128)} %param.15) | copy-start | bytes 40
  58.9 109.5 %all-gather.13.cloned.1.call-start = ((), (), s32[]{:S(2)}) async-start(), calls=%async_computation.3 | async-start | bytes 2228224 | tf_op jit(solution)/shard_map/all_gather | solution.py:146
  59.6 174.2 %reduce-scatter.3.cloned.1.call-start = ((), (), s32[]{:S(2)}) async-start(), calls=%async_computation.4 | async-start | bytes 4718592 | tf_op jit(solution)/shard_map/reduce_scatter | solution.py:152
  118.4 5.7 %copy-start.2 = (f32[4,256,4096]{2,1,0:T(8,128)}, f32[4,256,4096]{2,1,0:T(8,128)S(1)}, u32[]{:S(2)}) copy-start(f32[4,256,4096]{2,1,0:T(8,128)S(1)} %get-tuple-element.50) | copy-start | bytes 50331652
  168.3 8.7 %copy-start.10 = (f32[64,64]{1,0:T(8,128)S(1)}, f32[64,64]{1,0:T(8,128)}, u32[]{:S(2)}) copy-start(f32[64,64]{1,0:T(8,128)} %div.32) | copy-start | bytes 49156
  177.5 2.8 copy-start.12
  177.5 56.6 %copy-start.11 = (bf16[1,256,512]{2,1,0:T(8,128)(2,1)S(1)}, bf16[1,256,512]{2,1,0:T(8,128)(2,1)}, u32[]{:S(2)}) copy-start(bf16[1,256,512]{2,1,0:T(8,128)(2,1)} %param.13) | copy-start | bytes 786436
  180.2 55.9 %slice-start = ((bf16[1,2,4096,256]{3,2,1,0:T(8,128)(2,1)}), bf16[1,1,4096,256]{3,2,1,0:T(8,128)(2,1)S(1)}, s32[]{:S(2)}) async-start(bf16[1,2,4096,256]{3,2,1,0:T(8,128)(2,1)} %param.20), calls=%async_computation.10 | async-start | bytes 4194304 | tf_op jit(solution)/shard_map/slice | solution.py:157
  180.3 109.3 %all-gather.15.cloned.1.call-start = ((), (), s32[]{:S(2)}) async-start(), calls=%async_computation.5 | async-start | bytes 4718592 | tf_op jit(solution)/shard_map/all_gather | solution.py:154
  236.1 137.4 %all-gather.19.cloned.1.call-start = ((), (), s32[]{:S(2)}) async-start(), calls=%async_computation.8 | async-start | bytes 2228224 | tf_op jit(solution)/shard_map/all_gather | solution.py:175
  289.6 3.4 copy-start.3
  292.3 1.8 copy-start.8
  295.3 16.2 %collective-permute-start = (bf16[2,256,256]{1,2,0:T(8,128)(2,1)S(1)}, bf16[2,256,256]{1,2,0:T(8,128)(2,1)S(1)}, u32[]{:S(2)}, u32[]{:S(2)}) collective-permute-start(bf16[2,256,256]{1,2,0:T(8,128)(2,1)S(1)} %pad_maximum_fusion), channel_id=1, source_target_pairs={{0,8},{1,9},{2,10},{3,11},{4,12},{5,13},{6,14},{7,15},{16,24},{17,... | collective-permute-start | bytes 786440 | tf_op jit(solution)/shard_map/ppermute | solution.py:18
  312.3 115.8 %all-gather.21.cloned.1.call-start = ((), (), s32[]{:S(2)}) async-start(), calls=%async_computation.9 | async-start | bytes 2228224 | tf_op jit(solution)/shard_map/all_gather | solution.py:176
  313.0 181.6 %reduce-scatter.5.cloned.1.call-start = ((), (), s32[]{:S(2)}) async-start(), calls=%async_computation.6 | async-start | bytes 4718592 | tf_op jit(solution)/shard_map/reduce_scatter | solution.py:191
  441.1 53.5 %copy-start.4 = (f32[256,512]{1,0:T(8,128)S(1)}, f32[256,512]{1,0:T(8,128)}, u32[]{:S(2)}) copy-start(f32[256,512]{1,0:T(8,128)} %fusion.43) | copy-start | bytes 1572868
  441.1 55.5 %copy-start.1 = (bf16[1,256,4096]{2,1,0:T(8,128)(2,1)S(1)}, bf16[1,256,4096]{2,1,0:T(8,128)(2,1)}, u32[]{:S(2)}) copy-start(bf16[1,256,4096]{2,1,0:T(8,128)(2,1)} %param.19) | copy-start | bytes 6291460
Sparse Core Ops, SparseCore 0:
  9.2 37.1 all-gather.16
  59.0 54.7 all-gather.10
  116.2 52.0 all-gather.12
  180.4 53.3 reduce-scatter.2
  236.2 53.2 all-gather.14
  312.4 61.0 all-gather.18
  375.9 52.0 all-gather.20
  441.2 53.3 reduce-scatter.4
where the time goes:
time: 508 us; the launch traced here: 503 us
  waiting for transfers between devices  384 us (76%)
  matrix products  48 us (9%)
  other arithmetic  29 us (6%)
  blocking collectives  14.5 us (3%)
  between operations  13.8 us (3%)
  local copies, waits for them, and re-layouts  11.8 us (2%)
    all_gather x1, waiting for transfers between devices, body(): lax.all_gather(arrived[0], 'seq', axis=0, tiled=True)  60.2 us
    reduce_scatter x1, waiting for transfers between devices, body(): lax.psum_scatter(cross_terms, 'mp', scatter_dimension=1, tiled=True)  53.5 us
    reduce_scatter x1, waiting for transfers between devices, body(): shares = lax.psum_scatter(self_terms, 'mp', scatter_dimension=1, tiled=True)  53.3 us
    all_gather x1, waiting for transfers between devices, body(): lax.all_gather(rotated[1], 'seq', axis=0, tiled=True)  52.2 us
    all_gather x1, waiting for transfers between devices, body(): layer_rows = lax.all_gather(local_rows, 'mp', axis=1, tiled=True)  50.4 us
    all_gather x1, waiting for transfers between devices, body(): lax.all_gather(rotated[2], 'seq', axis=0, tiled=True)  44.2 us
    all_gather x1, waiting for transfers between devices, body(): lax.all_gather(arrived[1], 'seq', axis=0, tiled=True)  36.2 us
    all_gather x1, waiting for transfers between devices, body(): lax.all_gather(mantissas[0], 'mp', axis=1, tiled=True)  17.2 us
  transfers between devices with their start and end apart: 9, of which 9 were waited for; matrix products, arithmetic and copies ran while one was open for 8% of the time, Pallas kernels for 0%

commit v1 on v0

v1 whole, which is shorter than its diff:
```python
import functools
import math

import jax
import jax.numpy as jnp
from jax import lax
from jax.experimental import pallas as pl
from jax.experimental.pallas import tpu as pltpu
from jax.sharding import PartitionSpec as P

MESH = pl.DeviceIdType.MESH
EPS = 1e-06
F32 = jnp.float32
BF16 = jnp.bfloat16
ROWS = 256
BLOCKS = 16
QSCALE = math.log2(math.e) / 8.0
VMEM_LIMIT = 50 * 1024 * 1024


def remote(src, dst, send, recv, device):
    return pltpu.make_async_remote_copy(
        src_ref=src, dst_ref=dst, send_sem=send, recv_sem=recv, device_id=device, device_id_type=MESH
    )


def barrier_with(devices_and_guards):
    barrier = pltpu.get_barrier_semaphore()
    for device, guard in devices_and_guards:
        if guard is None:
            pl.semaphore_signal(barrier, inc=1, device_id=device, device_id_type=MESH)
        else:

            @pl.when(guard)
            def _(device=device):
                pl.semaphore_signal(barrier, inc=1, device_id=device, device_id_type=MESH)

    count = sum(1 if guard is None else guard.astype(jnp.int32) for _, guard in devices_and_guards)
    pl.semaphore_wait(barrier, count)


class Place:
    def __init__(self):
        self.mp = lax.axis_index("mp")
        self.seq = lax.axis_index("seq")
        self.sec = lax.axis_index("sec")
        self.p = self.mp // 2
        self.c = self.mp % 2
        y, x = self.seq // 4, self.seq % 4
        self.a = jnp.where(self.c == 0, y, x)
        self.g = jnp.where(self.c == 0, x, y)
        self.sa = 4 - 3 * self.c
        self.sg = 1 + 3 * self.c

    def line(self, step):
        return {"mp": self.mp + 2 * step}

    def sibling(self):
        return {"mp": self.p * 2 + 1 - self.c}

    def seq_at(self, a, g):
        return a * self.sa + g * self.sg

    def a_peer(self, d):
        return {"seq": self.seq_at((self.a + d) % 4, self.g)}

    def g_peer(self, d):
        return {"seq": self.seq_at(self.a, (self.g + d) % 4)}

    def line_devices(self):
        return [
            (self.line(1), self.p < 3),
            (self.line(-1), self.p > 0),
            (self.sibling(), None),
        ]

    def a_devices(self):
        return [(self.a_peer(d), None) for d in (1, 2, 3)]

    def g_devices(self):
        return [(self.g_peer(d), None) for d in (1, 3)]


def line_gather(at, buf, chunks, send, recv):
    rows = buf.shape[1] // chunks

    def piece(block, k):
        return buf.at[block, pl.ds(k * rows, rows)]

    def copy(block, k, slot, device):
        return remote(piece(block, k), piece(block, k), send.at[slot, k], recv.at[block, k], device)

    def own(p):
        return p * 2 + at.c

    def up(t, k):
        return copy(own(at.p - t), k, t, at.line(1))

    def down(t, k):
        return copy(own(at.p + t), k, 3 + t, at.line(-1))

    def across(p, k):
        return copy(own(p), k, 6 + p, at.sibling())

    for k in range(chunks):

        @pl.when(at.p < 3)
        def _():
            up(0, k).start()

        @pl.when(at.p > 0)
        def _():
            down(0, k).start()

        across(at.p, k).start()
    for t in (1, 2, 3):
        for k in range(chunks):

            @pl.when(at.p >= t)
            def _():
                up(t, k).wait_recv()

                if t < 3:

                    @pl.when(at.p < 3)
                    def _():
                        up(t, k).start()

                across(at.p - t, k).start()

            @pl.when(at.p <= 3 - t)
            def _():
                down(t, k).wait_recv()

                if t < 3:

                    @pl.when(at.p > 0)
                    def _():
                        down(t, k).start()

                across(at.p + t, k).start()

    for p in range(4):
        for k in range(chunks):
            copy(p * 2 + 1 - at.c, k, 6 + p, at.sibling()).wait_recv()
    for k in range(chunks):
        for t in range(3):

            @pl.when((at.p >= t) & (at.p < 3))
            def _():
                up(t, k).wait_send()

            @pl.when((at.p <= 3 - t) & (at.p > 0))
            def _():
                down(t, k).wait_send()

        for p in range(4):
            across(p, k).wait_send()


def exchange_heads(at, src, dst, send, recv):
    copies = []
    for d in (1, 2, 3):
        copy = remote(
            src.at[(at.a + d) % 4], dst.at[at.a], send.at[d], recv.at[d], at.a_peer(d)
        )
        copy.start()
        copies.append(copy)
    return copies


def from_a(at, dst, send, recv, d):
    unit = dst.at[(at.a + 4 - d) % 4]
    return remote(unit, unit, send.at[d], recv.at[d], at.a_peer(d))


def ring_gather(at, kv, arrive, send, recv):
    def unit(g, d):
        return kv.at[(at.g + 4 + g) % 4, (at.a + 4 - d) % 4]

    def hop(g, d, slot, step):
        return remote(unit(g, d), unit(g, d), send.at[slot, d], recv.at[slot, d], at.g_peer(step))

    for d in range(4):
        arrive(d)
        hop(0, d, 0, 1).start()
        hop(0, d, 1, 3).start()
    for d in range(4):
        hop(-1, d, 0, 1).wait_recv()
        if d < 2:
            hop(-1, d, 2, 1).start()
        hop(1, d, 1, 3).wait_recv()
        if d >= 2:
            hop(1, d, 2, 3).start()
    for d in range(4):
        hop(2, d, 2, 1).wait_recv()
    for d in range(4):
        hop(0, d, 0, 1).wait_send()
        hop(0, d, 1, 3).wait_send()
        if d < 2:
            hop(-1, d, 2, 1).wait_send()
        else:
            hop(1, d, 2, 3).wait_send()


def low_half():
    return lax.broadcasted_iota(jnp.int32, (ROWS, 128), 1) < 64


def pair_heads(first, second, dst):
    low = low_half()
    for pair in (0, 1):
        columns = slice(pair * 128, pair * 128 + 128)
        f = first[:, columns]
        f_turned = pltpu.roll(f, 64, 1)
        if second is None:
            s = s_turned = jnp.zeros_like(f)
        else:
            s = second[:, columns]
            s_turned = pltpu.roll(s, 64, 1)
        dst[2 * pair] = jnp.where(low, f, s_turned).astype(BF16)
        dst[2 * pair + 1] = jnp.where(low, f_turned, s).astype(BF16)


def project(buf, gain_ref, weights, acc, count):
    acc[...] = jnp.zeros_like(acc)

    def step(j, squares):
        block = buf[j].astype(F32)
        scaled = (block * gain_ref[j]).astype(BF16)
        for i in range(count):
            acc[i] += jnp.dot(
                scaled, weights[i, pl.ds(pl.multiple_of(j * 512, 512), 512), :], preferred_element_type=F32
            )
        return squares + jnp.sum(block * block, axis=1, keepdims=True)

    squares = lax.fori_loop(0, 8, step, jnp.zeros((ROWS, 1), F32))
    return lax.rsqrt(squares / 4096.0 + EPS)


def self_kernel(
    x_ref, gain_ref, w_ref, q_out, kv_out,
    buf, w_vmem, acc, q4, kv4, load_sem,
    line_send, line_recv, kv_send, kv_recv, q_send, q_recv, ring_send, ring_recv,
):
    at = Place()
    load = pltpu.make_async_copy(w_ref, w_vmem, load_sem)
    load.start()
    buf[at.mp] = x_ref[...]
    barrier_with(at.line_devices() + at.a_devices() + at.g_devices())
    line_gather(at, buf, 2, line_send, line_recv)
    load.wait()
    scale = project(buf, gain_ref, w_vmem, acc, 3)
    pair_heads(acc[1] * scale, acc[2] * scale, kv4)
    kv_copies = exchange_heads(at, kv4, kv_out.at[at.g], kv_send, kv_recv)
    pair_heads(acc[0] * (scale * QSCALE), None, q4)
    q_copies = exchange_heads(at, q4, q_out, q_send, q_recv)
    kv_out[at.g, at.a] = kv4[at.a]
    q_out[at.a] = q4[at.a]

    def arrive(d):
        if d:
            from_a(at, kv_out.at[at.g], kv_send, kv_recv, d).wait_recv()

    ring_gather(at, kv_out, arrive, ring_send, ring_recv)
    for d in (1, 2, 3):
        from_a(at, q_out, q_send, q_recv, d).wait_recv()
    for copy in kv_copies + q_copies:
        copy.wait_send()


def params(collective_id):
    return pltpu.CompilerParams(
        collective_id=collective_id, has_side_effects=True, vmem_limit_bytes=VMEM_LIMIT
    )


VMEM = pl.BlockSpec(memory_space=pltpu.VMEM)
ANY = pl.BlockSpec(memory_space=pl.ANY)
DMA = pltpu.SemaphoreType.DMA


def self_project(x, gain, weights):
    return pl.pallas_call(
        self_kernel,
        out_shape=(
            jax.ShapeDtypeStruct((4, ROWS, 128), BF16),
            jax.ShapeDtypeStruct((4, 4, ROWS, 128), BF16),
        ),
        in_specs=[VMEM, VMEM, ANY],
        out_specs=(VMEM, VMEM),
        scratch_shapes=[
            pltpu.VMEM((8, ROWS, 512), BF16),
            pltpu.VMEM((3, 4096, 256), BF16),
            pltpu.VMEM((3, ROWS, 256), F32),
            pltpu.VMEM((4, ROWS, 128), BF16),
            pltpu.VMEM((4, ROWS, 128), BF16),
            DMA,
            DMA((10, 2)),
            DMA((8, 2)),
            DMA((4,)),
            DMA((4,)),
            DMA((4,)),
            DMA((4,)),
            DMA((3, 4)),
            DMA((3, 4)),
        ],
        compiler_params=params(0),
        name="self_project",
    )(x, gain, weights)


def attend_kernel(masked, lengths_ref, q_ref, kv_ref, out_ref, scores):
    at = Place()
    query_block = pl.program_id(0)
    q = q_ref[0]
    if masked:
        first = at.seq_at(query_block, at.g) * ROWS
        rows = first + lax.broadcasted_iota(jnp.int32, (ROWS, 1), 0)
        one = lengths_ref[0]
        two = one + lengths_ref[1]
        begin = jnp.where(rows >= two, two, jnp.where(rows >= one, one, 0))
        end = jnp.where(rows >= two, BLOCKS * ROWS, jnp.where(rows >= one, two, one))
        end = jnp.where(at.sec == 1, jnp.minimum(end, rows + 1), end)
        lane = lax.broadcasted_iota(jnp.int32, (ROWS, ROWS), 1)
    top = jnp.full((ROWS, ROWS), -jnp.inf, F32)
    for k in range(BLOCKS):
        block = lax.dot_general(
            q, kv_ref[k // 4, k % 4], (((1,), (1,)), ((), ())), preferred_element_type=F32
        )
        if masked:
            base = at.seq_at(k % 4, k // 4) * ROWS
            block = jnp.where((lane >= begin - base) & (lane < end - base), block, -jnp.inf)
        scores[k] = block
        top = jnp.maximum(top, block)
    top = jnp.max(top, axis=1, keepdims=True)
    total = jnp.zeros((ROWS, ROWS), F32)
    mixed = jnp.zeros((ROWS, 128), F32)
    for k in range(BLOCKS):
        weight = jnp.exp2(scores[k] - top)
        total += weight
        mixed += jnp.dot(weight.astype(BF16), kv_ref[k // 4, k % 4], preferred_element_type=F32)
    out_ref[0] = (mixed / jnp.sum(total, axis=1, keepdims=True)).astype(BF16)


def attend(lengths, q, kv, masked):
    return pl.pallas_call(
        functools.partial(attend_kernel, masked),
        out_shape=jax.ShapeDtypeStruct((4, ROWS, 128), BF16),
        grid=(4,),
        in_specs=[
            pl.BlockSpec(memory_space=pltpu.SMEM),
            pl.BlockSpec((1, ROWS, 128), lambda i: (i, 0, 0)),
            pl.BlockSpec((4, 4, ROWS, 128), lambda i: (0, 0, 0, 0)),
        ],
        out_specs=pl.BlockSpec((1, ROWS, 128), lambda i: (i, 0, 0)),
        scratch_shapes=[pltpu.VMEM((BLOCKS, ROWS, ROWS), F32)],
        compiler_params=pltpu.CompilerParams(vmem_limit_bytes=VMEM_LIMIT),
        name="attend_masked" if masked else "attend_all",
    )(lengths, q, kv)


def collect_mixed(at, mixed_ref, heads, buf, send, recv, line_send, line_recv):
    copies = exchange_heads(at, mixed_ref, heads, send, recv)
    heads[at.a] = mixed_ref[at.a]
    for d in (1, 2, 3):
        from_a(at, heads, send, recv, d).wait_recv()
    low = low_half()
    for pair in (0, 1):
        even = pltpu.roll(heads[2 * pair].astype(F32), 64, 1)
        odd = heads[2 * pair + 1].astype(F32)
        buf[at.mp, :, pair * 128 : pair * 128 + 128] = jnp.where(low, even, odd).astype(BF16)
    for copy in copies:
        copy.wait_send()
    line_gather(at, buf, 1, line_send, line_recv)


def cross_kernel(
    mixed_ref, wo_ref, x_ref, gain_ref, w_ref, rows_out, q_out, kv_out,
    heads, mixed_buf, buf, w_vmem, acc, q4, kv4, relay, load_sem,
    back_send, back_recv, mix_send, mix_recv,
    line_send, line_recv, q_send, q_recv, over_send, over_recv, relay_send, relay_recv, ring_send, ring_recv,
):
    at = Place()
    load = pltpu.make_async_copy(w_ref, w_vmem, load_sem)
    load.start()
    encoder, decoder = at.sec == 0, at.sec == 1
    far = (at.p + 2) % 4 * 2 + at.c

    def over(d):
        return {"seq": at.seq_at((at.a + d) % 4, at.g), "sec": 1 - at.sec, "mp": far}

    barrier_with(
        at.line_devices()
        + at.a_devices()
        + at.g_devices()
        + [(over(d), None) for d in range(4)]
        + [({"mp": far}, decoder)]
    )
    collect_mixed(at, mixed_ref, heads, mixed_buf, back_send, back_recv, mix_send, mix_recv)
    total = x_ref[...].astype(F32)
    for j in range(8):
        total += jnp.dot(mixed_buf[j], wo_ref[j], preferred_element_type=F32)
    rows_out[...] = total
    buf[at.mp] = total.astype(BF16)
    line_gather(at, buf, 2, line_send, line_recv)
    load.wait()
    scale = project(buf, gain_ref, w_vmem, acc, 2)

    def send_over(d):
        return remote(kv4.at[(at.a + d) % 4], relay.at[at.a], over_send.at[d], over_recv.at[d], over(d))

    def relayed(d):
        unit = relay.at[(at.a + 4 - d) % 4]
        return remote(unit, unit, over_send.at[d], over_recv.at[d], over(d))

    def onward(d):
        source = (at.a + 4 - d) % 4
        return remote(
            relay.at[source], kv_out.at[at.g, source], relay_send.at[d], relay_recv.at[d], {"mp": far}
        )

    @pl.when(encoder)
    def _():
        pair_heads(acc[0] * scale, acc[1] * scale, kv4)
        for d in range(4):
            send_over(d).start()
        q_out[...] = jnp.zeros_like(q_out)
        kv_out[...] = jnp.zeros_like(kv_out)
        for d in range(4):
            send_over(d).wait_send()

    @pl.when(decoder)
    def _():
        pair_heads(acc[0] * (scale * QSCALE), None, q4)
        q_copies = exchange_heads(at, q4, q_out, q_send, q_recv)
        q_out[at.a] = q4[at.a]
        for d in range(4):
            relayed(d).wait_recv()
            onward(d).start()

        def arrive(d):
            onward(d).wait_recv()

        ring_gather(at, kv_out, arrive, ring_send, ring_recv)
        for d in (1, 2, 3):
            from_a(at, q_out, q_send, q_recv, d).wait_recv()
        for copy in q_copies:
            copy.wait_send()
        for d in range(4):
            onward(d).wait_send()


def cross_project(mixed, wo, x, gain, weights):
    return pl.pallas_call(
        cross_kernel,
        out_shape=(
            jax.ShapeDtypeStruct((ROWS, 512), F32),
            jax.ShapeDtypeStruct((4, ROWS, 128), BF16),
            jax.ShapeDtypeStruct((4, 4, ROWS, 128), BF16),
        ),
        in_specs=[VMEM, VMEM, VMEM, VMEM, ANY],
        out_specs=(VMEM, VMEM, VMEM),
        scratch_shapes=[
            pltpu.VMEM((4, ROWS, 128), BF16),
            pltpu.VMEM((8, ROWS, 256), BF16),
            pltpu.VMEM((8, ROWS, 512), BF16),
            pltpu.VMEM((2, 4096, 256), BF16),
            pltpu.VMEM((2, ROWS, 256), F32),
            pltpu.VMEM((4, ROWS, 128), BF16),
            pltpu.VMEM((4, ROWS, 128), BF16),
            pltpu.VMEM((4, ROWS, 128), BF16),
            DMA,
            DMA((4,)),
            DMA((4,)),
            DMA((10, 1)),
            DMA((8, 1)),
            DMA((10, 2)),
            DMA((8, 2)),
            DMA((4,)),
            DMA((4,)),
            DMA((4,)),
            DMA((4,)),
            DMA((4,)),
            DMA((4,)),
            DMA((3, 4)),
            DMA((3, 4)),
        ],
        compiler_params=params(1),
        name="cross_project",
    )(mixed, wo, x, gain, weights)


def output_kernel(mixed_ref, w_ref, rows_ref, out_ref, heads, buf, back_send, back_recv, line_send, line_recv):
    at = Place()

    @pl.when(at.sec == 0)
    def _():
        out_ref[...] = rows_ref[...]

    barrier_with(at.line_devices() + at.a_devices())

    @pl.when(at.sec == 1)
    def _():
        collect_mixed(at, mixed_ref, heads, buf, back_send, back_recv, line_send, line_recv)
        total = rows_ref[...]
        for j in range(8):
            total += lax.dot_general(
                buf[j], w_ref[j], (((1,), (1,)), ((), ())), preferred_element_type=F32
            )
        out_ref[...] = total


def output(mixed, weights, rows):
    return pl.pallas_call(
        output_kernel,
        out_shape=jax.ShapeDtypeStruct((ROWS, 512), F32),
        in_specs=[VMEM, VMEM, VMEM],
        out_specs=VMEM,
        scratch_shapes=[
            pltpu.VMEM((4, ROWS, 128), BF16),
            pltpu.VMEM((8, ROWS, 256), BF16),
            DMA((4,)),
            DMA((4,)),
            DMA((10, 1)),
            DMA((8, 1)),
        ],
        compiler_params=params(2),
        name="output",
    )(mixed, weights, rows)


def body(
    mantissas, exponents, source_lengths, target_lengths, norm_gains, self_weights, self_output, cross_weights
):
    seq, sec = lax.axis_index("seq"), lax.axis_index("sec")
    scale = jnp.exp2(exponents[0].astype(F32))
    x = (mantissas[0].astype(F32).reshape(ROWS, 4, 128) * scale[:, :, None]).reshape(ROWS, 512).astype(BF16)
    gains = norm_gains[0].reshape(2, 8, 1, 512)
    lengths = jnp.where(sec == 1, target_lengths, source_lengths)

    piece = lax.dynamic_index_in_dim(self_output[0].reshape(16, 16, 8, 512), seq, 0, keepdims=False)
    piece = lax.all_to_all(piece.transpose(1, 0, 2), "mp", 0, 0)
    wo = lax.all_gather(piece, "seq", axis=0).transpose(1, 0, 2, 3).reshape(8, 256, 512)
    piece = lax.dynamic_index_in_dim(cross_weights[0, 1].reshape(8, 16, 32, 256), seq, 1, keepdims=False)
    piece = lax.all_to_all(piece, "mp", 0, 0)
    wc = lax.all_gather(piece, "seq", axis=0).transpose(1, 0, 2, 3).reshape(8, 512, 256)

    q, kv = self_project(x, gains[0], self_weights[0])
    mixed = attend(lengths, q, kv, True)
    rows, q, kv = cross_project(mixed, wo, x, gains[1], cross_weights[0])
    mixed = attend(lengths, q, kv, False)
    return output(mixed, wc, rows)[None]


def solution(mesh):
    in_specs = (
        P("sec", "seq", "mp"),
        P("sec", "seq", "mp"),
        P(),
        P(),
        P("sec", None, None),
        P("sec", None, None, "mp"),
        P("sec", "mp", None),
        P("sec", None, None, "mp"),
    )
    out_specs = P("sec", "seq", "mp")
    return jax.shard_map(body, mesh=mesh, in_specs=in_specs, out_specs=out_specs, check_vma=False)
```

time: 508 us -> 239 us (0.47)
  waiting for transfers between devices: 384 us -> 36.9 us
  Pallas kernels: 0 us -> 156 us
  matrix products: 48 us -> 0 us
  other arithmetic: 29 us -> 0.09 us
    all_gather x6 -> x2, waiting for transfers between devices: 260 us -> 36.8 us  [body(): lax.all_gather(piece, 'seq', axis=0).transpose(1, 0, 2, 3)]
    pallas_call x0 -> x5, Pallas kernels: none -> 156 us  [the longest x1 72.9 us: cross_project(): pl.pallas_call(cross_kernel, out_shape=(jax.ShapeDtypeStruct((ROWS, 512),...]
    reduce_scatter x2 -> x0, waiting for transfers between devices: 107 us -> none  [the longest x1 53.5 us: body(): lax.psum_scatter(cross_terms, 'mp', scatter_dimension=1, tiled=True)]
    dot_general x12 -> x0, matrix products: 48 us -> none  [the longest x2 17 us: accumulate(): jnp.einsum('hrk,khd->hrd', weights.astype(jnp.bfloat16), value_block.resh...]
    all_to_all x0 -> x2, blocking collectives: none -> 19.4 us  [the longest x1 9.84 us: body(): piece = lax.all_to_all(piece, 'mp', 0, 0)]
    reduce_sum x6 -> x0, other arithmetic: 18.9 us -> none  [the longest x2 13.6 us: accumulate(): denominator = denominator * rescale + jnp.sum(weights, axis=2)]
    ppermute x1 -> x0, waiting for transfers between devices: 14.9 us -> none  [shifted(): lax.ppermute(value, axis, [(source, source + steps) for source in range(i...]
    all_gather x1 -> x0, blocking collectives: 14.5 us -> none  [body(): lax.all_gather(exponents[0], 'mp', axis=1, tiled=True)]
  transfers between devices with their start and end apart: 9 -> 2, of which waited for: 9 -> 1; matrix products, arithmetic and copies ran while one was open for 8% -> 2% of each run, Pallas kernels for 0% -> 23%
where the time goes in v1:
time: 239 us; the launch traced here: 237 us
  Pallas kernels  156 us (65%)
  waiting for transfers between devices  36.9 us (15%)
  blocking collectives  19.4 us (8%)
  between operations  13.6 us (6%)
  local copies, waits for them, and re-layouts  10.4 us (4%)
    pallas_call x1, Pallas kernels, cross_project(): pl.pallas_call(cross_kernel, out_shape=(jax.ShapeDtypeStruct((ROWS, 512),...  72.9 us
    pallas_call x1, Pallas kernels, self_project(): pl.pallas_call(self_kernel, out_shape=(jax.ShapeDtypeStruct((4, ROWS, 128...  44.6 us
    all_gather x2, waiting for transfers between devices, body(): lax.all_gather(piece, 'seq', axis=0).transpose(1, 0, 2, 3)  36.8 us
    pallas_call x1, Pallas kernels, output(): pl.pallas_call(output_kernel, out_shape=jax.ShapeDtypeStruct((ROWS, 512),...  20.5 us
    pallas_call x2, Pallas kernels, attend(): pl.pallas_call(functools.partial(attend_kernel, masked), out_shape=jax.Sh...  18.2 us
    all_to_all x1, blocking collectives, body(): piece = lax.all_to_all(piece, 'mp', 0, 0)  9.84 us
    all_to_all x1, blocking collectives, body(): piece = lax.all_to_all(piece.transpose(1, 0, 2), 'mp', 0, 0)  9.59 us
    transpose x2, local copies, waits for them, and re-layouts, body(): lax.all_gather(piece, 'seq', axis=0).transpose(1, 0, 2, 3)  5 us
  transfers between devices with their start and end apart: 2, of which 1 were waited for; matrix products, arithmetic and copies ran while one was open for 2% of the time, Pallas kernels for 23%

profile of v1, /device:TPU:129, one launch (start us, length us, event | category | flops | bytes accessed | tf_op | source)
XLA Modules:
  0.0 236.6 jit_solution(18094658721589477384)
XLA Ops:
  6.5 0.0 all-gather.5.cloned.1.call-start
  6.5 2.5 %copy.23 = bf16[32,8,8,512]{3,2,1,0:T(8,128)(2,1)S(1)} copy(bf16[32,8,8,512]{3,1,2,0:T(8,128)(2,1)} %bitcast.47) | data formatting | bytes 4194304
  9.1 9.6 %all_to_all.10 = bf16[8,16,512]{2,1,0:T(8,128)(2,1)} all-to-all(bf16[8,16,512]{2,1,0:T(8,128)(2,1)S(1)} %bitcast.50), channel_id=1, replica_groups=mesh['seq'=16,'sec'=2,'mp'=8] {'mp'}, dimensions={0} | all-to-all | bytes 262144 | tf_op jit(solution)/shard_map/all_to_all | solution.py:543
  18.7 0.0 all-gather.5.cloned.1.call-update
  18.7 0.0 slice-start
  18.7 0.0 copy-start.2
  18.7 0.0 copy-start
  18.7 0.0 all-gather.7.cloned.1.call-start
  18.8 0.0 copy-start.1
  18.8 1.5 slice-done
  20.3 9.8 %all_to_all.11 = bf16[8,32,256]{2,1,0:T(8,128)(2,1)} all-to-all(bf16[8,32,256]{2,1,0:T(8,128)(2,1)S(1)} %dynamic-slice_bitcast_fusion), channel_id=1, replica_groups=mesh['seq'=16,'sec'=2,'mp'=8] {'mp'}, dimensions={0} | all-to-all | bytes 262144 | tf_op jit(solution)/shard_map/all_to_all | solution.py:546
  30.2 0.0 all-gather.7.cloned.1.call-update
  30.2 0.0 copy-done.2
  30.2 0.1 copy.15
  30.4 0.3 mul.11
  30.7 0.0 copy-done
  30.7 0.1 fusion.x_ref
  30.8 0.0 copy-done.1
  30.8 0.0 copy-start.3
  30.8 0.0 copy-start.4
  30.9 44.6 %self_project.1 = (bf16[4,256,128]{2,1,0:T(8,128)(2,1)S(1)}, bf16[4,4,256,128]{3,2,1,0:T(8,128)(2,1)S(1)}) custom-call(bf16[256,512]{1,0:T(8,128)(2,1)S(1)} %fusion.x_ref, f32[8,1,512]{2,1,0:T(1,128)S(1)} %bitcast.40, bf16[3,4096,256]{2,1,0:T(8,128)(2,1)} %bitcast.44), custom_call_target="tpu_custom_call" | custom-call | tf_op jit(solution)/shard_map/self_project/pallas_call | solution.py:284
  75.5 0.0 copy-done.3
  75.5 0.0 copy-done.4
  75.5 10.1 %attend_masked.1.mixed_ref = bf16[4,256,128]{2,1,0:T(8,128)(2,1)S(1)} custom-call(s32[3]{0:T(128)S(1)} %broadcast_select_fusion.lengths_ref, bf16[4,256,128]{2,1,0:T(8,128)(2,1)S(1)} %get-tuple-element.10.q_ref, bf16[4,4,256,128]{3,2,1,0:T(8,128)(2,1)S(1)} %get-tuple-element.11.kv_ref), custom_call_target="tpu_custom_call" | custom-call | tf_op jit(solution)/shard_map/attend_masked/pallas_call | solution.py:347
  85.6 0.0 all-gather.5.cloned.1.call-done
  85.7 3.2 %copy.17 = bf16[8,16,16,512]{3,2,1,0:T(8,128)(2,1)} copy(bf16[8,16,16,512]{3,2,0,1:T(8,128)(2,1)} %bitcast.48) | data formatting | bytes 4194304 | tf_op jit(solution)/shard_map/transpose | solution.py:544
  88.8 36.8 %all-gather.7.cloned.1.call-done = bf16[128,32,256]{2,1,0:T(8,128)(2,1)} async-done(((bf16[8,32,256]{2,1,0:T(8,128)(2,1)}), bf16[128,32,256]{2,1,0:T(8,128)(2,1)}) %all-gather.7.cloned.1.call-update) | async-done | bytes 2097168 | tf_op jit(solution)/shard_map/all_gather | solution.py:547
  125.7 1.8 copy.19
  127.5 72.9 %cross_project.1 = (f32[256,512]{1,0:T(8,128)S(1)}, bf16[4,256,128]{2,1,0:T(8,128)(2,1)S(1)}, bf16[4,4,256,128]{3,2,1,0:T(8,128)(2,1)S(1)}) custom-call(bf16[4,256,128]{2,1,0:T(8,128)(2,1)S(1)} %attend_masked.1.mixed_ref, bf16[8,256,512]{2,1,0:T(8,128)(2,1)} %bitcast.43, bf16[256,512]{1,0:T(8,128)(2,1)S(1)} %fusion.x_ref, f32[8,1,512]{2,1,0:T(1,128)S(1)} %bitcast.39, ...), custom_call_target="tpu_custom_call" | custom-call | tf_op jit(solution)/shard_map/cross_project/pallas_call | solution.py:455
  200.4 8.1 %attend_all.1.mixed_ref = bf16[4,256,128]{2,1,0:T(8,128)(2,1)S(1)} custom-call(s32[3]{0:T(128)S(1)} %broadcast_select_fusion.lengths_ref, bf16[4,256,128]{2,1,0:T(8,128)(2,1)S(1)} %get-tuple-element.12.q_ref, bf16[4,4,256,128]{3,2,1,0:T(8,128)(2,1)S(1)} %get-tuple-element.13.kv_ref), custom_call_target="tpu_custom_call" | custom-call | tf_op jit(solution)/shard_map/attend_all/pallas_call | solution.py:347
  208.5 20.5 %output.1 = f32[256,512]{1,0:T(8,128)S(1)} custom-call(bf16[4,256,128]{2,1,0:T(8,128)(2,1)S(1)} %attend_all.1.mixed_ref, bf16[8,512,256]{2,1,0:T(8,128)(2,1)S(1)} %bitcast.37, f32[256,512]{1,0:T(8,128)S(1)} %get-tuple-element.14.rows_ref), custom_call_target="tpu_custom_call" | custom-call | tf_op jit(solution)/shard_map/output/pallas_call | solution.py:515
  229.0 0.8 copy.28
  (6 shorter events, 0.1 us)
Async XLA Ops:
  6.5 79.1 %all-gather.5.cloned.1.call-start = ((), (), s32[]{:S(2)}) async-start(), calls=%async_computation.2 | async-start | bytes 2228224 | tf_op jit(solution)/shard_map/all_gather | solution.py:544
  18.7 1.6 slice-start
  18.7 11.5 %copy-start.2 = (s32[1,256,4]{1,2,0:T(4,128)S(1)}, s32[1,256,4]{1,2,0:T(4,128)}, u32[]{:S(2)}) copy-start(s32[1,256,4]{1,2,0:T(4,128)} %param.9) | copy-start | bytes 12292
  18.7 12.0 %copy-start = (bf16[1,256,512]{2,1,0:T(8,128)(2,1)S(1)}, bf16[1,256,512]{2,1,0:T(8,128)(2,1)}, u32[]{:S(2)}) copy-start(bf16[1,256,512]{2,1,0:T(8,128)(2,1)} %param.8) | copy-start | bytes 786436
  18.7 106.9 %all-gather.7.cloned.1.call-start = ((), (), s32[]{:S(2)}) async-start(), calls=%async_computation.3 | async-start | bytes 2228224 | tf_op jit(solution)/shard_map/all_gather | solution.py:547
  18.8 12.0 %copy-start.1 = (f32[1,2,4096]{2,1,0:T(2,128)S(1)}, f32[1,2,4096]{2,1,0:T(2,128)}, u32[]{:S(2)}) copy-start(f32[1,2,4096]{2,1,0:T(2,128)} %param.12) | copy-start | bytes 98308
  30.8 44.7 %copy-start.3 = (s32[3]{0:T(128)S(1)}, s32[3]{0:T(128)}, u32[]{:S(2)}) copy-start(s32[3]{0:T(128)} %param.11) | copy-start | bytes 40
  30.8 44.7 %copy-start.4 = (s32[3]{0:T(128)S(1)}, s32[3]{0:T(128)}, u32[]{:S(2)}) copy-start(s32[3]{0:T(128)} %param.10) | copy-start | bytes 40
Sparse Core Ops, SparseCore 0:
  18.8 56.1 all-gather.4
  77.4 48.1 all-gather.6

commit v2 on v1

--- a/solution.py
+++ b/solution.py
@@ -74,6 +74,9 @@
             (self.sibling(), None),
         ]
 
+    def mp_devices(self):
+        return [({"mp": (self.mp + d) % 8}, None) for d in range(1, 8)]
+
     def a_devices(self):
         return [(self.a_peer(d), None) for d in (1, 2, 3)]
 
@@ -81,8 +84,9 @@
         return [(self.g_peer(d), None) for d in (1, 3)]
 
 
-def line_gather(at, buf, chunks, send, recv):
+def line_gather(at, buf, chunks, send, recv, hooks=(), process=None):
     rows = buf.shape[1] // chunks
+    hooks = list(hooks)
 
     def piece(block, k):
         return buf.at[block, pl.ds(k * rows, rows)]
@@ -101,6 +105,10 @@
 
     def across(p, k):
         return copy(own(p), k, 6 + p, at.sibling())
+
+    def await_across(p):
+        for k in range(chunks):
+            copy(p * 2 + 1 - at.c, k, 6 + p, at.sibling()).wait_recv()
 
     for k in range(chunks):
 
@@ -113,6 +121,8 @@
             down(0, k).start()
 
         across(at.p, k).start()
+    if process is not None:
+        process(at.mp)
     for t in (1, 2, 3):
         for k in range(chunks):
 
@@ -140,9 +150,30 @@
 
                 across(at.p + t, k).start()
 
-    for p in range(4):
-        for k in range(chunks):
-            copy(p * 2 + 1 - at.c, k, 6 + p, at.sibling()).wait_recv()
+            if hooks:
+                hooks.pop(0)()
+
+        if t == 1:
+            await_across(at.p)
+            if process is not None:
+                process(at.mp + 1 - 2 * at.c)
+
+        @pl.loop(0, 4)
+        def _(i):
+            p = at.p + t * (1 - i // 2 * 2)
+            core = i % 2
+
+            @pl.when((p >= 0) & (p <= 3))
+            def _():
+                @pl.when(core != at.c)
+                def _():
+                    await_across(p)
+
+                if process is not None:
+                    process(p * 2 + core)
+
+    for hook in hooks:
+        hook()
     for k in range(chunks):
         for t in range(3):
 
@@ -156,6 +187,68 @@
 
         for p in range(4):
             across(p, k).wait_send()
+
+
+def spread_stages(at, w, g_send, g_recv, a_send, a_recv):
+    def unit(a, g):
+        return w.at[:, at.seq_at((at.a + 4 + a) % 4, (at.g + 4 + g) % 4)]
+
+    def half(k, g):
+        return w.at[pl.ds(4 * k, 4), at.seq_at(at.a, (at.g + 4 + g) % 4)]
+
+    def g_hop(g, slot, step):
+        return remote(unit(0, g), unit(0, g), g_send.at[slot], g_recv.at[slot], at.g_peer(step))
+
+    def g_onward(g, slot, step):
+        ref = half(slot - 2, g)
+        return remote(ref, ref, g_send.at[slot], g_recv.at[slot], at.g_peer(step))
+
+    def a_hop(a, d, slot, step):
+        ref = unit(a, -d)
+        return remote(ref, ref, a_send.at[slot, d], a_recv.at[slot, d], at.a_peer(step))
+
+    def start():
+        g_hop(0, 0, 1).start()
+        g_hop(0, 1, 3).start()
+
+    def forward():
+        g_hop(-1, 0, 1).wait_recv()
+        g_onward(-1, 2, 1).start()
+        g_hop(1, 1, 3).wait_recv()
+        g_onward(1, 3, 3).start()
+
+    def second():
+        g_onward(2, 2, 1).wait_recv()
+        g_onward(2, 3, 3).wait_recv()
+        for d in range(4):
+            a_hop(0, d, 0, 1).start()
+            a_hop(0, d, 1, 3).start()
+
+    def second_forward():
+        for d in range(4):
+            a_hop(-1, d, 0, 1).wait_recv()
+            if d < 2:
+                a_hop(-1, d, 2, 1).start()
+            a_hop(1, d, 1, 3).wait_recv()
+            if d >= 2:
+                a_hop(1, d, 2, 3).start()
+
+    def finish():
+        for d in range(4):
+            a_hop(2, d, 2, 1).wait_recv()
+        g_hop(0, 0, 1).wait_send()
+        g_hop(0, 1, 3).wait_send()
+        g_onward(-1, 2, 1).wait_send()
+        g_onward(1, 3, 3).wait_send()
+        for d in range(4):
+            a_hop(0, d, 0, 1).wait_send()
+            a_hop(0, d, 1, 3).wait_send()
+            if d < 2:
+                a_hop(-1, d, 2, 1).wait_send()
+            else:
+                a_hop(1, d, 2, 3).wait_send()
+
+    return [start, forward, second, second_forward, finish]
 
 
 def exchange_heads(at, src, dst, send, recv):
@@ -222,35 +315,84 @@
         dst[2 * pair + 1] = jnp.where(low, f_turned, s).astype(BF16)
 
 
-def project(buf, gain_ref, weights, acc, count):
+def projector(buf, gain_ref, weights, acc, squares, count):
     acc[...] = jnp.zeros_like(acc)
-
-    def step(j, squares):
+    squares[...] = jnp.zeros_like(squares)
+
+    def process(j):
         block = buf[j].astype(F32)
         scaled = (block * gain_ref[j]).astype(BF16)
         for i in range(count):
             acc[i] += jnp.dot(
                 scaled, weights[i, pl.ds(pl.multiple_of(j * 512, 512), 512), :], preferred_element_type=F32
             )
-        return squares + jnp.sum(block * block, axis=1, keepdims=True)
-
-    squares = lax.fori_loop(0, 8, step, jnp.zeros((ROWS, 1), F32))
-    return lax.rsqrt(squares / 4096.0 + EPS)
+        powers = block * block
+        squares[...] += sum(powers[:, 128 * i : 128 * i + 128] for i in range(4))
+
+    return process
+
+
+def row_scale(squares):
+    return lax.rsqrt(jnp.sum(squares[...], axis=1, keepdims=True) / 4096.0 + EPS)
 
 
 def self_kernel(
-    x_ref, gain_ref, w_ref, q_out, kv_out,
-    buf, w_vmem, acc, q4, kv4, load_sem,
+    x_ref, gain_ref, w_ref, wo_ref, wc_ref, q_out, kv_out, wo_out, wc_out,
+    buf, w_vmem, acc, squares, q4, kv4, load_sem, own_sem,
     line_send, line_recv, kv_send, kv_recv, q_send, q_recv, ring_send, ring_recv,
+    wo_send, wo_recv, wc_send, wc_recv, g_send, g_recv, a_send, a_recv,
 ):
     at = Place()
     load = pltpu.make_async_copy(w_ref, w_vmem, load_sem)
     load.start()
     buf[at.mp] = x_ref[...]
-    barrier_with(at.line_devices() + at.a_devices() + at.g_devices())
-    line_gather(at, buf, 2, line_send, line_recv)
+
+    def wo_piece(j):
+        return wo_ref.at[pl.ds(pl.multiple_of(at.seq * 16, 16), 16), pl.ds(pl.multiple_of(j * 512, 512), 512)]
+
+    def wc_piece(j):
+        return wc_ref.at[1, pl.ds(pl.multiple_of(j * 512 + at.seq * 32, 32), 32)]
+
+    own_wo = pltpu.make_async_copy(wo_piece(at.mp), wo_out.at[at.mp, at.seq], own_sem.at[0])
+    own_wo.start()
+    own_wc = pltpu.make_async_copy(wc_piece(at.mp), wc_out.at[at.mp], own_sem.at[1])
+    own_wc.start()
+    barrier_with(at.mp_devices() + at.a_devices() + at.g_devices())
+
+    def wo_copy(d):
+        to = (at.mp + d) % 8
+        return remote(
+            wo_piece(to), wo_out.at[at.mp, at.seq], wo_send.at[d], wo_recv.at[d], {"mp": to}
+        )
+
+    def wo_from(d):
+        ref = wo_out.at[(at.mp + 8 - d) % 8, at.seq]
+        return remote(ref, ref, wo_send.at[d], wo_recv.at[d], {"mp": (at.mp + d) % 8})
+
+    def wc_copy(d):
+        to = (at.mp + d) % 8
+        return remote(wc_piece(to), wc_out.at[at.mp], wc_send.at[d], wc_recv.at[d], {"mp": to})
+
+    def wc_from(d):
+        ref = wc_out.at[(at.mp + 8 - d) % 8]
+        return remote(ref, ref, wc_send.at[d], wc_recv.at[d], {"mp": (at.mp + d) % 8})
+
+    for d in range(1, 8):
+        wo_copy(d).start()
+    process = projector(buf, gain_ref, w_vmem, acc, squares, 3)
+    stages = spread_stages(at, wo_out, g_send, g_recv, a_send, a_recv)
+
+    def first_stage():
+        own_wo.wait()
+        for d in range(1, 8):
+            wo_from(d).wait_recv()
+        stages[0]()
+
     load.wait()
-    scale = project(buf, gain_ref, w_vmem, acc, 3)
+    line_gather(at, buf, 2, line_send, line_recv, [first_stage] + stages[1:4], process)
+    for d in range(1, 8):
+        wc_copy(d).start()
+    scale = row_scale(squares)
     pair_heads(acc[1] * scale, acc[2] * scale, kv4)
     kv_copies = exchange_heads(at, kv4, kv_out.at[at.g], kv_send, kv_recv)
     pair_heads(acc[0] * (scale * QSCALE), None, q4)
@@ -267,6 +409,13 @@
         from_a(at, q_out, q_send, q_recv, d).wait_recv()
     for copy in kv_copies + q_copies:
         copy.wait_send()
+    stages[4]()
+    own_wc.wait()
+    for d in range(1, 8):
+        wc_from(d).wait_recv()
+    for d in range(1, 8):
+        wo_copy(d).wait_send()
+        wc_copy(d).wait_send()
 
 
 def params(collective_id):
@@ -280,26 +429,38 @@
 DMA = pltpu.SemaphoreType.DMA
 
 
-def self_project(x, gain, weights):
+def self_project(x, gain, weights, wo, wc):
     return pl.pallas_call(
         self_kernel,
         out_shape=(
             jax.ShapeDtypeStruct((4, ROWS, 128), BF16),
             jax.ShapeDtypeStruct((4, 4, ROWS, 128), BF16),
+            jax.ShapeDtypeStruct((8, 16, 16, 512), BF16),
+            jax.ShapeDtypeStruct((8, 32, 256), BF16),
         ),
-        in_specs=[VMEM, VMEM, ANY],
-        out_specs=(VMEM, VMEM),
+        in_specs=[VMEM, VMEM, ANY, ANY, ANY],
+        out_specs=(VMEM, VMEM, VMEM, VMEM),
         scratch_shapes=[
             pltpu.VMEM((8, ROWS, 512), BF16),
             pltpu.VMEM((3, 4096, 256), BF16),
             pltpu.VMEM((3, ROWS, 256), F32),
+            pltpu.VMEM((ROWS, 128), F32),
             pltpu.VMEM((4, ROWS, 128), BF16),
             pltpu.VMEM((4, ROWS, 128), BF16),
             DMA,
+            DMA((2,)),
             DMA((10, 2)),
             DMA((8, 2)),
             DMA((4,)),
             DMA((4,)),
+            DMA((4,)),
+            DMA((4,)),
+            DMA((3, 4)),
+            DMA((3, 4)),
+            DMA((8,)),
+            DMA((8,)),
+            DMA((8,)),
+            DMA((8,)),
             DMA((4,)),
             DMA((4,)),
             DMA((3, 4)),
@@ -307,7 +468,7 @@
         ],
         compiler_params=params(0),
         name="self_project",
-    )(x, gain, weights)
+    )(x, gain, weights, wo, wc)
 
 
 def attend_kernel(masked, lengths_ref, q_ref, kv_ref, out_ref, scores):
@@ -360,7 +521,7 @@
     )(lengths, q, kv)
 
 
-def collect_mixed(at, mixed_ref, heads, buf, send, recv, line_send, line_recv):
+def collect_mixed(at, mixed_ref, heads, buf, send, recv, line_send, line_recv, hooks=()):
     copies = exchange_heads(at, mixed_ref, heads, send, recv)
     heads[at.a] = mixed_ref[at.a]
     for d in (1, 2, 3):
@@ -372,14 +533,15 @@
         buf[at.mp, :, pair * 128 : pair * 128 + 128] = jnp.where(low, even, odd).astype(BF16)
     for copy in copies:
         copy.wait_send()
-    line_gather(at, buf, 1, line_send, line_recv)
+    line_gather(at, buf, 1, line_send, line_recv, hooks)
 
 
 def cross_kernel(
-    mixed_ref, wo_ref, x_ref, gain_ref, w_ref, rows_out, q_out, kv_out,
-    heads, mixed_buf, buf, w_vmem, acc, q4, kv4, relay, load_sem,
+    mixed_ref, wo_ref, x_ref, gain_ref, w_ref, wc_ref, rows_out, q_out, kv_out, wc_out,
+    heads, mixed_buf, buf, w_vmem, acc, squares, q4, kv4, relay, load_sem,
     back_send, back_recv, mix_send, mix_recv,
     line_send, line_recv, q_send, q_recv, over_send, over_recv, relay_send, relay_recv, ring_send, ring_recv,
+    g_send, g_recv, a_send, a_recv,
 ):
     at = Place()
     load = pltpu.make_async_copy(w_ref, w_vmem, load_sem)
@@ -397,15 +559,24 @@
         + [(over(d), None) for d in range(4)]
         + [({"mp": far}, decoder)]
     )
-    collect_mixed(at, mixed_ref, heads, mixed_buf, back_send, back_recv, mix_send, mix_recv)
+    stages = spread_stages(at, wc_out, g_send, g_recv, a_send, a_recv)
+
+    def first_stage():
+        wc_out[:, at.seq] = wc_ref[...]
+        stages[0]()
+
+    collect_mixed(
+        at, mixed_ref, heads, mixed_buf, back_send, back_recv, mix_send, mix_recv, [first_stage, stages[1], stages[2]]
+    )
     total = x_ref[...].astype(F32)
     for j in range(8):
-        total += jnp.dot(mixed_buf[j], wo_ref[j], preferred_element_type=F32)
+        total += jnp.dot(mixed_buf[j], wo_ref[j].reshape(256, 512), preferred_element_type=F32)
     rows_out[...] = total
     buf[at.mp] = total.astype(BF16)
-    line_gather(at, buf, 2, line_send, line_recv)
+    process = projector(buf, gain_ref, w_vmem, acc, squares, 2)
     load.wait()
-    scale = project(buf, gain_ref, w_vmem, acc, 2)
+    line_gather(at, buf, 2, line_send, line_recv, [stages[3]], process)
+    scale = row_scale(squares)
 
     def send_over(d):
         return remote(kv4.at[(at.a + d) % 4], relay.at[at.a], over_send.at[d], over_recv.at[d], over(d))
@@ -450,23 +621,27 @@
         for d in range(4):
             onward(d).wait_send()
 
-
-def cross_project(mixed, wo, x, gain, weights):
+    stages[4]()
+
+
+def cross_project(mixed, wo, x, gain, weights, wc):
     return pl.pallas_call(
         cross_kernel,
         out_shape=(
             jax.ShapeDtypeStruct((ROWS, 512), F32),
             jax.ShapeDtypeStruct((4, ROWS, 128), BF16),
             jax.ShapeDtypeStruct((4, 4, ROWS, 128), BF16),
+            jax.ShapeDtypeStruct((8, 16, 32, 256), BF16),
         ),
-        in_specs=[VMEM, VMEM, VMEM, VMEM, ANY],
-        out_specs=(VMEM, VMEM, VMEM),
+        in_specs=[VMEM, VMEM, VMEM, VMEM, ANY, VMEM],
+        out_specs=(VMEM, VMEM, VMEM, VMEM),
         scratch_shapes=[
             pltpu.VMEM((4, ROWS, 128), BF16),
             pltpu.VMEM((8, ROWS, 256), BF16),
             pltpu.VMEM((8, ROWS, 512), BF16),
             pltpu.VMEM((2, 4096, 256), BF16),
             pltpu.VMEM((2, ROWS, 256), F32),
+            pltpu.VMEM((ROWS, 128), F32),
             pltpu.VMEM((4, ROWS, 128), BF16),
             pltpu.VMEM((4, ROWS, 128), BF16),
             pltpu.VMEM((4, ROWS, 128), BF16),
@@ -481,6 +656,10 @@
             DMA((4,)),
             DMA((4,)),
             DMA((4,)),
+            DMA((4,)),
+            DMA((4,)),
+            DMA((3, 4)),
+            DMA((3, 4)),
             DMA((4,)),
             DMA((4,)),
             DMA((3, 4)),
@@ -488,7 +667,7 @@
         ],
         compiler_params=params(1),
         name="cross_project",
-    )(mixed, wo, x, gain, weights)
+    )(mixed, wo, x, gain, weights, wc)
 
 
 def output_kernel(mixed_ref, w_ref, rows_ref, out_ref, heads, buf, back_send, back_recv, line_send, line_recv):
@@ -506,7 +685,7 @@
         total = rows_ref[...]
         for j in range(8):
             total += lax.dot_general(
-                buf[j], w_ref[j], (((1,), (1,)), ((), ())), preferred_element_type=F32
+                buf[j], w_ref[j].reshape(512, 256), (((1,), (1,)), ((), ())), preferred_element_type=F32
             )
         out_ref[...] = total
 
@@ -533,22 +712,15 @@
 def body(
     mantissas, exponents, source_lengths, target_lengths, norm_gains, self_weights, self_output, cross_weights
 ):
-    seq, sec = lax.axis_index("seq"), lax.axis_index("sec")
+    sec = lax.axis_index("sec")
     scale = jnp.exp2(exponents[0].astype(F32))
     x = (mantissas[0].astype(F32).reshape(ROWS, 4, 128) * scale[:, :, None]).reshape(ROWS, 512).astype(BF16)
     gains = norm_gains[0].reshape(2, 8, 1, 512)
     lengths = jnp.where(sec == 1, target_lengths, source_lengths)
 
-    piece = lax.dynamic_index_in_dim(self_output[0].reshape(16, 16, 8, 512), seq, 0, keepdims=False)
-    piece = lax.all_to_all(piece.transpose(1, 0, 2), "mp", 0, 0)
-    wo = lax.all_gather(piece, "seq", axis=0).transpose(1, 0, 2, 3).reshape(8, 256, 512)
-    piece = lax.dynamic_index_in_dim(cross_weights[0, 1].reshape(8, 16, 32, 256), seq, 1, keepdims=False)
-    piece = lax.all_to_all(piece, "mp", 0, 0)
-    wc = lax.all_gather(piece, "seq", axis=0).transpose(1, 0, 2, 3).reshape(8, 512, 256)
-
-    q, kv = self_project(x, gains[0], self_weights[0])
+    q, kv, wo, wc = self_project(x, gains[0], self_weights[0], self_output[0], cross_weights[0])
     mixed = attend(lengths, q, kv, True)
-    rows, q, kv = cross_project(mixed, wo, x, gains[1], cross_weights[0])
+    rows, q, kv, wc = cross_project(mixed, wo, x, gains[1], cross_weights[0], wc)
     mixed = attend(lengths, q, kv, False)
     return output(mixed, wc, rows)[None]
 

time: 239 us -> 167 us (0.70)
  waiting for transfers between devices: 36.9 us -> 0 us
  blocking collectives: 19.4 us -> 0 us
  between operations: 13.6 us -> 0.07 us
  local copies, waits for them, and re-layouts: 10.4 us -> 5.03 us
  Pallas kernels: 156 us -> 159 us
    all_gather x2 -> x0, waiting for transfers between devices: 36.8 us -> none  [body(): lax.all_gather(piece, 'seq', axis=0).transpose(1, 0, 2, 3)]
    all_to_all x2 -> x0, blocking collectives: 19.4 us -> none  [the longest x1 9.84 us: body(): piece = lax.all_to_all(piece, 'mp', 0, 0)]
    transpose x2 -> x0, local copies, waits for them, and re-layouts: 5 us -> none  [body(): lax.all_gather(piece, 'seq', axis=0).transpose(1, 0, 2, 3)]
  transfers between devices with their start and end apart: 2 -> 0, of which waited for: 1 -> 0; matrix products, arithmetic and copies ran while one was open for 2% -> 0% of each run, Pallas kernels for 23% -> 0%
where the time goes in v2:
time: 167 us; the launch traced here: 166 us
  Pallas kernels  159 us (95%)
  local copies, waits for them, and re-layouts  5.03 us (3%)
  other arithmetic  2.39 us (1%)
    pallas_call x1, Pallas kernels, cross_project(): pl.pallas_call(cross_kernel, out_shape=(jax.ShapeDtypeStruct((ROWS, 512),...  73.2 us
    pallas_call x1, Pallas kernels, self_project(): pl.pallas_call(self_kernel, out_shape=(jax.ShapeDtypeStruct((4, ROWS, 128...  45.9 us
    pallas_call x1, Pallas kernels, output(): pl.pallas_call(output_kernel, out_shape=jax.ShapeDtypeStruct((ROWS, 512),...  21.6 us
    pallas_call x2, Pallas kernels, attend(): pl.pallas_call(functools.partial(attend_kernel, masked), out_shape=jax.Sh...  18.1 us
    unnamed x5, local copies, waits for them, and re-layouts  3.7 us

profile of v2, /device:TPU:129, one launch (start us, length us, event | category | flops | bytes accessed | tf_op | source)
XLA Modules:
  0.0 166.2 jit_solution(10365504001199337005)
XLA Ops:
  0.0 0.7 broadcast_select_fusion.lengths_ref
  0.7 0.7 exponential_bitcast_fusion
  1.4 0.9 fusion.1
  2.2 0.1 copy.9
  2.4 0.3 mul.11
  2.7 1.0 fusion.x_ref
  3.7 45.9 %self_project.1 = (bf16[4,256,128]{2,1,0:T(8,128)(2,1)S(1)}, bf16[4,4,256,128]{3,2,1,0:T(8,128)(2,1)S(1)}, bf16[8,16,16,512]{3,2,1,0:T(8,128)(2,1)S(1)}, bf16[8,32,256]{2,1,0:T(8,128)(2,1)S(1)}) custom-call(bf16[256,512]{1,0:T(8,128)(2,1)S(1)} %fusion.x_ref, f32[8,1,512]{2,1,0:T(1,128)S(1)} %bitcast.18, bf16[3,4096,256]{2,1,0:T(8,128)(2,1)} %bitcast.21, ...), custom_call_target="tpu_custom_call" | custom-call | tf_op jit(solution)/shard_map/self_project/pallas_call | solution.py:433
  49.7 0.0 copy-start
  49.7 1.3 copy-done
  51.0 10.0 %attend_masked.1.mixed_ref = bf16[4,256,128]{2,1,0:T(8,128)(2,1)S(1)} custom-call(s32[3]{0:T(128)S(1)} %broadcast_select_fusion.lengths_ref, bf16[4,256,128]{2,1,0:T(8,128)(2,1)S(1)} %get-tuple-element.13.q_ref, bf16[4,4,256,128]{3,2,1,0:T(8,128)(2,1)S(1)} %get-tuple-element.14.kv_ref), custom_call_target="tpu_custom_call" | custom-call | tf_op jit(solution)/shard_map/attend_masked/pallas_call | solution.py:508
  61.0 73.2 %cross_project.1 = (f32[256,512]{1,0:T(8,128)S(1)}, bf16[4,256,128]{2,1,0:T(8,128)(2,1)S(1)}, bf16[4,4,256,128]{3,2,1,0:T(8,128)(2,1)S(1)}, bf16[8,16,32,256]{3,2,1,0:T(8,128)(2,1)}) custom-call(bf16[4,256,128]{2,1,0:T(8,128)(2,1)S(1)} %attend_masked.1.mixed_ref, bf16[8,16,16,512]{3,2,1,0:T(8,128)(2,1)} %copy-done, bf16[256,512]{1,0:T(8,128)(2,1)S(1)} %fusion.x_ref, ...), custom_call_target="tpu_custom_call" | custom-call | tf_op jit(solution)/shard_map/cross_project/pallas_call | solution.py:628
  134.2 8.1 %attend_all.1.mixed_ref = bf16[4,256,128]{2,1,0:T(8,128)(2,1)S(1)} custom-call(s32[3]{0:T(128)S(1)} %broadcast_select_fusion.lengths_ref, bf16[4,256,128]{2,1,0:T(8,128)(2,1)S(1)} %get-tuple-element.17.q_ref, bf16[4,4,256,128]{3,2,1,0:T(8,128)(2,1)S(1)} %get-tuple-element.18.kv_ref), custom_call_target="tpu_custom_call" | custom-call | tf_op jit(solution)/shard_map/attend_all/pallas_call | solution.py:508
  142.2 0.0 copy-start.1
  142.3 1.6 copy-done.1
  143.8 21.6 %output.1 = f32[256,512]{1,0:T(8,128)S(1)} custom-call(bf16[4,256,128]{2,1,0:T(8,128)(2,1)S(1)} %attend_all.1.mixed_ref, bf16[8,16,32,256]{3,2,1,0:T(8,128)(2,1)S(1)} %copy-done.1, f32[256,512]{1,0:T(8,128)S(1)} %get-tuple-element.20.rows_ref), custom_call_target="tpu_custom_call" | custom-call | tf_op jit(solution)/shard_map/output/pallas_call | solution.py:694
  165.4 0.8 copy.13
Async XLA Ops:
  49.7 1.3 copy-start
  142.2 1.6 copy-start.1

commit v3 on v2

v3 whole, which is shorter than its diff:
```python
import math

import jax
import jax.numpy as jnp
from jax import lax
from jax.experimental import pallas as pl
from jax.experimental.pallas import tpu as pltpu
from jax.sharding import PartitionSpec as P

MESH = pl.DeviceIdType.MESH
EPS = 1e-06
F32 = jnp.float32
BF16 = jnp.bfloat16
ROWS = 256
BLOCKS = 16
QSCALE = math.log2(math.e) / 8.0
VMEM_LIMITS = (52 << 20, 44 << 20, 44 << 20)


def remote(src, dst, send, recv, device):
    return pltpu.make_async_remote_copy(
        src_ref=src, dst_ref=dst, send_sem=send, recv_sem=recv, device_id=device, device_id_type=MESH
    )


def signal_all(devices_and_guards):
    barrier = pltpu.get_barrier_semaphore()
    for device, guard in devices_and_guards:
        if guard is None:
            pl.semaphore_signal(barrier, inc=1, device_id=device, device_id_type=MESH)
        else:

            @pl.when(guard)
            def _(device=device):
                pl.semaphore_signal(barrier, inc=1, device_id=device, device_id_type=MESH)


def wait_all(devices_and_guards):
    count = sum(1 if guard is None else guard.astype(jnp.int32) for _, guard in devices_and_guards)
    pl.semaphore_wait(pltpu.get_barrier_semaphore(), count)


class Place:
    def __init__(self):
        self.mp = lax.axis_index("mp")
        self.seq = lax.axis_index("seq")
        self.sec = lax.axis_index("sec")
        self.p = self.mp // 2
        self.c = self.mp % 2
        y, x = self.seq // 4, self.seq % 4
        self.a = jnp.where(self.c == 0, y, x)
        self.g = jnp.where(self.c == 0, x, y)
        self.sa = 4 - 3 * self.c
        self.sg = 1 + 3 * self.c

    def line(self, step):
        return {"mp": self.mp + 2 * step}

    def sibling(self):
        return {"mp": self.p * 2 + 1 - self.c}

    def seq_at(self, a, g):
        return a * self.sa + g * self.sg

    def a_peer(self, d):
        return {"seq": self.seq_at((self.a + d) % 4, self.g)}

    def g_peer(self, d):
        return {"seq": self.seq_at(self.a, (self.g + d) % 4)}

    def line_devices(self):
        return [
            (self.line(1), self.p < 3),
            (self.line(-1), self.p > 0),
            (self.sibling(), None),
        ]

    def mp_devices(self):
        return [({"mp": (self.mp + d) % 8}, None) for d in range(1, 8)]

    def a_devices(self):
        return [(self.a_peer(d), None) for d in (1, 2, 3)]

    def g_devices(self):
        return [(self.g_peer(d), None) for d in (1, 3)]


HALF = ROWS // 2


def half(h):
    return pl.ds(h * HALF, HALF)


class Line:
    def __init__(self, at, buf, send, recv):
        self.at, self.buf, self.send, self.recv = at, buf, send, recv

    def copy(self, block, h, slot, device):
        ref = self.buf.at[block, half(h)]
        return remote(ref, ref, self.send.at[slot, h], self.recv.at[block, h], device)

    def up(self, t, h):
        return self.copy((self.at.p - t) * 2 + self.at.c, h, t, self.at.line(1))

    def down(self, t, h):
        return self.copy((self.at.p + t) * 2 + self.at.c, h, 3 + t, self.at.line(-1))

    def across(self, p, h):
        return self.copy(p * 2 + self.at.c, h, 6 + p, self.at.sibling())

    def begin(self, h):
        at = self.at

        @pl.when(at.p < 3)
        def _():
            self.up(0, h).start()

        @pl.when(at.p > 0)
        def _():
            self.down(0, h).start()

        self.across(at.p, h).start()

    def step(self, t, h):
        at = self.at

        @pl.when(at.p >= t)
        def _():
            self.up(t, h).wait_recv()

            if t < 3:

                @pl.when(at.p < 3)
                def _():
                    self.up(t, h).start()

            self.across(at.p - t, h).start()

        @pl.when(at.p <= 3 - t)
        def _():
            self.down(t, h).wait_recv()

            if t < 3:

                @pl.when(at.p > 0)
                def _():
                    self.down(t, h).start()

            self.across(at.p + t, h).start()

    def siblings(self, h):
        for p in range(4):
            self.copy(p * 2 + 1 - self.at.c, h, 6 + p, self.at.sibling()).wait_recv()

    def finish(self):
        at = self.at
        for h in (0, 1):
            for t in range(3):

                @pl.when((at.p >= t) & (at.p < 3))
                def _():
                    self.up(t, h).wait_send()

                @pl.when((at.p <= 3 - t) & (at.p > 0))
                def _():
                    self.down(t, h).wait_send()

            for p in range(4):
                self.across(p, h).wait_send()


def spread_stages(at, w, g_send, g_recv, a_send, a_recv):
    def unit(a, g):
        return w.at[:, at.seq_at((at.a + 4 + a) % 4, (at.g + 4 + g) % 4)]

    def part(k, g):
        return w.at[pl.ds(4 * k, 4), at.seq_at(at.a, (at.g + 4 + g) % 4)]

    def g_hop(g, slot, step):
        return remote(unit(0, g), unit(0, g), g_send.at[slot], g_recv.at[slot], at.g_peer(step))

    def g_onward(g, slot, step):
        ref = part(slot - 2, g)
        return remote(ref, ref, g_send.at[slot], g_recv.at[slot], at.g_peer(step))

    def a_hop(a, d, slot, step):
        ref = unit(a, -d)
        return remote(ref, ref, a_send.at[slot, d], a_recv.at[slot, d], at.a_peer(step))

    def start():
        g_hop(0, 0, 1).start()
        g_hop(0, 1, 3).start()

    def forward():
        g_hop(-1, 0, 1).wait_recv()
        g_onward(-1, 2, 1).start()
        g_hop(1, 1, 3).wait_recv()
        g_onward(1, 3, 3).start()

    def second():
        g_onward(2, 2, 1).wait_recv()
        g_onward(2, 3, 3).wait_recv()
        for d in range(4):
            a_hop(0, d, 0, 1).start()
            a_hop(0, d, 1, 3).start()

    def second_forward():
        for d in range(4):
            a_hop(-1, d, 0, 1).wait_recv()
            if d < 2:
                a_hop(-1, d, 2, 1).start()
            a_hop(1, d, 1, 3).wait_recv()
            if d >= 2:
                a_hop(1, d, 2, 3).start()

    def finish():
        for d in range(4):
            a_hop(2, d, 2, 1).wait_recv()
        g_hop(0, 0, 1).wait_send()
        g_hop(0, 1, 3).wait_send()
        g_onward(-1, 2, 1).wait_send()
        g_onward(1, 3, 3).wait_send()
        for d in range(4):
            a_hop(0, d, 0, 1).wait_send()
            a_hop(0, d, 1, 3).wait_send()
            if d < 2:
                a_hop(-1, d, 2, 1).wait_send()
            else:
                a_hop(1, d, 2, 3).wait_send()

    return [start, forward, second, second_forward, finish]


class Exchange:
    def __init__(self, at, src, dst, send, recv, pieces):
        self.at, self.src, self.dst, self.send, self.recv = at, src, dst, send, recv
        self.rows = ROWS // pieces

    def to(self, d, k):
        at, rows = self.at, pl.ds(k * self.rows, self.rows)
        return remote(
            self.src.at[(at.a + d) % 4, rows],
            self.dst.at[at.a, rows],
            self.send.at[k, d],
            self.recv.at[k, d],
            at.a_peer(d),
        )

    def start(self, k):
        at, rows = self.at, pl.ds(k * self.rows, self.rows)
        for d in (1, 2, 3):
            self.to(d, k).start()
        self.dst[at.a, rows] = self.src[at.a, rows]

    def arrive(self, d, k):
        at = self.at
        ref = self.dst.at[(at.a + 4 - d) % 4, pl.ds(k * self.rows, self.rows)]
        remote(ref, ref, self.send.at[k, d], self.recv.at[k, d], at.a_peer(d)).wait_recv()

    def arrive_all(self, k):
        for d in (1, 2, 3):
            self.arrive(d, k)

    def finish(self, k):
        for d in (1, 2, 3):
            self.to(d, k).wait_send()


class Ring:
    def __init__(self, at, kv, send, recv):
        self.at, self.kv, self.send, self.recv = at, kv, send, recv

    def hop(self, g, d, h, slot, step):
        at = self.at
        ref = self.kv.at[(at.g + 4 + g) % 4, (at.a + 4 - d) % 4, half(h)]
        return remote(ref, ref, self.send.at[h, slot, d], self.recv.at[h, slot, d], at.g_peer(step))

    def start(self, d, h):
        self.hop(0, d, h, 0, 1).start()
        self.hop(0, d, h, 1, 3).start()

    def forward(self, h):
        for d in range(4):
            self.hop(-1, d, h, 0, 1).wait_recv()
            if d < 2:
                self.hop(-1, d, h, 2, 1).start()
            self.hop(1, d, h, 1, 3).wait_recv()
            if d >= 2:
                self.hop(1, d, h, 2, 3).start()

    def finish(self, h):
        for d in range(4):
            self.hop(2, d, h, 2, 1).wait_recv()
        for d in range(4):
            self.hop(0, d, h, 0, 1).wait_send()
            self.hop(0, d, h, 1, 3).wait_send()
            if d < 2:
                self.hop(-1, d, h, 2, 1).wait_send()
            else:
                self.hop(1, d, h, 2, 3).wait_send()


def pair_heads(first, second, dst, h):
    low = lax.broadcasted_iota(jnp.int32, (HALF, 128), 1) < 64
    rows = half(h)
    for pair in (0, 1):
        columns = slice(pair * 128, pair * 128 + 128)
        f = first[:, columns]
        f_turned = pltpu.roll(f, 64, 1)
        if second is None:
            s = s_turned = jnp.zeros_like(f)
        else:
            s = second[:, columns]
            s_turned = pltpu.roll(s, 64, 1)
        dst[2 * pair, rows] = jnp.where(low, f, s_turned).astype(BF16)
        dst[2 * pair + 1, rows] = jnp.where(low, f_turned, s).astype(BF16)


def decoded(mantissa_ref, exponent_ref):
    scale = jnp.exp2(exponent_ref[...].astype(F32))
    scale = jnp.concatenate([scale, scale], axis=0).T
    return [mantissa_ref[:, 128 * i : 128 * i + 128].astype(F32) * scale[:, i : i + 1] for i in range(4)]


def project(h, buf, gain_ref, which, weights, acc, count):
    rows = half(h)
    acc[:, rows] = jnp.zeros((count, HALF, 256), F32)

    def step(j, squares):
        columns = pl.ds(pl.multiple_of(j * 512, 512), 512)
        block = buf[j, rows].astype(F32)
        scaled = (block * gain_ref[which : which + 1, columns]).astype(BF16)
        for i in range(count):
            acc[i, rows] += jnp.dot(scaled, weights[i, columns, :], preferred_element_type=F32)
        powers = block * block
        return squares + sum(powers[:, 128 * i : 128 * i + 128] for i in range(4))

    squares = lax.fori_loop(0, 8, step, jnp.zeros((HALF, 128), F32))
    return lax.rsqrt(jnp.sum(squares, axis=1, keepdims=True) / 4096.0 + EPS)


def self_kernel(
    mantissa_ref, exponent_ref, gain_ref, w_ref, wo_ref, wc_ref, q_out, kv_out, wo_out, wc_out,
    buf, w_vmem, acc, q4, kv4, load_sem, own_sem,
    line_send, line_recv, kv_send, kv_recv, q_send, q_recv, ring_send, ring_recv,
    wo_send, wo_recv, wc_send, wc_recv, g_send, g_recv, a_send, a_recv,
):
    at = Place()
    peers = at.mp_devices() + at.a_devices() + at.g_devices()
    signal_all(peers)
    load = pltpu.make_async_copy(w_ref, w_vmem, load_sem)
    load.start()

    def wo_piece(j):
        return wo_ref.at[pl.ds(pl.multiple_of(at.seq * 16, 16), 16), pl.ds(pl.multiple_of(j * 512, 512), 512)]

    def wc_piece(j):
        return wc_ref.at[1, pl.ds(pl.multiple_of(j * 512 + at.seq * 32, 32), 32)]

    own_wo = pltpu.make_async_copy(wo_piece(at.mp), wo_out.at[at.mp, at.seq], own_sem.at[0])
    own_wo.start()
    own_wc = pltpu.make_async_copy(wc_piece(at.mp), wc_out.at[at.mp], own_sem.at[1])
    own_wc.start()

    def wo_copy(d):
        to = (at.mp + d) % 8
        return remote(wo_piece(to), wo_out.at[at.mp, at.seq], wo_send.at[d], wo_recv.at[d], {"mp": to})

    def wo_from(d):
        ref = wo_out.at[(at.mp + 8 - d) % 8, at.seq]
        return remote(ref, ref, wo_send.at[d], wo_recv.at[d], {"mp": (at.mp + d) % 8})

    def wc_copy(d):
        to = (at.mp + d) % 8
        return remote(wc_piece(to), wc_out.at[at.mp], wc_send.at[d], wc_recv.at[d], {"mp": to})

    def wc_from(d):
        ref = wc_out.at[(at.mp + 8 - d) % 8]
        return remote(ref, ref, wc_send.at[d], wc_recv.at[d], {"mp": (at.mp + d) % 8})

    line = Line(at, buf, line_send, line_recv)
    kv_exchange = Exchange(at, kv4, kv_out.at[at.g], kv_send, kv_recv, 2)
    q_exchange = Exchange(at, q4, q_out, q_send, q_recv, 2)
    ring = Ring(at, kv_out, ring_send, ring_recv)
    stages = spread_stages(at, wo_out, g_send, g_recv, a_send, a_recv)

    def heads(h):
        scale = project(h, buf, gain_ref, 0, w_vmem, acc, 3)
        rows = half(h)
        pair_heads(acc[1, rows] * scale, acc[2, rows] * scale, kv4, h)
        kv_exchange.start(h)
        pair_heads(acc[0, rows] * (scale * QSCALE), None, q4, h)
        q_exchange.start(h)

    def start_ring(h):
        for d in range(4):
            if d:
                kv_exchange.arrive(d, h)
            ring.start(d, h)

    for i, part in enumerate(decoded(mantissa_ref, exponent_ref)):
        buf[at.mp, :, 128 * i : 128 * i + 128] = part.astype(BF16)
    wait_all(peers)
    line.begin(0)
    for d in range(1, 8):
        wo_copy(d).start()
    line.step(1, 0)
    line.begin(1)
    own_wo.wait()
    for d in range(1, 8):
        wo_from(d).wait_recv()
    stages[0]()
    line.step(2, 0)
    line.step(1, 1)
    stages[1]()
    line.step(3, 0)
    load.wait()
    line.siblings(0)
    heads(0)
    line.step(2, 1)
    stages[2]()
    start_ring(0)
    line.step(3, 1)
    line.siblings(1)
    for d in range(1, 8):
        wc_copy(d).start()
    heads(1)
    stages[3]()
    ring.forward(0)
    start_ring(1)
    ring.forward(1)
    for h in (0, 1):
        q_exchange.arrive_all(h)
        ring.finish(h)
        q_exchange.finish(h)
        kv_exchange.finish(h)
    line.finish()
    stages[4]()
    own_wc.wait()
    for d in range(1, 8):
        wc_from(d).wait_recv()
    for d in range(1, 8):
        wo_copy(d).wait_send()
        wc_copy(d).wait_send()


def params(collective_id):
    return pltpu.CompilerParams(
        collective_id=collective_id, has_side_effects=True, vmem_limit_bytes=VMEM_LIMITS[collective_id]
    )


VMEM = pl.BlockSpec(memory_space=pltpu.VMEM)
SMEM = pl.BlockSpec(memory_space=pltpu.SMEM)
ANY = pl.BlockSpec(memory_space=pltpu.HBM)
DMA = pltpu.SemaphoreType.DMA


def dma(*shapes):
    return [DMA(shape) for shape in shapes]


def self_project(mantissas, exponents, gains, weights, wo, wc):
    return pl.pallas_call(
        self_kernel,
        out_shape=(
            jax.ShapeDtypeStruct((4, ROWS, 128), BF16),
            jax.ShapeDtypeStruct((4, 4, ROWS, 128), BF16),
            jax.ShapeDtypeStruct((8, 16, 16, 512), BF16),
            jax.ShapeDtypeStruct((8, 32, 256), BF16),
        ),
        in_specs=[VMEM, VMEM, VMEM, ANY, ANY, ANY],
        out_specs=(VMEM, VMEM, VMEM, VMEM),
        scratch_shapes=[
            pltpu.VMEM((8, ROWS, 512), BF16),
            pltpu.VMEM((3, 4096, 256), BF16),
            pltpu.VMEM((3, ROWS, 256), F32),
            pltpu.VMEM((4, ROWS, 128), BF16),
            pltpu.VMEM((4, ROWS, 128), BF16),
            DMA,
            *dma((2,), (10, 2), (8, 2), (2, 4), (2, 4), (2, 4), (2, 4), (2, 3, 4), (2, 3, 4)),
            *dma((8,), (8,), (8,), (8,), (4,), (4,), (3, 4), (3, 4)),
        ],
        compiler_params=params(0),
        name="self_project",
    )(mantissas, exponents, gains, weights, wo, wc)


STEP = ROWS // 4


def attention_step(at, c, q_ref, kv_ref, scores, mixed, lengths):
    rows = pl.ds(c * STEP, STEP)
    q = q_ref[:, rows, :].reshape(ROWS, 128)
    if lengths is not None:
        index = lax.broadcasted_iota(jnp.int32, (ROWS, 128), 0)
        lane = lax.broadcasted_iota(jnp.int32, (ROWS, 128), 1)
        row = at.seq_at(index // STEP, at.g) * ROWS + c * STEP + index % STEP
        one = lengths[0]
        two = one + lengths[1]
        begin = jnp.where(row >= two, two, jnp.where(row >= one, one, 0))
        end = jnp.where(row >= two, BLOCKS * ROWS, jnp.where(row >= one, two, one))
        end = jnp.where(at.sec == 1, jnp.minimum(end, row + 1), end)
        after, before = lane - begin, lane - end
    top = jnp.full((ROWS, 128), -jnp.inf, F32)
    for k in range(BLOCKS):
        block = lax.dot_general(
            q, kv_ref[k // 4, k % 4], (((1,), (1,)), ((), ())), preferred_element_type=F32
        )
        base = at.seq_at(k % 4, k // 4) * ROWS
        for i in (0, 1):
            part = block[:, 128 * i : 128 * i + 128]
            if lengths is not None:
                offset = base + 128 * i
                part = jnp.where((after >= -offset) & (before < -offset), part, -jnp.inf)
            scores[k, :, 128 * i : 128 * i + 128] = part
            top = jnp.maximum(top, part)
    top = jnp.max(top, axis=1, keepdims=True)
    total = jnp.zeros((ROWS, 128), F32)
    result = jnp.zeros((ROWS, 128), F32)
    for k in range(BLOCKS):
        weight = jnp.exp2(scores[k] - top)
        total += weight[:, :128] + weight[:, 128:]
        result += jnp.dot(weight.astype(BF16), kv_ref[k // 4, k % 4], preferred_element_type=F32)
    result = (result / jnp.sum(total, axis=1, keepdims=True)).astype(BF16)
    mixed[:, rows, :] = result.reshape(4, STEP, 128)


def attend_and_collect(at, peers, step, back, heads, line, product, after):
    def collect(h):
        back.arrive_all(2 * h)
        back.arrive_all(2 * h + 1)
        low = lax.broadcasted_iota(jnp.int32, (HALF, 128), 1) < 64
        rows = half(h)
        for pair in (0, 1):
            even = pltpu.roll(heads[2 * pair, rows].astype(F32), 64, 1)
            odd = heads[2 * pair + 1, rows].astype(F32)
            line.buf[at.mp, rows, pair * 128 : pair * 128 + 128] = jnp.where(low, even, odd).astype(BF16)
        line.begin(h)

    step(0)
    wait_all(peers)
    back.start(0)
    step(1)
    back.start(1)
    step(2)
    back.start(2)
    collect(0)
    step(3)
    back.start(3)
    line.step(1, 0)
    collect(1)
    after(0)
    line.step(2, 0)
    line.step(1, 1)
    after(1)
    line.step(3, 0)
    line.step(2, 1)
    line.siblings(0)
    product(0)
    after(2)
    line.step(3, 1)
    after(3)
    line.siblings(1)
    product(1)
    for c in range(4):
        back.finish(c)
    line.finish()


def cross_kernel(
    source_ref, target_ref, q_ref, kv_ref, wo_ref, mantissa_ref, exponent_ref, gain_ref, w_ref, wc_ref,
    rows_out, q_out, kv_out, wc_out,
    scores, mixed, heads, mixed_buf, buf, w_vmem, acc, q4, kv4, relay, load_sem,
    back_send, back_recv, mix_send, mix_recv, line_send, line_recv, q_send, q_recv,
    over_send, over_recv, relay_send, relay_recv, ring_send, ring_recv, g_send, g_recv, a_send, a_recv,
):
    at = Place()
    encoder, decoder = at.sec == 0, at.sec == 1
    far = (at.p + 2) % 4 * 2 + at.c

    def over_device(d):
        return {"seq": at.seq_at((at.a + d) % 4, at.g), "sec": 1 - at.sec, "mp": far}

    peers = (
        at.line_devices()
        + at.a_devices()
        + at.g_devices()
        + [(over_device(d), None) for d in range(4)]
        + [({"mp": far}, decoder)]
    )
    signal_all(peers)
    load = pltpu.make_async_copy(w_ref, w_vmem, load_sem)
    load.start()
    lengths = [jnp.where(decoder, target_ref[i], source_ref[i]) for i in (0, 1)]
    for i, part in enumerate(decoded(mantissa_ref, exponent_ref)):
        rows_out[:, 128 * i : 128 * i + 128] = part
    back = Exchange(at, mixed, heads, back_send, back_recv, 4)
    mix_line = Line(at, mixed_buf, mix_send, mix_recv)
    line = Line(at, buf, line_send, line_recv)
    stages = spread_stages(at, wc_out, g_send, g_recv, a_send, a_recv)

    def step(c):
        attention_step(at, c, q_ref, kv_ref, scores, mixed, lengths)

    def product(h):
        rows = half(h)
        total = rows_out[rows]
        for j in range(8):
            total += jnp.dot(mixed_buf[j, rows], wo_ref[j].reshape(256, 512), preferred_element_type=F32)
        rows_out[rows] = total
        buf[at.mp, rows] = total.astype(BF16)
        line.begin(h)

    def after(n):
        if n == 0:
            wc_out[:, at.seq] = wc_ref[...]
            stages[0]()
        elif n == 1:
            stages[1]()
        elif n == 2:
            stages[2]()
        else:
            line.step(1, 0)

    attend_and_collect(at, peers, step, back, heads, mix_line, product, after)
    line.step(2, 0)
    line.step(1, 1)
    stages[3]()
    line.step(3, 0)
    line.step(2, 1)
    load.wait()
    line.siblings(0)

    def over(d, h):
        rows = half(h)
        return remote(
            kv4.at[(at.a + d) % 4, rows], relay.at[at.a, rows], over_send.at[h, d], over_recv.at[h, d], over_device(d)
        )

    def relayed(d, h):
        ref = relay.at[(at.a + 4 - d) % 4, half(h)]
        return remote(ref, ref, over_send.at[h, d], over_recv.at[h, d], over_device(d))

    def onward(d, h):
        source, rows = (at.a + 4 - d) % 4, half(h)
        return remote(
            relay.at[source, rows], kv_out.at[at.g, source, rows], relay_send.at[h, d], relay_recv.at[h, d], {"mp": far}
        )

    q_exchange = Exchange(at, q4, q_out, q_send, q_recv, 2)
    ring = Ring(at, kv_out, ring_send, ring_recv)

    def send_heads(h):
        scale = project(h, buf, gain_ref, 1, w_vmem, acc, 2)
        rows = half(h)

        @pl.when(encoder)
        def _():
            pair_heads(acc[0, rows] * scale, acc[1, rows] * scale, kv4, h)
            for d in range(4):
                over(d, h).start()

        @pl.when(decoder)
        def _():
            pair_heads(acc[0, rows] * (scale * QSCALE), None, q4, h)
            q_exchange.start(h)

    def start_ring(h):
        for d in range(4):
            onward(d, h).wait_recv()
            ring.start(d, h)

    send_heads(0)
    line.step(3, 1)
    line.siblings(1)
    send_heads(1)

    @pl.when(encoder)
    def _():
        q_out[...] = jnp.zeros_like(q_out)
        kv_out[...] = jnp.zeros_like(kv_out)
        for h in (0, 1):
            for d in range(4):
                over(d, h).wait_send()

    @pl.when(decoder)
    def _():
        for h in (0, 1):
            for d in range(4):
                relayed(d, h).wait_recv()
                onward(d, h).start()
            if h:
                start_ring(0)
        ring.forward(0)
        start_ring(1)
        ring.forward(1)
        for h in (0, 1):
            q_exchange.arrive_all(h)
            ring.finish(h)
            q_exchange.finish(h)
            for d in range(4):
                onward(d, h).wait_send()

    line.finish()
    stages[4]()


def cross_project(source, target, q, kv, wo, mantissas, exponents, gains, weights, wc):
    return pl.pallas_call(
        cross_kernel,
        out_shape=(
            jax.ShapeDtypeStruct((ROWS, 512), F32),
            jax.ShapeDtypeStruct((4, ROWS, 128), BF16),
            jax.ShapeDtypeStruct((4, 4, ROWS, 128), BF16),
            jax.ShapeDtypeStruct((8, 16, 32, 256), BF16),
        ),
        in_specs=[SMEM, SMEM, VMEM, VMEM, VMEM, VMEM, VMEM, VMEM, ANY, VMEM],
        out_specs=(VMEM, VMEM, VMEM, VMEM),
        scratch_shapes=[
            pltpu.VMEM((BLOCKS, ROWS, ROWS), F32),
            pltpu.VMEM((4, ROWS, 128), BF16),
            pltpu.VMEM((4, ROWS, 128), BF16),
            pltpu.VMEM((8, ROWS, 256), BF16),
            pltpu.VMEM((8, ROWS, 512), BF16),
            pltpu.VMEM((2, 4096, 256), BF16),
            pltpu.VMEM((2, ROWS, 256), F32),
            pltpu.VMEM((4, ROWS, 128), BF16),
            pltpu.VMEM((4, ROWS, 128), BF16),
            pltpu.VMEM((4, ROWS, 128), BF16),
            DMA,
            *dma((4, 4), (4, 4), (10, 2), (8, 2), (10, 2), (8, 2), (2, 4), (2, 4)),
            *dma((2, 4), (2, 4), (2, 4), (2, 4), (2, 3, 4), (2, 3, 4), (4,), (4,), (3, 4), (3, 4)),
        ],
        compiler_params=params(1),
        name="cross_project",
    )(source, target, q, kv, wo, mantissas, exponents, gains, weights, wc)


def output_kernel(
    q_ref, kv_ref, w_ref, rows_ref, out_ref, scores, mixed, heads, buf, back_send, back_recv, line_send, line_recv
):
    at = Place()
    peers = at.line_devices() + at.a_devices()
    signal_all(peers)

    @pl.when(at.sec == 0)
    def _():
        out_ref[...] = rows_ref[...]
        wait_all(peers)

    @pl.when(at.sec == 1)
    def _():
        back = Exchange(at, mixed, heads, back_send, back_recv, 4)
        line = Line(at, buf, line_send, line_recv)

        def step(c):
            attention_step(at, c, q_ref, kv_ref, scores, mixed, None)

        def product(h):
            rows = half(h)
            total = rows_ref[rows]
            for j in range(8):
                total += lax.dot_general(
                    buf[j, rows], w_ref[j].reshape(512, 256), (((1,), (1,)), ((), ())), preferred_element_type=F32
                )
            out_ref[rows] = total

        attend_and_collect(at, peers, step, back, heads, line, product, lambda n: None)


def output(q, kv, weights, rows):
    return pl.pallas_call(
        output_kernel,
        out_shape=jax.ShapeDtypeStruct((ROWS, 512), F32),
        in_specs=[VMEM, VMEM, VMEM, VMEM],
        out_specs=VMEM,
        scratch_shapes=[
            pltpu.VMEM((BLOCKS, ROWS, ROWS), F32),
            pltpu.VMEM((4, ROWS, 128), BF16),
            pltpu.VMEM((4, ROWS, 128), BF16),
            pltpu.VMEM((8, ROWS, 256), BF16),
            *dma((4, 4), (4, 4), (10, 2), (8, 2)),
        ],
        compiler_params=params(2),
        name="output",
    )(q, kv, weights, rows)


def body(
    mantissas, exponents, source_lengths, target_lengths, norm_gains, self_weights, self_output, cross_weights
):
    x, e, gains = mantissas[0], exponents[0].T, norm_gains[0]
    q, kv, wo, wc = self_project(x, e, gains, self_weights[0], self_output[0], cross_weights[0])
    rows, q, kv, wc = cross_project(
        source_lengths, target_lengths, q, kv, wo, x, e, gains, cross_weights[0], wc
    )
    return output(q, kv, wc, rows)[None]


def solution(mesh):
    in_specs = (
        P("sec", "seq", "mp"),
        P("sec", "seq", "mp"),
        P(),
        P(),
        P("sec", None, None),
        P("sec", None, None, "mp"),
        P("sec", "mp", None),
        P("sec", None, None, "mp"),
    )
    out_specs = P("sec", "seq", "mp")
    return jax.shard_map(body, mesh=mesh, in_specs=in_specs, out_specs=out_specs, check_vma=False)
```

time: 167 us -> 152 us (0.910)
  Pallas kernels: 159 us -> 146 us
  other arithmetic: 2.39 us -> 0 us
    pallas_call x2 -> x0, Pallas kernels: 18.1 us -> none  [attend(): pl.pallas_call(functools.partial(attend_kernel, masked), out_shape=jax.Sh...]
    pallas_call x1, Pallas kernels: 21.6 us -> 28.6 us  [output(): pl.pallas_call(output_kernel, out_shape=jax.ShapeDtypeStruct((ROWS, 512),...]
    unnamed x5 -> x13, local copies, waits for them, and re-layouts: 3.7 us -> 4.78 us
where the time goes in v3:
time: 152 us; the launch traced here: 151 us
  Pallas kernels  146 us (96%)
  local copies, waits for them, and re-layouts  4.78 us (3%)
    pallas_call x1, Pallas kernels, cross_project(): pl.pallas_call(cross_kernel, out_shape=(jax.ShapeDtypeStruct((ROWS, 512),...  72.1 us
    pallas_call x1, Pallas kernels, self_project(): pl.pallas_call(self_kernel, out_shape=(jax.ShapeDtypeStruct((4, ROWS, 128...  45.8 us
    pallas_call x1, Pallas kernels, output(): pl.pallas_call(output_kernel, out_shape=jax.ShapeDtypeStruct((ROWS, 512),...  28.6 us
    unnamed x13, local copies, waits for them, and re-layouts  4.78 us

profile of v3, /device:TPU:129, one launch (start us, length us, event | category | flops | bytes accessed | tf_op | source)
XLA Modules:
  0.0 151.3 jit_solution(3666293430655923859)
XLA Ops:
  0.0 0.0 copy-start.1
  0.0 0.9 copy-done.1
  1.0 0.0 copy-start.2
  1.0 0.8 copy-done.2
  1.7 0.0 copy-start.3
  1.7 0.7 copy-done.3
  2.4 0.0 copy-start.4
  2.4 0.0 copy-start.5
  2.4 45.8 %self_project.1 = (bf16[4,256,128]{2,1,0:T(8,128)(2,1)S(1)}, bf16[4,4,256,128]{3,2,1,0:T(8,128)(2,1)S(1)}, bf16[8,16,16,512]{3,2,1,0:T(8,128)(2,1)}, bf16[8,32,256]{2,1,0:T(8,128)(2,1)S(1)}) custom-call(bf16[256,512]{1,0:T(8,128)(2,1)S(1)} %bitcast.10, s32[4,256]{1,0:T(4,128)S(1)} %bitcast.14, f32[2,4096]{1,0:T(2,128)S(1)} %bitcast.12, ...), custom_call_target="tpu_custom_call" | custom-call | tf_op jit(solution)/shard_map/self_project/pallas_call | solution.py:465
  48.2 0.0 copy-done.4
  48.2 0.0 copy-done.5
  48.2 0.0 copy-start
  48.2 1.6 %copy-done = bf16[8,16,16,512]{3,2,1,0:T(8,128)(2,1)S(1)} copy-done((bf16[8,16,16,512]{3,2,1,0:T(8,128)(2,1)S(1)}, bf16[8,16,16,512]{3,2,1,0:T(8,128)(2,1)}, u32[]{:S(2)}) %copy-start) | copy-done | bytes 2097176
  49.8 72.1 %cross_project.1 = (f32[256,512]{1,0:T(8,128)S(1)}, bf16[4,256,128]{2,1,0:T(8,128)(2,1)S(1)}, bf16[4,4,256,128]{3,2,1,0:T(8,128)(2,1)S(1)}, bf16[8,16,32,256]{3,2,1,0:T(8,128)(2,1)S(1)}) custom-call(s32[3]{0:T(128)S(1)} %copy-done.4, s32[3]{0:T(128)S(1)} %copy-done.5, bf16[4,256,128]{2,1,0:T(8,128)(2,1)S(1)} %get-tuple-element.13.q_ref, ...), custom_call_target="tpu_custom_call" | custom-call | tf_op jit(solution)/shard_map/cross_project/pallas_call | solution.py:711
  121.9 28.6 %output.1 = f32[256,512]{1,0:T(8,128)S(1)} custom-call(bf16[4,256,128]{2,1,0:T(8,128)(2,1)S(1)} %get-tuple-element.17.q_ref, bf16[4,4,256,128]{3,2,1,0:T(8,128)(2,1)S(1)} %get-tuple-element.18.kv_ref, bf16[8,16,32,256]{3,2,1,0:T(8,128)(2,1)S(1)} %get-tuple-element.19.w_ref, f32[256,512]{1,0:T(8,128)S(1)} %get-tuple-element.20.rows_ref), custom_call_target="tpu_custom_call" | custom-call | tf_op jit(solution)/shard_map/output/pallas_call | solution.py:774
  150.5 0.8 copy.10
Async XLA Ops:
  0.0 0.9 copy-start.1
  1.0 0.8 copy-start.2
  1.7 0.7 copy-start.3
  2.4 45.8 %copy-start.4 = (s32[3]{0:T(128)S(1)}, s32[3]{0:T(128)}, u32[]{:S(2)}) copy-start(s32[3]{0:T(128)} %source_ref.1) | copy-start | bytes 40
  2.4 45.8 %copy-start.5 = (s32[3]{0:T(128)S(1)}, s32[3]{0:T(128)}, u32[]{:S(2)}) copy-start(s32[3]{0:T(128)} %target_ref.1) | copy-start | bytes 40
  48.2 1.6 %copy-start = (bf16[8,16,16,512]{3,2,1,0:T(8,128)(2,1)S(1)}, bf16[8,16,16,512]{3,2,1,0:T(8,128)(2,1)}, u32[]{:S(2)}) copy-start(bf16[8,16,16,512]{3,2,1,0:T(8,128)(2,1)} %get-tuple-element.15.wo_ref) | copy-start | bytes 6291460

commit v4 on v3

--- a/solution.py
+++ b/solution.py
@@ -14,7 +14,7 @@
 ROWS = 256
 BLOCKS = 16
 QSCALE = math.log2(math.e) / 8.0
-VMEM_LIMITS = (52 << 20, 44 << 20, 44 << 20)
+VMEM_LIMITS = (52 << 20, 50 << 20, 48 << 20)
 
 
 def remote(src, dst, send, recv, device):
@@ -170,68 +170,6 @@
                 self.across(p, h).wait_send()
 
 
-def spread_stages(at, w, g_send, g_recv, a_send, a_recv):
-    def unit(a, g):
-        return w.at[:, at.seq_at((at.a + 4 + a) % 4, (at.g + 4 + g) % 4)]
-
-    def part(k, g):
-        return w.at[pl.ds(4 * k, 4), at.seq_at(at.a, (at.g + 4 + g) % 4)]
-
-    def g_hop(g, slot, step):
-        return remote(unit(0, g), unit(0, g), g_send.at[slot], g_recv.at[slot], at.g_peer(step))
-
-    def g_onward(g, slot, step):
-        ref = part(slot - 2, g)
-        return remote(ref, ref, g_send.at[slot], g_recv.at[slot], at.g_peer(step))
-
-    def a_hop(a, d, slot, step):
-        ref = unit(a, -d)
-        return remote(ref, ref, a_send.at[slot, d], a_recv.at[slot, d], at.a_peer(step))
-
-    def start():
-        g_hop(0, 0, 1).start()
-        g_hop(0, 1, 3).start()
-
-    def forward():
-        g_hop(-1, 0, 1).wait_recv()
-        g_onward(-1, 2, 1).start()
-        g_hop(1, 1, 3).wait_recv()
-        g_onward(1, 3, 3).start()
-
-    def second():
-        g_onward(2, 2, 1).wait_recv()
-        g_onward(2, 3, 3).wait_recv()
-        for d in range(4):
-            a_hop(0, d, 0, 1).start()
-            a_hop(0, d, 1, 3).start()
-
-    def second_forward():
-        for d in range(4):
-            a_hop(-1, d, 0, 1).wait_recv()
-            if d < 2:
-                a_hop(-1, d, 2, 1).start()
-            a_hop(1, d, 1, 3).wait_recv()
-            if d >= 2:
-                a_hop(1, d, 2, 3).start()
-
-    def finish():
-        for d in range(4):
-            a_hop(2, d, 2, 1).wait_recv()
-        g_hop(0, 0, 1).wait_send()
-        g_hop(0, 1, 3).wait_send()
-        g_onward(-1, 2, 1).wait_send()
-        g_onward(1, 3, 3).wait_send()
-        for d in range(4):
-            a_hop(0, d, 0, 1).wait_send()
-            a_hop(0, d, 1, 3).wait_send()
-            if d < 2:
-                a_hop(-1, d, 2, 1).wait_send()
-            else:
-                a_hop(1, d, 2, 3).wait_send()
-
-    return [start, forward, second, second_forward, finish]
-
-
 class Exchange:
     def __init__(self, at, src, dst, send, recv, pieces):
         self.at, self.src, self.dst, self.send, self.recv = at, src, dst, send, recv
@@ -299,6 +237,75 @@
                 self.hop(-1, d, h, 2, 1).wait_send()
             else:
                 self.hop(1, d, h, 2, 3).wait_send()
+
+
+class FirstSpread:
+    def __init__(self, at, part, send, recv):
+        self.at, self.part, self.send, self.recv = at, part, send, recv
+
+    def hop(self, g, slot, step):
+        ref = self.part.at[(self.at.g + 4 + g) % 4]
+        if slot >= 2:
+            ref = ref.at[pl.ds(4 * (slot - 2), 4)]
+        return remote(ref, ref, self.send.at[slot], self.recv.at[slot], self.at.g_peer(step))
+
+    def start(self):
+        self.hop(0, 0, 1).start()
+        self.hop(0, 1, 3).start()
+
+    def forward(self):
+        self.hop(-1, 0, 1).wait_recv()
+        self.hop(-1, 2, 1).start()
+        self.hop(1, 1, 3).wait_recv()
+        self.hop(1, 3, 3).start()
+
+    def finish(self):
+        self.hop(2, 2, 1).wait_recv()
+        self.hop(2, 3, 3).wait_recv()
+        self.hop(0, 0, 1).wait_send()
+        self.hop(0, 1, 3).wait_send()
+        self.hop(-1, 2, 1).wait_send()
+        self.hop(1, 3, 3).wait_send()
+
+
+class SecondSpread:
+    def __init__(self, at, part, whole, send, recv):
+        self.at, self.part, self.whole, self.send, self.recv = at, part, whole, send, recv
+
+    def hop(self, a, d, slot, step):
+        at = self.at
+        g = (at.g + 4 - d) % 4
+        dst = self.whole.at[:, at.seq_at((at.a + 4 + a) % 4, g)]
+        src = self.part.at[g] if a == 0 else dst
+        return remote(src, dst, self.send.at[slot, d], self.recv.at[slot, d], at.a_peer(step))
+
+    def start(self):
+        at = self.at
+        for d in range(4):
+            self.hop(0, d, 0, 1).start()
+            self.hop(0, d, 1, 3).start()
+        for g in range(4):
+            self.whole[:, at.seq_at(at.a, g)] = self.part[g]
+
+    def forward(self):
+        for d in range(4):
+            self.hop(-1, d, 0, 1).wait_recv()
+            if d < 2:
+                self.hop(-1, d, 2, 1).start()
+            self.hop(1, d, 1, 3).wait_recv()
+            if d >= 2:
+                self.hop(1, d, 2, 3).start()
+
+    def finish(self):
+        for d in range(4):
+            self.hop(2, d, 2, 1).wait_recv()
+        for d in range(4):
+            self.hop(0, d, 0, 1).wait_send()
+            self.hop(0, d, 1, 3).wait_send()
+            if d < 2:
+                self.hop(-1, d, 2, 1).wait_send()
+            else:
+                self.hop(1, d, 2, 3).wait_send()
 
 
 def pair_heads(first, second, dst, h):
@@ -344,7 +351,7 @@
     mantissa_ref, exponent_ref, gain_ref, w_ref, wo_ref, wc_ref, q_out, kv_out, wo_out, wc_out,
     buf, w_vmem, acc, q4, kv4, load_sem, own_sem,
     line_send, line_recv, kv_send, kv_recv, q_send, q_recv, ring_send, ring_recv,
-    wo_send, wo_recv, wc_send, wc_recv, g_send, g_recv, a_send, a_recv,
+    wo_send, wo_recv, wc_send, wc_recv, g_send, g_recv,
 ):
     at = Place()
     peers = at.mp_devices() + at.a_devices() + at.g_devices()
@@ -358,17 +365,18 @@
     def wc_piece(j):
         return wc_ref.at[1, pl.ds(pl.multiple_of(j * 512 + at.seq * 32, 32), 32)]
 
-    own_wo = pltpu.make_async_copy(wo_piece(at.mp), wo_out.at[at.mp, at.seq], own_sem.at[0])
+    own_wo = pltpu.make_async_copy(wo_piece(at.mp), wo_out.at[at.g, at.mp], own_sem.at[0])
     own_wo.start()
     own_wc = pltpu.make_async_copy(wc_piece(at.mp), wc_out.at[at.mp], own_sem.at[1])
     own_wc.start()
 
     def wo_copy(d):
         to = (at.mp + d) % 8
-        return remote(wo_piece(to), wo_out.at[at.mp, at.seq], wo_send.at[d], wo_recv.at[d], {"mp": to})
+        slot = jnp.where(to % 2 == at.c, at.g, at.a)
+        return remote(wo_piece(to), wo_out.at[slot, at.mp], wo_send.at[d], wo_recv.at[d], {"mp": to})
 
     def wo_from(d):
-        ref = wo_out.at[(at.mp + 8 - d) % 8, at.seq]
+        ref = wo_out.at[at.g, (at.mp + 8 - d) % 8]
         return remote(ref, ref, wo_send.at[d], wo_recv.at[d], {"mp": (at.mp + d) % 8})
 
     def wc_copy(d):
@@ -383,7 +391,7 @@
     kv_exchange = Exchange(at, kv4, kv_out.at[at.g], kv_send, kv_recv, 2)
     q_exchange = Exchange(at, q4, q_out, q_send, q_recv, 2)
     ring = Ring(at, kv_out, ring_send, ring_recv)
-    stages = spread_stages(at, wo_out, g_send, g_recv, a_send, a_recv)
+    spread = FirstSpread(at, wo_out, g_send, g_recv)
 
     def heads(h):
         scale = project(h, buf, gain_ref, 0, w_vmem, acc, 3)
@@ -410,23 +418,21 @@
     own_wo.wait()
     for d in range(1, 8):
         wo_from(d).wait_recv()
-    stages[0]()
+    spread.start()
     line.step(2, 0)
     line.step(1, 1)
-    stages[1]()
+    spread.forward()
     line.step(3, 0)
     load.wait()
     line.siblings(0)
     heads(0)
     line.step(2, 1)
-    stages[2]()
     start_ring(0)
     line.step(3, 1)
     line.siblings(1)
     for d in range(1, 8):
         wc_copy(d).start()
     heads(1)
-    stages[3]()
     ring.forward(0)
     start_ring(1)
     ring.forward(1)
@@ -436,7 +442,7 @@
         q_exchange.finish(h)
         kv_exchange.finish(h)
     line.finish()
-    stages[4]()
+    spread.finish()
     own_wc.wait()
     for d in range(1, 8):
         wc_from(d).wait_recv()
@@ -467,7 +473,7 @@
         out_shape=(
             jax.ShapeDtypeStruct((4, ROWS, 128), BF16),
             jax.ShapeDtypeStruct((4, 4, ROWS, 128), BF16),
-            jax.ShapeDtypeStruct((8, 16, 16, 512), BF16),
+            jax.ShapeDtypeStruct((4, 8, 16, 512), BF16),
             jax.ShapeDtypeStruct((8, 32, 256), BF16),
         ),
         in_specs=[VMEM, VMEM, VMEM, ANY, ANY, ANY],
@@ -480,7 +486,7 @@
             pltpu.VMEM((4, ROWS, 128), BF16),
             DMA,
             *dma((2,), (10, 2), (8, 2), (2, 4), (2, 4), (2, 4), (2, 4), (2, 3, 4), (2, 3, 4)),
-            *dma((8,), (8,), (8,), (8,), (4,), (4,), (3, 4), (3, 4)),
+            *dma((8,), (8,), (8,), (8,), (4,), (4,)),
         ],
         compiler_params=params(0),
         name="self_project",
@@ -527,7 +533,7 @@
     mixed[:, rows, :] = result.reshape(4, STEP, 128)
 
 
-def attend_and_collect(at, peers, step, back, heads, line, product, after):
+def attend_and_collect(at, peers, step, back, heads, line, spread, product, after):
     def collect(h):
         back.arrive_all(2 * h)
         back.arrive_all(2 * h + 1)
@@ -542,6 +548,7 @@
     step(0)
     wait_all(peers)
     back.start(0)
+    spread.start()
     step(1)
     back.start(1)
     step(2)
@@ -551,6 +558,7 @@
     back.start(3)
     line.step(1, 0)
     collect(1)
+    spread.forward()
     after(0)
     line.step(2, 0)
     line.step(1, 1)
@@ -558,6 +566,7 @@
     line.step(3, 0)
     line.step(2, 1)
     line.siblings(0)
+    spread.finish()
     product(0)
     after(2)
     line.step(3, 1)
@@ -572,9 +581,9 @@
 def cross_kernel(
     source_ref, target_ref, q_ref, kv_ref, wo_ref, mantissa_ref, exponent_ref, gain_ref, w_ref, wc_ref,
     rows_out, q_out, kv_out, wc_out,
-    scores, mixed, heads, mixed_buf, buf, w_vmem, acc, q4, kv4, relay, load_sem,
+    scores, mixed, heads, mixed_buf, buf, wo, w_vmem, acc, q4, kv4, load_sem,
     back_send, back_recv, mix_send, mix_recv, line_send, line_recv, q_send, q_recv,
-    over_send, over_recv, relay_send, relay_recv, ring_send, ring_recv, g_send, g_recv, a_send, a_recv,
+    over_send, over_recv, ring_send, ring_recv, g_send, g_recv, a_send, a_recv,
 ):
     at = Place()
     encoder, decoder = at.sec == 0, at.sec == 1
@@ -582,13 +591,16 @@
 
     def over_device(d):
         return {"seq": at.seq_at((at.a + d) % 4, at.g), "sec": 1 - at.sec, "mp": far}
+
+    def far_device(d):
+        return {"seq": at.seq_at((at.a + d) % 4, at.g), "mp": far}
 
     peers = (
         at.line_devices()
         + at.a_devices()
         + at.g_devices()
         + [(over_device(d), None) for d in range(4)]
-        + [({"mp": far}, decoder)]
+        + [(far_device(d), decoder) for d in range(4)]
     )
     signal_all(peers)
     load = pltpu.make_async_copy(w_ref, w_vmem, load_sem)
@@ -599,7 +611,8 @@
     back = Exchange(at, mixed, heads, back_send, back_recv, 4)
     mix_line = Line(at, mixed_buf, mix_send, mix_recv)
     line = Line(at, buf, line_send, line_recv)
-    stages = spread_stages(at, wc_out, g_send, g_recv, a_send, a_recv)
+    spread = SecondSpread(at, wo_ref, wo, a_send, a_recv)
+    wc_spread = FirstSpread(at, wc_out, g_send, g_recv)
 
     def step(c):
         attention_step(at, c, q_ref, kv_ref, scores, mixed, lengths)
@@ -608,26 +621,30 @@
         rows = half(h)
         total = rows_out[rows]
         for j in range(8):
-            total += jnp.dot(mixed_buf[j, rows], wo_ref[j].reshape(256, 512), preferred_element_type=F32)
+            total += jnp.dot(mixed_buf[j, rows], wo[j].reshape(256, 512), preferred_element_type=F32)
         rows_out[rows] = total
         buf[at.mp, rows] = total.astype(BF16)
         line.begin(h)
 
     def after(n):
-        if n == 0:
-            wc_out[:, at.seq] = wc_ref[...]
-            stages[0]()
-        elif n == 1:
-            stages[1]()
-        elif n == 2:
-            stages[2]()
-        else:
+        if n == 3:
             line.step(1, 0)
 
-    attend_and_collect(at, peers, step, back, heads, mix_line, product, after)
+    @pl.when(encoder)
+    def _():
+        wc_out[...] = jnp.zeros_like(wc_out)
+
+    @pl.when(decoder)
+    def _():
+        wc_out[at.g] = wc_ref[...]
+
+    attend_and_collect(at, peers, step, back, heads, mix_line, spread, product, after)
+    @pl.when(decoder)
+    def _():
+        wc_spread.start()
+
     line.step(2, 0)
     line.step(1, 1)
-    stages[3]()
     line.step(3, 0)
     line.step(2, 1)
     load.wait()
@@ -636,20 +653,21 @@
     def over(d, h):
         rows = half(h)
         return remote(
-            kv4.at[(at.a + d) % 4, rows], relay.at[at.a, rows], over_send.at[h, d], over_recv.at[h, d], over_device(d)
+            kv4.at[(at.a + d) % 4, rows], kv_out.at[at.g, at.a, rows], over_send.at[h, d], over_recv.at[h, d], over_device(d)
         )
 
-    def relayed(d, h):
-        ref = relay.at[(at.a + 4 - d) % 4, half(h)]
+    def over_from(d, h):
+        ref = kv_out.at[at.g, (at.a + 4 - d) % 4, half(h)]
         return remote(ref, ref, over_send.at[h, d], over_recv.at[h, d], over_device(d))
 
-    def onward(d, h):
-        source, rows = (at.a + 4 - d) % 4, half(h)
-        return remote(
-            relay.at[source, rows], kv_out.at[at.g, source, rows], relay_send.at[h, d], relay_recv.at[h, d], {"mp": far}
-        )
-
-    q_exchange = Exchange(at, q4, q_out, q_send, q_recv, 2)
+    def query(d, h):
+        rows = half(h)
+        return remote(q4.at[(at.a + d) % 4, rows], q_out.at[at.a, rows], q_send.at[h, d], q_recv.at[h, d], far_device(d))
+
+    def query_from(d, h):
+        ref = q_out.at[(at.a + 4 - d) % 4, half(h)]
+        return remote(ref, ref, q_send.at[h, d], q_recv.at[h, d], far_device(d))
+
     ring = Ring(at, kv_out, ring_send, ring_recv)
 
     def send_heads(h):
@@ -665,46 +683,37 @@
         @pl.when(decoder)
         def _():
             pair_heads(acc[0, rows] * (scale * QSCALE), None, q4, h)
-            q_exchange.start(h)
-
-    def start_ring(h):
-        for d in range(4):
-            onward(d, h).wait_recv()
-            ring.start(d, h)
+            for d in range(4):
+                query(d, h).start()
 
     send_heads(0)
     line.step(3, 1)
     line.siblings(1)
     send_heads(1)
+    line.finish()
+    pieces = [(h, d) for h in (0, 1) for d in range(4)]
 
     @pl.when(encoder)
     def _():
         q_out[...] = jnp.zeros_like(q_out)
         kv_out[...] = jnp.zeros_like(kv_out)
+        for h, d in pieces:
+            over(d, h).wait_send()
+
+    @pl.when(decoder)
+    def _():
+        wc_spread.forward()
         for h in (0, 1):
             for d in range(4):
-                over(d, h).wait_send()
-
-    @pl.when(decoder)
-    def _():
+                over_from(d, h).wait_recv()
+                ring.start(d, h)
+            ring.forward(h)
+        wc_spread.finish()
+        for h, d in pieces:
+            query_from(d, h).wait_recv()
+            query(d, h).wait_send()
         for h in (0, 1):
-            for d in range(4):
-                relayed(d, h).wait_recv()
-                onward(d, h).start()
-            if h:
-                start_ring(0)
-        ring.forward(0)
-        start_ring(1)
-        ring.forward(1)
-        for h in (0, 1):
-            q_exchange.arrive_all(h)
             ring.finish(h)
-            q_exchange.finish(h)
-            for d in range(4):
-                onward(d, h).wait_send()
-
-    line.finish()
-    stages[4]()
 
 
 def cross_project(source, target, q, kv, wo, mantissas, exponents, gains, weights, wc):
@@ -714,7 +723,7 @@
             jax.ShapeDtypeStruct((ROWS, 512), F32),
             jax.ShapeDtypeStruct((4, ROWS, 128), BF16),
             jax.ShapeDtypeStruct((4, 4, ROWS, 128), BF16),
-            jax.ShapeDtypeStruct((8, 16, 32, 256), BF16),
+            jax.ShapeDtypeStruct((4, 8, 32, 256), BF16),
         ),
         in_specs=[SMEM, SMEM, VMEM, VMEM, VMEM, VMEM, VMEM, VMEM, ANY, VMEM],
         out_specs=(VMEM, VMEM, VMEM, VMEM),
@@ -724,14 +733,14 @@
             pltpu.VMEM((4, ROWS, 128), BF16),
             pltpu.VMEM((8, ROWS, 256), BF16),
             pltpu.VMEM((8, ROWS, 512), BF16),
+            pltpu.VMEM((8, 16, 16, 512), BF16),
             pltpu.VMEM((2, 4096, 256), BF16),
             pltpu.VMEM((2, ROWS, 256), F32),
             pltpu.VMEM((4, ROWS, 128), BF16),
             pltpu.VMEM((4, ROWS, 128), BF16),
-            pltpu.VMEM((4, ROWS, 128), BF16),
             DMA,
             *dma((4, 4), (4, 4), (10, 2), (8, 2), (10, 2), (8, 2), (2, 4), (2, 4)),
-            *dma((2, 4), (2, 4), (2, 4), (2, 4), (2, 3, 4), (2, 3, 4), (4,), (4,), (3, 4), (3, 4)),
+            *dma((2, 4), (2, 4), (2, 3, 4), (2, 3, 4), (4,), (4,), (3, 4), (3, 4)),
         ],
         compiler_params=params(1),
         name="cross_project",
@@ -739,7 +748,8 @@
 
 
 def output_kernel(
-    q_ref, kv_ref, w_ref, rows_ref, out_ref, scores, mixed, heads, buf, back_send, back_recv, line_send, line_recv
+    q_ref, kv_ref, w_ref, rows_ref, out_ref,
+    scores, mixed, heads, buf, w, back_send, back_recv, line_send, line_recv, a_send, a_recv,
 ):
     at = Place()
     peers = at.line_devices() + at.a_devices()
@@ -754,6 +764,7 @@
     def _():
         back = Exchange(at, mixed, heads, back_send, back_recv, 4)
         line = Line(at, buf, line_send, line_recv)
+        spread = SecondSpread(at, w_ref, w, a_send, a_recv)
 
         def step(c):
             attention_step(at, c, q_ref, kv_ref, scores, mixed, None)
@@ -763,11 +774,14 @@
             total = rows_ref[rows]
             for j in range(8):
                 total += lax.dot_general(
-                    buf[j, rows], w_ref[j].reshape(512, 256), (((1,), (1,)), ((), ())), preferred_element_type=F32
+                    buf[j, rows],
+                    w[(j + 4) % 8].reshape(512, 256),
+                    (((1,), (1,)), ((), ())),
+                    preferred_element_type=F32,
                 )
             out_ref[rows] = total
 
-        attend_and_collect(at, peers, step, back, heads, line, product, lambda n: None)
+        attend_and_collect(at, peers, step, back, heads, line, spread, product, lambda n: None)
 
 
 def output(q, kv, weights, rows):
@@ -781,7 +795,8 @@
             pltpu.VMEM((4, ROWS, 128), BF16),
             pltpu.VMEM((4, ROWS, 128), BF16),
             pltpu.VMEM((8, ROWS, 256), BF16),
-            *dma((4, 4), (4, 4), (10, 2), (8, 2)),
+            pltpu.VMEM((8, 16, 32, 256), BF16),
+            *dma((4, 4), (4, 4), (10, 2), (8, 2), (3, 4), (3, 4)),
         ],
         compiler_params=params(2),
         name="output",

time: 152 us -> 149 us (0.980)
  local copies, waits for them, and re-layouts: 4.78 us -> 3.21 us
    pallas_call x1, Pallas kernels: 28.6 us -> 34.2 us  [output(): pl.pallas_call(output_kernel, out_shape=jax.ShapeDtypeStruct((ROWS, 512),...]
    pallas_call x1, Pallas kernels: 72.1 us -> 68.2 us  [cross_project(): pl.pallas_call(cross_kernel, out_shape=(jax.ShapeDtypeStruct((ROWS, 512),...]
    pallas_call x1, Pallas kernels: 45.8 us -> 42.7 us  [self_project(): pl.pallas_call(self_kernel, out_shape=(jax.ShapeDtypeStruct((4, ROWS, 128...]
    unnamed x13 -> x17, local copies, waits for them, and re-layouts: 4.78 us -> 3.21 us
where the time goes in v4:
time: 149 us; the launch traced here: 148 us
  Pallas kernels  145 us (97%)
  local copies, waits for them, and re-layouts  3.21 us (2%)
    pallas_call x1, Pallas kernels, cross_project(): pl.pallas_call(cross_kernel, out_shape=(jax.ShapeDtypeStruct((ROWS, 512),...  68.2 us
    pallas_call x1, Pallas kernels, self_project(): pl.pallas_call(self_kernel, out_shape=(jax.ShapeDtypeStruct((4, ROWS, 128...  42.7 us
    pallas_call x1, Pallas kernels, output(): pl.pallas_call(output_kernel, out_shape=jax.ShapeDtypeStruct((ROWS, 512),...  34.2 us
    unnamed x17, local copies, waits for them, and re-layouts  3.21 us

profile of v4, /device:TPU:129, one launch (start us, length us, event | category | flops | bytes accessed | tf_op | source)
XLA Modules:
  0.0 148.3 jit_solution(18331654408013471946)
XLA Ops:
  0.0 0.0 copy-start
  0.0 0.9 copy-done
  1.0 0.0 copy-start.2
  1.0 0.8 copy-done.2
  1.7 0.0 copy-start.4
  1.7 0.7 copy-done.4
  2.4 0.0 copy-start.1
  2.4 0.0 copy-start.3
  2.4 0.0 copy-start.5
  2.4 0.0 copy-start.6
  2.4 0.0 copy-start.7
  2.4 42.7 %self_project.1 = (bf16[4,256,128]{2,1,0:T(8,128)(2,1)S(1)}, bf16[4,4,256,128]{3,2,1,0:T(8,128)(2,1)}, bf16[4,8,16,512]{3,2,1,0:T(8,128)(2,1)S(1)}, bf16[8,32,256]{2,1,0:T(8,128)(2,1)S(1)}) custom-call(bf16[256,512]{1,0:T(8,128)(2,1)S(1)} %bitcast.10, s32[4,256]{1,0:T(4,128)S(1)} %bitcast.14, f32[2,4096]{1,0:T(2,128)S(1)} %bitcast.12, ...), custom_call_target="tpu_custom_call" | custom-call | tf_op jit(solution)/shard_map/self_project/pallas_call | solution.py:471
  45.1 0.0 copy-done.1
  45.1 0.0 copy-done.3
  45.1 0.0 copy-done.5
  45.1 0.0 copy-done.6
  45.1 0.0 copy-done.7
  45.1 68.2 %cross_project.1 = (f32[256,512]{1,0:T(8,128)S(1)}, bf16[4,256,128]{2,1,0:T(8,128)(2,1)S(1)}, bf16[4,4,256,128]{3,2,1,0:T(8,128)(2,1)S(1)}, bf16[4,8,32,256]{3,2,1,0:T(8,128)(2,1)S(1)}) custom-call(s32[3]{0:T(128)S(1)} %copy-done.6, s32[3]{0:T(128)S(1)} %copy-done.7, bf16[4,256,128]{2,1,0:T(8,128)(2,1)S(1)} %get-tuple-element.13.q_ref, ...), custom_call_target="tpu_custom_call" | custom-call | tf_op jit(solution)/shard_map/cross_project/pallas_call | solution.py:720
  113.4 34.2 %output.1 = f32[256,512]{1,0:T(8,128)S(1)} custom-call(bf16[4,256,128]{2,1,0:T(8,128)(2,1)S(1)} %get-tuple-element.17.q_ref, bf16[4,4,256,128]{3,2,1,0:T(8,128)(2,1)S(1)} %get-tuple-element.18.kv_ref, bf16[4,8,32,256]{3,2,1,0:T(8,128)(2,1)S(1)} %get-tuple-element.19.w_ref, f32[256,512]{1,0:T(8,128)S(1)} %get-tuple-element.20.rows_ref), custom_call_target="tpu_custom_call" | custom-call | tf_op jit(solution)/shard_map/output/pallas_call | solution.py:788
  147.5 0.8 copy.10
Async XLA Ops:
  0.0 0.9 copy-start
  1.0 0.8 copy-start.2
  1.7 0.7 copy-start.4
  2.4 42.7 %copy-start.1 = (bf16[1,256,512]{2,1,0:T(8,128)(2,1)S(1)}, bf16[1,256,512]{2,1,0:T(8,128)(2,1)}, u32[]{:S(2)}) copy-start(bf16[1,256,512]{2,1,0:T(8,128)(2,1)} %param.8) | copy-start | bytes 786436
  2.4 42.7 %copy-start.3 = (f32[1,2,4096]{2,1,0:T(2,128)S(1)}, f32[1,2,4096]{2,1,0:T(2,128)}, u32[]{:S(2)}) copy-start(f32[1,2,4096]{2,1,0:T(2,128)} %param.12) | copy-start | bytes 98308
  2.4 42.7 %copy-start.5 = (s32[1,256,4]{1,2,0:T(4,128)S(1)}, s32[1,256,4]{1,2,0:T(4,128)}, u32[]{:S(2)}) copy-start(s32[1,256,4]{1,2,0:T(4,128)} %param.9) | copy-start | bytes 12292
  2.4 42.7 %copy-start.6 = (s32[3]{0:T(128)S(1)}, s32[3]{0:T(128)}, u32[]{:S(2)}) copy-start(s32[3]{0:T(128)} %source_ref.1) | copy-start | bytes 40
  2.4 42.7 %copy-start.7 = (s32[3]{0:T(128)S(1)}, s32[3]{0:T(128)}, u32[]{:S(2)}) copy-start(s32[3]{0:T(128)} %target_ref.1) | copy-start | bytes 40

commit v5 on v4

--- a/solution.py
+++ b/solution.py
@@ -14,7 +14,7 @@
 ROWS = 256
 BLOCKS = 16
 QSCALE = math.log2(math.e) / 8.0
-VMEM_LIMITS = (52 << 20, 50 << 20, 48 << 20)
+VMEM_LIMITS = (52 << 20, 48 << 20, 48 << 20)
 
 
 def remote(src, dst, send, recv, device):
@@ -72,6 +72,8 @@
         return [
             (self.line(1), self.p < 3),
             (self.line(-1), self.p > 0),
+            (self.line(2), self.p < 2),
+            (self.line(-2), self.p > 1),
             (self.sibling(), None),
         ]
 
@@ -96,76 +98,61 @@
     def __init__(self, at, buf, send, recv):
         self.at, self.buf, self.send, self.recv = at, buf, send, recv
 
-    def copy(self, block, h, slot, device):
-        ref = self.buf.at[block, half(h)]
-        return remote(ref, ref, self.send.at[slot, h], self.recv.at[block, h], device)
-
-    def up(self, t, h):
-        return self.copy((self.at.p - t) * 2 + self.at.c, h, t, self.at.line(1))
-
-    def down(self, t, h):
-        return self.copy((self.at.p + t) * 2 + self.at.c, h, 3 + t, self.at.line(-1))
+    def copy(self, p, h, slot, device):
+        ref = self.buf.at[p * 2 + self.at.c, half(h)]
+        return remote(ref, ref, self.send.at[slot, h], self.recv.at[p * 2 + self.at.c, h], device)
+
+    def sends(self, h):
+        at = self.at
+        own = [
+            (at.p < 3, self.copy(at.p, h, 0, at.line(1))),
+            (at.p > 0, self.copy(at.p, h, 1, at.line(-1))),
+            (at.p < 2, self.copy(at.p, h, 2, at.line(2))),
+            (at.p > 1, self.copy(at.p, h, 3, at.line(-2))),
+        ]
+        onward = [
+            (at.p == 2, self.copy(0, h, 4, at.line(1))),
+            (at.p == 1, self.copy(3, h, 5, at.line(-1))),
+        ]
+        return own, onward
 
     def across(self, p, h):
-        return self.copy(p * 2 + self.at.c, h, 6 + p, self.at.sibling())
+        return self.copy(p, h, 6 + p, self.at.sibling())
 
     def begin(self, h):
-        at = self.at
-
-        @pl.when(at.p < 3)
-        def _():
-            self.up(0, h).start()
-
-        @pl.when(at.p > 0)
-        def _():
-            self.down(0, h).start()
-
-        self.across(at.p, h).start()
+        for guard, copy in self.sends(h)[0]:
+            pl.when(guard)(copy.start)
+        self.across(self.at.p, h).start()
 
     def step(self, t, h):
         at = self.at
+        up, down = self.sends(h)[1]
 
         @pl.when(at.p >= t)
         def _():
-            self.up(t, h).wait_recv()
-
-            if t < 3:
-
-                @pl.when(at.p < 3)
-                def _():
-                    self.up(t, h).start()
-
+            self.copy(at.p - t, h, 0, at.line(1)).wait_recv()
+            if t == 2:
+                pl.when(up[0])(up[1].start)
             self.across(at.p - t, h).start()
 
         @pl.when(at.p <= 3 - t)
         def _():
-            self.down(t, h).wait_recv()
-
-            if t < 3:
-
-                @pl.when(at.p > 0)
-                def _():
-                    self.down(t, h).start()
-
+            self.copy(at.p + t, h, 0, at.line(-1)).wait_recv()
+            if t == 2:
+                pl.when(down[0])(down[1].start)
             self.across(at.p + t, h).start()
 
     def siblings(self, h):
         for p in range(4):
-            self.copy(p * 2 + 1 - self.at.c, h, 6 + p, self.at.sibling()).wait_recv()
+            ref = self.buf.at[p * 2 + 1 - self.at.c, half(h)]
+            recv = self.recv.at[p * 2 + 1 - self.at.c, h]
+            remote(ref, ref, self.send.at[6 + p, h], recv, self.at.sibling()).wait_recv()
 
     def finish(self):
-        at = self.at
         for h in (0, 1):
-            for t in range(3):
-
-                @pl.when((at.p >= t) & (at.p < 3))
-                def _():
-                    self.up(t, h).wait_send()
-
-                @pl.when((at.p <= 3 - t) & (at.p > 0))
-                def _():
-                    self.down(t, h).wait_send()
-
+            own, onward = self.sends(h)
+            for guard, copy in own + onward:
+                pl.when(guard)(copy.wait_send)
             for p in range(4):
                 self.across(p, h).wait_send()
 
@@ -349,9 +336,9 @@
 
 def self_kernel(
     mantissa_ref, exponent_ref, gain_ref, w_ref, wo_ref, wc_ref, q_out, kv_out, wo_out, wc_out,
-    buf, w_vmem, acc, q4, kv4, load_sem, own_sem,
+    buf, w_vmem, acc, q4, kv4, wo_part, load_sem, own_sem,
     line_send, line_recv, kv_send, kv_recv, q_send, q_recv, ring_send, ring_recv,
-    wo_send, wo_recv, wc_send, wc_recv, g_send, g_recv,
+    wo_send, wo_recv, wc_send, wc_recv, g_send, g_recv, a_send, a_recv,
 ):
     at = Place()
     peers = at.mp_devices() + at.a_devices() + at.g_devices()
@@ -365,7 +352,7 @@
     def wc_piece(j):
         return wc_ref.at[1, pl.ds(pl.multiple_of(j * 512 + at.seq * 32, 32), 32)]
 
-    own_wo = pltpu.make_async_copy(wo_piece(at.mp), wo_out.at[at.g, at.mp], own_sem.at[0])
+    own_wo = pltpu.make_async_copy(wo_piece(at.mp), wo_part.at[at.g, at.mp], own_sem.at[0])
     own_wo.start()
     own_wc = pltpu.make_async_copy(wc_piece(at.mp), wc_out.at[at.mp], own_sem.at[1])
     own_wc.start()
@@ -373,10 +360,10 @@
     def wo_copy(d):
         to = (at.mp + d) % 8
         slot = jnp.where(to % 2 == at.c, at.g, at.a)
-        return remote(wo_piece(to), wo_out.at[slot, at.mp], wo_send.at[d], wo_recv.at[d], {"mp": to})
+        return remote(wo_piece(to), wo_part.at[slot, at.mp], wo_send.at[d], wo_recv.at[d], {"mp": to})
 
     def wo_from(d):
-        ref = wo_out.at[at.g, (at.mp + 8 - d) % 8]
+        ref = wo_part.at[at.g, (at.mp + 8 - d) % 8]
         return remote(ref, ref, wo_send.at[d], wo_recv.at[d], {"mp": (at.mp + d) % 8})
 
     def wc_copy(d):
@@ -391,7 +378,8 @@
     kv_exchange = Exchange(at, kv4, kv_out.at[at.g], kv_send, kv_recv, 2)
     q_exchange = Exchange(at, q4, q_out, q_send, q_recv, 2)
     ring = Ring(at, kv_out, ring_send, ring_recv)
-    spread = FirstSpread(at, wo_out, g_send, g_recv)
+    spread = FirstSpread(at, wo_part, g_send, g_recv)
+    second = SecondSpread(at, wo_part, wo_out, a_send, a_recv)
 
     def heads(h):
         scale = project(h, buf, gain_ref, 0, w_vmem, acc, 3)
@@ -420,13 +408,16 @@
         wo_from(d).wait_recv()
     spread.start()
     line.step(2, 0)
+    spread.forward()
     line.step(1, 1)
-    spread.forward()
+    spread.finish()
+    second.start()
     line.step(3, 0)
     load.wait()
     line.siblings(0)
     heads(0)
     line.step(2, 1)
+    second.forward()
     start_ring(0)
     line.step(3, 1)
     line.siblings(1)
@@ -442,7 +433,7 @@
         q_exchange.finish(h)
         kv_exchange.finish(h)
     line.finish()
-    spread.finish()
+    second.finish()
     own_wc.wait()
     for d in range(1, 8):
         wc_from(d).wait_recv()
@@ -473,7 +464,7 @@
         out_shape=(
             jax.ShapeDtypeStruct((4, ROWS, 128), BF16),
             jax.ShapeDtypeStruct((4, 4, ROWS, 128), BF16),
-            jax.ShapeDtypeStruct((4, 8, 16, 512), BF16),
+            jax.ShapeDtypeStruct((8, 16, 16, 512), BF16),
             jax.ShapeDtypeStruct((8, 32, 256), BF16),
         ),
         in_specs=[VMEM, VMEM, VMEM, ANY, ANY, ANY],
@@ -484,9 +475,10 @@
             pltpu.VMEM((3, ROWS, 256), F32),
             pltpu.VMEM((4, ROWS, 128), BF16),
             pltpu.VMEM((4, ROWS, 128), BF16),
+            pltpu.VMEM((4, 8, 16, 512), BF16),
             DMA,
             *dma((2,), (10, 2), (8, 2), (2, 4), (2, 4), (2, 4), (2, 4), (2, 3, 4), (2, 3, 4)),
-            *dma((8,), (8,), (8,), (8,), (4,), (4,)),
+            *dma((8,), (8,), (8,), (8,), (4,), (4,), (3, 4), (3, 4)),
         ],
         compiler_params=params(0),
         name="self_project",
@@ -533,10 +525,9 @@
     mixed[:, rows, :] = result.reshape(4, STEP, 128)
 
 
-def attend_and_collect(at, peers, step, back, heads, line, spread, product, after):
+def attend_and_collect(at, peers, step, back, heads, line, product, after):
     def collect(h):
-        back.arrive_all(2 * h)
-        back.arrive_all(2 * h + 1)
+        back.arrive_all(h)
         low = lax.broadcasted_iota(jnp.int32, (HALF, 128), 1) < 64
         rows = half(h)
         for pair in (0, 1):
@@ -547,41 +538,36 @@
 
     step(0)
     wait_all(peers)
+    step(1)
     back.start(0)
-    spread.start()
-    step(1)
-    back.start(1)
     step(2)
-    back.start(2)
     collect(0)
     step(3)
-    back.start(3)
+    back.start(1)
     line.step(1, 0)
+    line.step(2, 0)
     collect(1)
-    spread.forward()
     after(0)
-    line.step(2, 0)
+    line.step(3, 0)
     line.step(1, 1)
     after(1)
-    line.step(3, 0)
+    line.siblings(0)
+    product(0)
     line.step(2, 1)
-    line.siblings(0)
-    spread.finish()
-    product(0)
     after(2)
     line.step(3, 1)
-    after(3)
     line.siblings(1)
     product(1)
-    for c in range(4):
-        back.finish(c)
+    after(3)
+    for h in (0, 1):
+        back.finish(h)
     line.finish()
 
 
 def cross_kernel(
     source_ref, target_ref, q_ref, kv_ref, wo_ref, mantissa_ref, exponent_ref, gain_ref, w_ref, wc_ref,
     rows_out, q_out, kv_out, wc_out,
-    scores, mixed, heads, mixed_buf, buf, wo, w_vmem, acc, q4, kv4, load_sem,
+    scores, mixed, heads, mixed_buf, buf, wc_part, w_vmem, acc, q4, kv4, load_sem,
     back_send, back_recv, mix_send, mix_recv, line_send, line_recv, q_send, q_recv,
     over_send, over_recv, ring_send, ring_recv, g_send, g_recv, a_send, a_recv,
 ):
@@ -608,11 +594,11 @@
     lengths = [jnp.where(decoder, target_ref[i], source_ref[i]) for i in (0, 1)]
     for i, part in enumerate(decoded(mantissa_ref, exponent_ref)):
         rows_out[:, 128 * i : 128 * i + 128] = part
-    back = Exchange(at, mixed, heads, back_send, back_recv, 4)
+    back = Exchange(at, mixed, heads, back_send, back_recv, 2)
     mix_line = Line(at, mixed_buf, mix_send, mix_recv)
     line = Line(at, buf, line_send, line_recv)
-    spread = SecondSpread(at, wo_ref, wo, a_send, a_recv)
-    wc_spread = FirstSpread(at, wc_out, g_send, g_recv)
+    first = FirstSpread(at, wc_part, g_send, g_recv)
+    second = SecondSpread(at, wc_part, wc_out, a_send, a_recv)
 
     def step(c):
         attention_step(at, c, q_ref, kv_ref, scores, mixed, lengths)
@@ -621,28 +607,31 @@
         rows = half(h)
         total = rows_out[rows]
         for j in range(8):
-            total += jnp.dot(mixed_buf[j, rows], wo[j].reshape(256, 512), preferred_element_type=F32)
+            total += jnp.dot(mixed_buf[j, rows], wo_ref[j].reshape(256, 512), preferred_element_type=F32)
         rows_out[rows] = total
         buf[at.mp, rows] = total.astype(BF16)
         line.begin(h)
 
     def after(n):
-        if n == 3:
+        @pl.when(decoder)
+        def _():
+            if n == 0:
+                wc_part[at.g] = wc_ref[...]
+                first.start()
+            elif n == 1:
+                first.forward()
+            elif n == 3:
+                first.finish()
+                second.start()
+
+        if n == 2:
             line.step(1, 0)
 
     @pl.when(encoder)
     def _():
         wc_out[...] = jnp.zeros_like(wc_out)
 
-    @pl.when(decoder)
-    def _():
-        wc_out[at.g] = wc_ref[...]
-
-    attend_and_collect(at, peers, step, back, heads, mix_line, spread, product, after)
-    @pl.when(decoder)
-    def _():
-        wc_spread.start()
-
+    attend_and_collect(at, peers, step, back, heads, mix_line, product, after)
     line.step(2, 0)
     line.step(1, 1)
     line.step(3, 0)
@@ -702,13 +691,13 @@
 
     @pl.when(decoder)
     def _():
-        wc_spread.forward()
+        second.forward()
         for h in (0, 1):
             for d in range(4):
                 over_from(d, h).wait_recv()
                 ring.start(d, h)
             ring.forward(h)
-        wc_spread.finish()
+        second.finish()
         for h, d in pieces:
             query_from(d, h).wait_recv()
             query(d, h).wait_send()
@@ -723,7 +712,7 @@
             jax.ShapeDtypeStruct((ROWS, 512), F32),
             jax.ShapeDtypeStruct((4, ROWS, 128), BF16),
             jax.ShapeDtypeStruct((4, 4, ROWS, 128), BF16),
-            jax.ShapeDtypeStruct((4, 8, 32, 256), BF16),
+            jax.ShapeDtypeStruct((8, 16, 32, 256), BF16),
         ),
         in_specs=[SMEM, SMEM, VMEM, VMEM, VMEM, VMEM, VMEM, VMEM, ANY, VMEM],
         out_specs=(VMEM, VMEM, VMEM, VMEM),
@@ -733,13 +722,13 @@
             pltpu.VMEM((4, ROWS, 128), BF16),
             pltpu.VMEM((8, ROWS, 256), BF16),
             pltpu.VMEM((8, ROWS, 512), BF16),
-            pltpu.VMEM((8, 16, 16, 512), BF16),
+            pltpu.VMEM((4, 8, 32, 256), BF16),
             pltpu.VMEM((2, 4096, 256), BF16),
             pltpu.VMEM((2, ROWS, 256), F32),
             pltpu.VMEM((4, ROWS, 128), BF16),
             pltpu.VMEM((4, ROWS, 128), BF16),
             DMA,
-            *dma((4, 4), (4, 4), (10, 2), (8, 2), (10, 2), (8, 2), (2, 4), (2, 4)),
+            *dma((2, 4), (2, 4), (10, 2), (8, 2), (10, 2), (8, 2), (2, 4), (2, 4)),
             *dma((2, 4), (2, 4), (2, 3, 4), (2, 3, 4), (4,), (4,), (3, 4), (3, 4)),
         ],
         compiler_params=params(1),
@@ -749,7 +738,7 @@
 
 def output_kernel(
     q_ref, kv_ref, w_ref, rows_ref, out_ref,
-    scores, mixed, heads, buf, w, back_send, back_recv, line_send, line_recv, a_send, a_recv,
+    scores, mixed, heads, buf, back_send, back_recv, line_send, line_recv,
 ):
     at = Place()
     peers = at.line_devices() + at.a_devices()
@@ -762,9 +751,8 @@
 
     @pl.when(at.sec == 1)
     def _():
-        back = Exchange(at, mixed, heads, back_send, back_recv, 4)
+        back = Exchange(at, mixed, heads, back_send, back_recv, 2)
         line = Line(at, buf, line_send, line_recv)
-        spread = SecondSpread(at, w_ref, w, a_send, a_recv)
 
         def step(c):
             attention_step(at, c, q_ref, kv_ref, scores, mixed, None)
@@ -775,13 +763,13 @@
             for j in range(8):
                 total += lax.dot_general(
                     buf[j, rows],
-                    w[(j + 4) % 8].reshape(512, 256),
+                    w_ref[(j + 4) % 8].reshape(512, 256),
                     (((1,), (1,)), ((), ())),
                     preferred_element_type=F32,
                 )
             out_ref[rows] = total
 
-        attend_and_collect(at, peers, step, back, heads, line, spread, product, lambda n: None)
+        attend_and_collect(at, peers, step, back, heads, line, product, lambda n: None)
 
 
 def output(q, kv, weights, rows):
@@ -795,8 +783,7 @@
             pltpu.VMEM((4, ROWS, 128), BF16),
             pltpu.VMEM((4, ROWS, 128), BF16),
             pltpu.VMEM((8, ROWS, 256), BF16),
-            pltpu.VMEM((8, 16, 32, 256), BF16),
-            *dma((4, 4), (4, 4), (10, 2), (8, 2), (3, 4), (3, 4)),
+            *dma((2, 4), (2, 4), (10, 2), (8, 2)),
         ],
         compiler_params=params(2),
         name="output",

time: 149 us -> 152 us (1.020)
  Pallas kernels: 145 us -> 148 us
    pallas_call x1, Pallas kernels: 42.7 us -> 54.7 us  [self_project(): pl.pallas_call(self_kernel, out_shape=(jax.ShapeDtypeStruct((4, ROWS, 128...]
    pallas_call x1, Pallas kernels: 68.2 us -> 62.7 us  [cross_project(): pl.pallas_call(cross_kernel, out_shape=(jax.ShapeDtypeStruct((ROWS, 512),...]
    pallas_call x1, Pallas kernels: 34.2 us -> 30.8 us  [output(): pl.pallas_call(output_kernel, out_shape=jax.ShapeDtypeStruct((ROWS, 512),...]
    unnamed x17 -> x15, local copies, waits for them, and re-layouts: 3.21 us -> 3.2 us
where the time goes in v5:
time: 152 us
  Pallas kernels  148 us (97%)
  local copies, waits for them, and re-layouts  3.2 us (2%)
    pallas_call x1, Pallas kernels, cross_project(): pl.pallas_call(cross_kernel, out_shape=(jax.ShapeDtypeStruct((ROWS, 512),...  62.7 us
    pallas_call x1, Pallas kernels, self_project(): pl.pallas_call(self_kernel, out_shape=(jax.ShapeDtypeStruct((4, ROWS, 128...  54.7 us
    pallas_call x1, Pallas kernels, output(): pl.pallas_call(output_kernel, out_shape=jax.ShapeDtypeStruct((ROWS, 512),...  30.8 us
    unnamed x15, local copies, waits for them, and re-layouts  3.2 us

profile of v5, /device:TPU:129, one launch (start us, length us, event | category | flops | bytes accessed | tf_op | source)
XLA Modules:
  0.0 151.5 jit_solution(14317113872292844659)
XLA Ops:
  0.0 0.0 copy-start
  0.0 0.9 copy-done
  1.0 0.0 copy-start.1
  1.0 0.8 copy-done.1
  1.7 0.0 copy-start.3
  1.7 0.7 copy-done.3
  2.4 0.0 copy-start.2
  2.4 0.0 copy-start.4
  2.4 0.0 copy-start.5
  2.4 0.0 copy-start.6
  2.4 54.7 %self_project.1 = (bf16[4,256,128]{2,1,0:T(8,128)(2,1)S(1)}, bf16[4,4,256,128]{3,2,1,0:T(8,128)(2,1)S(1)}, bf16[8,16,16,512]{3,2,1,0:T(8,128)(2,1)}, bf16[8,32,256]{2,1,0:T(8,128)(2,1)S(1)}) custom-call(bf16[256,512]{1,0:T(8,128)(2,1)S(1)} %bitcast.10, s32[4,256]{1,0:T(4,128)S(1)} %bitcast.14, f32[2,4096]{1,0:T(2,128)S(1)} %bitcast.12, ...), custom_call_target="tpu_custom_call" | custom-call | tf_op jit(solution)/shard_map/self_project/pallas_call | solution.py:462
  57.1 0.0 copy-done.2
  57.1 0.0 copy-done.4
  57.1 0.0 copy-done.5
  57.1 0.0 copy-done.6
  57.1 62.7 %cross_project.1 = (f32[256,512]{1,0:T(8,128)S(1)}, bf16[4,256,128]{2,1,0:T(8,128)(2,1)S(1)}, bf16[4,4,256,128]{3,2,1,0:T(8,128)(2,1)S(1)}, bf16[8,16,32,256]{3,2,1,0:T(8,128)(2,1)S(1)}) custom-call(s32[3]{0:T(128)S(1)} %copy-done.5, s32[3]{0:T(128)S(1)} %copy-done.6, bf16[4,256,128]{2,1,0:T(8,128)(2,1)S(1)} %get-tuple-element.13.q_ref, ...), custom_call_target="tpu_custom_call" | custom-call | tf_op jit(solution)/shard_map/cross_project/pallas_call | solution.py:709
  119.9 30.8 %output.1 = f32[256,512]{1,0:T(8,128)S(1)} custom-call(bf16[4,256,128]{2,1,0:T(8,128)(2,1)S(1)} %get-tuple-element.17.q_ref, bf16[4,4,256,128]{3,2,1,0:T(8,128)(2,1)S(1)} %get-tuple-element.18.kv_ref, bf16[8,16,32,256]{3,2,1,0:T(8,128)(2,1)S(1)} %get-tuple-element.19.w_ref, f32[256,512]{1,0:T(8,128)S(1)} %get-tuple-element.20.rows_ref), custom_call_target="tpu_custom_call" | custom-call | tf_op jit(solution)/shard_map/output/pallas_call | solution.py:776
  150.7 0.8 copy.10
Async XLA Ops:
  0.0 0.9 copy-start
  1.0 0.8 copy-start.1
  1.7 0.7 copy-start.3
  2.4 54.7 %copy-start.2 = (f32[1,2,4096]{2,1,0:T(2,128)S(1)}, f32[1,2,4096]{2,1,0:T(2,128)}, u32[]{:S(2)}) copy-start(f32[1,2,4096]{2,1,0:T(2,128)} %param.12) | copy-start | bytes 98308
  2.4 54.7 %copy-start.4 = (s32[1,256,4]{1,2,0:T(4,128)S(1)}, s32[1,256,4]{1,2,0:T(4,128)}, u32[]{:S(2)}) copy-start(s32[1,256,4]{1,2,0:T(4,128)} %param.9) | copy-start | bytes 12292
  2.4 54.7 %copy-start.5 = (s32[3]{0:T(128)S(1)}, s32[3]{0:T(128)}, u32[]{:S(2)}) copy-start(s32[3]{0:T(128)} %source_ref.1) | copy-start | bytes 40
  2.4 54.7 %copy-start.6 = (s32[3]{0:T(128)S(1)}, s32[3]{0:T(128)}, u32[]{:S(2)}) copy-start(s32[3]{0:T(128)} %target_ref.1) | copy-start | bytes 40

commit v6 on v5

--- a/solution.py
+++ b/solution.py
@@ -14,7 +14,7 @@
 ROWS = 256
 BLOCKS = 16
 QSCALE = math.log2(math.e) / 8.0
-VMEM_LIMITS = (52 << 20, 48 << 20, 48 << 20)
+VMEM_LIMITS = (50 << 20, 48 << 20, 48 << 20)
 
 
 def remote(src, dst, send, recv, device):
@@ -336,9 +336,9 @@
 
 def self_kernel(
     mantissa_ref, exponent_ref, gain_ref, w_ref, wo_ref, wc_ref, q_out, kv_out, wo_out, wc_out,
-    buf, w_vmem, acc, q4, kv4, wo_part, load_sem, own_sem,
+    buf, w_vmem, acc, q4, kv4, load_sem, own_sem,
     line_send, line_recv, kv_send, kv_recv, q_send, q_recv, ring_send, ring_recv,
-    wo_send, wo_recv, wc_send, wc_recv, g_send, g_recv, a_send, a_recv,
+    wo_send, wo_recv, wc_send, wc_recv, g_send, g_recv,
 ):
     at = Place()
     peers = at.mp_devices() + at.a_devices() + at.g_devices()
@@ -352,7 +352,7 @@
     def wc_piece(j):
         return wc_ref.at[1, pl.ds(pl.multiple_of(j * 512 + at.seq * 32, 32), 32)]
 
-    own_wo = pltpu.make_async_copy(wo_piece(at.mp), wo_part.at[at.g, at.mp], own_sem.at[0])
+    own_wo = pltpu.make_async_copy(wo_piece(at.mp), wo_out.at[at.g, at.mp], own_sem.at[0])
     own_wo.start()
     own_wc = pltpu.make_async_copy(wc_piece(at.mp), wc_out.at[at.mp], own_sem.at[1])
     own_wc.start()
@@ -360,10 +360,10 @@
     def wo_copy(d):
         to = (at.mp + d) % 8
         slot = jnp.where(to % 2 == at.c, at.g, at.a)
-        return remote(wo_piece(to), wo_part.at[slot, at.mp], wo_send.at[d], wo_recv.at[d], {"mp": to})
+        return remote(wo_piece(to), wo_out.at[slot, at.mp], wo_send.at[d], wo_recv.at[d], {"mp": to})
 
     def wo_from(d):
-        ref = wo_part.at[at.g, (at.mp + 8 - d) % 8]
+        ref = wo_out.at[at.g, (at.mp + 8 - d) % 8]
         return remote(ref, ref, wo_send.at[d], wo_recv.at[d], {"mp": (at.mp + d) % 8})
 
     def wc_copy(d):
@@ -378,8 +378,7 @@
     kv_exchange = Exchange(at, kv4, kv_out.at[at.g], kv_send, kv_recv, 2)
     q_exchange = Exchange(at, q4, q_out, q_send, q_recv, 2)
     ring = Ring(at, kv_out, ring_send, ring_recv)
-    spread = FirstSpread(at, wo_part, g_send, g_recv)
-    second = SecondSpread(at, wo_part, wo_out, a_send, a_recv)
+    spread = FirstSpread(at, wo_out, g_send, g_recv)
 
     def heads(h):
         scale = project(h, buf, gain_ref, 0, w_vmem, acc, 3)
@@ -410,14 +409,11 @@
     line.step(2, 0)
     spread.forward()
     line.step(1, 1)
-    spread.finish()
-    second.start()
     line.step(3, 0)
     load.wait()
     line.siblings(0)
     heads(0)
     line.step(2, 1)
-    second.forward()
     start_ring(0)
     line.step(3, 1)
     line.siblings(1)
@@ -433,7 +429,7 @@
         q_exchange.finish(h)
         kv_exchange.finish(h)
     line.finish()
-    second.finish()
+    spread.finish()
     own_wc.wait()
     for d in range(1, 8):
         wc_from(d).wait_recv()
@@ -464,7 +460,7 @@
         out_shape=(
             jax.ShapeDtypeStruct((4, ROWS, 128), BF16),
             jax.ShapeDtypeStruct((4, 4, ROWS, 128), BF16),
-            jax.ShapeDtypeStruct((8, 16, 16, 512), BF16),
+            jax.ShapeDtypeStruct((4, 8, 16, 512), BF16),
             jax.ShapeDtypeStruct((8, 32, 256), BF16),
         ),
         in_specs=[VMEM, VMEM, VMEM, ANY, ANY, ANY],
@@ -475,10 +471,9 @@
             pltpu.VMEM((3, ROWS, 256), F32),
             pltpu.VMEM((4, ROWS, 128), BF16),
             pltpu.VMEM((4, ROWS, 128), BF16),
-            pltpu.VMEM((4, 8, 16, 512), BF16),
             DMA,
             *dma((2,), (10, 2), (8, 2), (2, 4), (2, 4), (2, 4), (2, 4), (2, 3, 4), (2, 3, 4)),
-            *dma((8,), (8,), (8,), (8,), (4,), (4,), (3, 4), (3, 4)),
+            *dma((8,), (8,), (8,), (8,), (4,), (4,)),
         ],
         compiler_params=params(0),
         name="self_project",
@@ -544,17 +539,17 @@
     collect(0)
     step(3)
     back.start(1)
+    after(0)
     line.step(1, 0)
     line.step(2, 0)
     collect(1)
-    after(0)
     line.step(3, 0)
+    after(1)
     line.step(1, 1)
-    after(1)
     line.siblings(0)
-    product(0)
     line.step(2, 1)
     after(2)
+    product(0)
     line.step(3, 1)
     line.siblings(1)
     product(1)
@@ -567,9 +562,9 @@
 def cross_kernel(
     source_ref, target_ref, q_ref, kv_ref, wo_ref, mantissa_ref, exponent_ref, gain_ref, w_ref, wc_ref,
     rows_out, q_out, kv_out, wc_out,
-    scores, mixed, heads, mixed_buf, buf, wc_part, w_vmem, acc, q4, kv4, load_sem,
+    scores, mixed, heads, mixed_buf, buf, wo, wc_part, w_vmem, acc, q4, kv4, load_sem,
     back_send, back_recv, mix_send, mix_recv, line_send, line_recv, q_send, q_recv,
-    over_send, over_recv, ring_send, ring_recv, g_send, g_recv, a_send, a_recv,
+    over_send, over_recv, ring_send, ring_recv, g_send, g_recv, a_send, a_recv, wo_send, wo_recv,
 ):
     at = Place()
     encoder, decoder = at.sec == 0, at.sec == 1
@@ -597,6 +592,7 @@
     back = Exchange(at, mixed, heads, back_send, back_recv, 2)
     mix_line = Line(at, mixed_buf, mix_send, mix_recv)
     line = Line(at, buf, line_send, line_recv)
+    spread = SecondSpread(at, wo_ref, wo, wo_send, wo_recv)
     first = FirstSpread(at, wc_part, g_send, g_recv)
     second = SecondSpread(at, wc_part, wc_out, a_send, a_recv)
 
@@ -607,37 +603,42 @@
         rows = half(h)
         total = rows_out[rows]
         for j in range(8):
-            total += jnp.dot(mixed_buf[j, rows], wo_ref[j].reshape(256, 512), preferred_element_type=F32)
+            total += jnp.dot(mixed_buf[j, rows], wo[j].reshape(256, 512), preferred_element_type=F32)
         rows_out[rows] = total
         buf[at.mp, rows] = total.astype(BF16)
         line.begin(h)
 
     def after(n):
-        @pl.when(decoder)
-        def _():
-            if n == 0:
-                wc_part[at.g] = wc_ref[...]
-                first.start()
-            elif n == 1:
-                first.forward()
-            elif n == 3:
+        if n == 0:
+            spread.start()
+        elif n == 1:
+            spread.forward()
+            pl.when(decoder)(first.start)
+        elif n == 2:
+            spread.finish()
+            pl.when(decoder)(first.forward)
+        else:
+            line.step(1, 0)
+
+            @pl.when(decoder)
+            def _():
                 first.finish()
                 second.start()
-
-        if n == 2:
-            line.step(1, 0)
 
     @pl.when(encoder)
     def _():
         wc_out[...] = jnp.zeros_like(wc_out)
 
+    wc_part[at.g] = wc_ref[...]
     attend_and_collect(at, peers, step, back, heads, mix_line, product, after)
     line.step(2, 0)
     line.step(1, 1)
+
     line.step(3, 0)
     line.step(2, 1)
     load.wait()
     line.siblings(0)
+    pl.when(decoder)(second.forward)
 
     def over(d, h):
         rows = half(h)
@@ -691,7 +692,6 @@
 
     @pl.when(decoder)
     def _():
-        second.forward()
         for h in (0, 1):
             for d in range(4):
                 over_from(d, h).wait_recv()
@@ -722,6 +722,7 @@
             pltpu.VMEM((4, ROWS, 128), BF16),
             pltpu.VMEM((8, ROWS, 256), BF16),
             pltpu.VMEM((8, ROWS, 512), BF16),
+            pltpu.VMEM((8, 16, 16, 512), BF16),
             pltpu.VMEM((4, 8, 32, 256), BF16),
             pltpu.VMEM((2, 4096, 256), BF16),
             pltpu.VMEM((2, ROWS, 256), F32),
@@ -729,7 +730,7 @@
             pltpu.VMEM((4, ROWS, 128), BF16),
             DMA,
             *dma((2, 4), (2, 4), (10, 2), (8, 2), (10, 2), (8, 2), (2, 4), (2, 4)),
-            *dma((2, 4), (2, 4), (2, 3, 4), (2, 3, 4), (4,), (4,), (3, 4), (3, 4)),
+            *dma((2, 4), (2, 4), (2, 3, 4), (2, 3, 4), (4,), (4,), (3, 4), (3, 4), (3, 4), (3, 4)),
         ],
         compiler_params=params(1),
         name="cross_project",

time: 152 us -> 147 us (0.967)
  Pallas kernels: 148 us -> 144 us
    pallas_call x1, Pallas kernels: 54.7 us -> 48.7 us  [self_project(): pl.pallas_call(self_kernel, out_shape=(jax.ShapeDtypeStruct((4, ROWS, 128...]
    pallas_call x1, Pallas kernels: 62.7 us -> 65 us  [cross_project(): pl.pallas_call(cross_kernel, out_shape=(jax.ShapeDtypeStruct((ROWS, 512),...]
    unnamed x15 -> x13, local copies, waits for them, and re-layouts: 3.2 us -> 3.2 us
where the time goes in v6:
time: 147 us
  Pallas kernels  144 us (98%)
  local copies, waits for them, and re-layouts  3.2 us (2%)
    pallas_call x1, Pallas kernels, cross_project(): pl.pallas_call(cross_kernel, out_shape=(jax.ShapeDtypeStruct((ROWS, 512),...  65 us
    pallas_call x1, Pallas kernels, self_project(): pl.pallas_call(self_kernel, out_shape=(jax.ShapeDtypeStruct((4, ROWS, 128...  48.7 us
    pallas_call x1, Pallas kernels, output(): pl.pallas_call(output_kernel, out_shape=jax.ShapeDtypeStruct((ROWS, 512),...  29.8 us
    unnamed x13, local copies, waits for them, and re-layouts  3.2 us

profile of v6, /device:TPU:129, one launch (start us, length us, event | category | flops | bytes accessed | tf_op | source)
XLA Modules:
  0.0 146.8 jit_solution(9990027688233622793)
XLA Ops:
  0.0 0.0 copy-start
  0.0 0.9 copy-done
  1.0 0.0 copy-start.2
  1.0 0.8 copy-done.2
  1.7 0.0 copy-start.3
  1.7 0.7 copy-done.3
  2.4 0.0 copy-start.1
  2.4 0.0 copy-start.4
  2.4 0.0 copy-start.5
  2.4 48.7 %self_project.1 = (bf16[4,256,128]{2,1,0:T(8,128)(2,1)S(1)}, bf16[4,4,256,128]{3,2,1,0:T(8,128)(2,1)S(1)}, bf16[4,8,16,512]{3,2,1,0:T(8,128)(2,1)S(1)}, bf16[8,32,256]{2,1,0:T(8,128)(2,1)S(1)}) custom-call(bf16[256,512]{1,0:T(8,128)(2,1)S(1)} %bitcast.10, s32[4,256]{1,0:T(4,128)S(1)} %bitcast.14, f32[2,4096]{1,0:T(2,128)S(1)} %bitcast.12, ...), custom_call_target="tpu_custom_call" | custom-call | tf_op jit(solution)/shard_map/self_project/pallas_call | solution.py:458
  51.2 0.0 copy-done.1
  51.2 0.0 copy-done.4
  51.2 0.0 copy-done.5
  51.2 65.0 %cross_project.1 = (f32[256,512]{1,0:T(8,128)S(1)}, bf16[4,256,128]{2,1,0:T(8,128)(2,1)S(1)}, bf16[4,4,256,128]{3,2,1,0:T(8,128)(2,1)S(1)}, bf16[8,16,32,256]{3,2,1,0:T(8,128)(2,1)S(1)}) custom-call(s32[3]{0:T(128)S(1)} %copy-done.4, s32[3]{0:T(128)S(1)} %copy-done.5, bf16[4,256,128]{2,1,0:T(8,128)(2,1)S(1)} %get-tuple-element.13.q_ref, ...), custom_call_target="tpu_custom_call" | custom-call | tf_op jit(solution)/shard_map/cross_project/pallas_call | solution.py:709
  116.2 29.8 %output.1 = f32[256,512]{1,0:T(8,128)S(1)} custom-call(bf16[4,256,128]{2,1,0:T(8,128)(2,1)S(1)} %get-tuple-element.17.q_ref, bf16[4,4,256,128]{3,2,1,0:T(8,128)(2,1)S(1)} %get-tuple-element.18.kv_ref, bf16[8,16,32,256]{3,2,1,0:T(8,128)(2,1)S(1)} %get-tuple-element.19.w_ref, f32[256,512]{1,0:T(8,128)S(1)} %get-tuple-element.20.rows_ref), custom_call_target="tpu_custom_call" | custom-call | tf_op jit(solution)/shard_map/output/pallas_call | solution.py:777
  146.0 0.8 copy.10
Async XLA Ops:
  0.0 0.9 copy-start
  1.0 0.8 copy-start.2
  1.7 0.7 copy-start.3
  2.4 48.8 %copy-start.1 = (bf16[1,256,512]{2,1,0:T(8,128)(2,1)S(1)}, bf16[1,256,512]{2,1,0:T(8,128)(2,1)}, u32[]{:S(2)}) copy-start(bf16[1,256,512]{2,1,0:T(8,128)(2,1)} %param.8) | copy-start | bytes 786436
  2.4 48.8 %copy-start.4 = (s32[3]{0:T(128)S(1)}, s32[3]{0:T(128)}, u32[]{:S(2)}) copy-start(s32[3]{0:T(128)} %source_ref.1) | copy-start | bytes 40
  2.4 48.8 %copy-start.5 = (s32[3]{0:T(128)S(1)}, s32[3]{0:T(128)}, u32[]{:S(2)}) copy-start(s32[3]{0:T(128)} %target_ref.1) | copy-start | bytes 40

commit v7 on v6

--- a/solution.py
+++ b/solution.py
@@ -153,6 +153,84 @@
             own, onward = self.sends(h)
             for guard, copy in own + onward:
                 pl.when(guard)(copy.wait_send)
+            for p in range(4):
+                self.across(p, h).wait_send()
+
+
+class HopLine:
+    def __init__(self, at, buf, send, recv):
+        self.at, self.buf, self.send, self.recv = at, buf, send, recv
+
+    def copy(self, block, h, slot, device):
+        ref = self.buf.at[block, half(h)]
+        return remote(ref, ref, self.send.at[slot, h], self.recv.at[block, h], device)
+
+    def up(self, t, h):
+        return self.copy((self.at.p - t) * 2 + self.at.c, h, t, self.at.line(1))
+
+    def down(self, t, h):
+        return self.copy((self.at.p + t) * 2 + self.at.c, h, 3 + t, self.at.line(-1))
+
+    def across(self, p, h):
+        return self.copy(p * 2 + self.at.c, h, 6 + p, self.at.sibling())
+
+    def begin(self, h):
+        at = self.at
+
+        @pl.when(at.p < 3)
+        def _():
+            self.up(0, h).start()
+
+        @pl.when(at.p > 0)
+        def _():
+            self.down(0, h).start()
+
+        self.across(at.p, h).start()
+
+    def step(self, t, h):
+        at = self.at
+
+        @pl.when(at.p >= t)
+        def _():
+            self.up(t, h).wait_recv()
+
+            if t < 3:
+
+                @pl.when(at.p < 3)
+                def _():
+                    self.up(t, h).start()
+
+            self.across(at.p - t, h).start()
+
+        @pl.when(at.p <= 3 - t)
+        def _():
+            self.down(t, h).wait_recv()
+
+            if t < 3:
+
+                @pl.when(at.p > 0)
+                def _():
+                    self.down(t, h).start()
+
+            self.across(at.p + t, h).start()
+
+    def siblings(self, h):
+        for p in range(4):
+            self.copy(p * 2 + 1 - self.at.c, h, 6 + p, self.at.sibling()).wait_recv()
+
+    def finish(self):
+        at = self.at
+        for h in (0, 1):
+            for t in range(3):
+
+                @pl.when((at.p >= t) & (at.p < 3))
+                def _():
+                    self.up(t, h).wait_send()
+
+                @pl.when((at.p <= 3 - t) & (at.p > 0))
+                def _():
+                    self.down(t, h).wait_send()
+
             for p in range(4):
                 self.across(p, h).wait_send()
 
@@ -374,7 +452,7 @@
         ref = wc_out.at[(at.mp + 8 - d) % 8]
         return remote(ref, ref, wc_send.at[d], wc_recv.at[d], {"mp": (at.mp + d) % 8})
 
-    line = Line(at, buf, line_send, line_recv)
+    line = HopLine(at, buf, line_send, line_recv)
     kv_exchange = Exchange(at, kv4, kv_out.at[at.g], kv_send, kv_recv, 2)
     q_exchange = Exchange(at, q4, q_out, q_send, q_recv, 2)
     ring = Ring(at, kv_out, ring_send, ring_recv)
@@ -407,8 +485,8 @@
         wo_from(d).wait_recv()
     spread.start()
     line.step(2, 0)
+    line.step(1, 1)
     spread.forward()
-    line.step(1, 1)
     line.step(3, 0)
     load.wait()
     line.siblings(0)
@@ -535,16 +613,16 @@
     wait_all(peers)
     step(1)
     back.start(0)
+    after(0)
     step(2)
     collect(0)
     step(3)
     back.start(1)
-    after(0)
     line.step(1, 0)
+    after(1)
     line.step(2, 0)
     collect(1)
     line.step(3, 0)
-    after(1)
     line.step(1, 1)
     line.siblings(0)
     line.step(2, 1)
@@ -591,7 +669,7 @@
         rows_out[:, 128 * i : 128 * i + 128] = part
     back = Exchange(at, mixed, heads, back_send, back_recv, 2)
     mix_line = Line(at, mixed_buf, mix_send, mix_recv)
-    line = Line(at, buf, line_send, line_recv)
+    line = HopLine(at, buf, line_send, line_recv)
     spread = SecondSpread(at, wo_ref, wo, wo_send, wo_recv)
     first = FirstSpread(at, wc_part, g_send, g_recv)
     second = SecondSpread(at, wc_part, wc_out, a_send, a_recv)
@@ -613,17 +691,12 @@
             spread.start()
         elif n == 1:
             spread.forward()
-            pl.when(decoder)(first.start)
         elif n == 2:
             spread.finish()
-            pl.when(decoder)(first.forward)
+            pl.when(decoder)(first.start)
         else:
             line.step(1, 0)
-
-            @pl.when(decoder)
-            def _():
-                first.finish()
-                second.start()
+            pl.when(decoder)(first.forward)
 
     @pl.when(encoder)
     def _():
@@ -634,11 +707,15 @@
     line.step(2, 0)
     line.step(1, 1)
 
+    @pl.when(decoder)
+    def _():
+        first.finish()
+        second.start()
+
     line.step(3, 0)
     line.step(2, 1)
     load.wait()
     line.siblings(0)
-    pl.when(decoder)(second.forward)
 
     def over(d, h):
         rows = half(h)
@@ -678,6 +755,7 @@
 
     send_heads(0)
     line.step(3, 1)
+    pl.when(decoder)(second.forward)
     line.siblings(1)
     send_heads(1)
     line.finish()

time: 147 us -> 138 us (0.939)
  Pallas kernels: 144 us -> 134 us
    pallas_call x1, Pallas kernels: 48.7 us -> 41.5 us  [self_project(): pl.pallas_call(self_kernel, out_shape=(jax.ShapeDtypeStruct((4, ROWS, 128...]
    pallas_call x1, Pallas kernels: 65 us -> 60.8 us  [cross_project(): pl.pallas_call(cross_kernel, out_shape=(jax.ShapeDtypeStruct((ROWS, 512),...]
    pallas_call x1, Pallas kernels: 29.8 us -> 32 us  [output(): pl.pallas_call(output_kernel, out_shape=jax.ShapeDtypeStruct((ROWS, 512),...]
where the time goes in v7:
time: 138 us
  Pallas kernels  134 us (97%)
  local copies, waits for them, and re-layouts  3.2 us (2%)
    pallas_call x1, Pallas kernels, cross_project(): pl.pallas_call(cross_kernel, out_shape=(jax.ShapeDtypeStruct((ROWS, 512),...  60.8 us
    pallas_call x1, Pallas kernels, self_project(): pl.pallas_call(self_kernel, out_shape=(jax.ShapeDtypeStruct((4, ROWS, 128...  41.5 us
    pallas_call x1, Pallas kernels, output(): pl.pallas_call(output_kernel, out_shape=jax.ShapeDtypeStruct((ROWS, 512),...  32 us
    unnamed x13, local copies, waits for them, and re-layouts  3.2 us

profile of v7, /device:TPU:129, one launch (start us, length us, event | category | flops | bytes accessed | tf_op | source)
XLA Modules:
  0.0 137.5 jit_solution(14986900375613316892)
XLA Ops:
  0.0 0.0 copy-start
  0.0 0.9 copy-done
  1.0 0.0 copy-start.2
  1.0 0.8 copy-done.2
  1.7 0.0 copy-start.3
  1.7 0.7 copy-done.3
  2.4 0.0 copy-start.1
  2.4 0.0 copy-start.4
  2.4 0.0 copy-start.5
  2.4 41.5 %self_project.1 = (bf16[4,256,128]{2,1,0:T(8,128)(2,1)S(1)}, bf16[4,4,256,128]{3,2,1,0:T(8,128)(2,1)S(1)}, bf16[4,8,16,512]{3,2,1,0:T(8,128)(2,1)S(1)}, bf16[8,32,256]{2,1,0:T(8,128)(2,1)S(1)}) custom-call(bf16[256,512]{1,0:T(8,128)(2,1)S(1)} %bitcast.10, s32[4,256]{1,0:T(4,128)S(1)} %bitcast.14, f32[2,4096]{1,0:T(2,128)S(1)} %bitcast.12, ...), custom_call_target="tpu_custom_call" | custom-call | tf_op jit(solution)/shard_map/self_project/pallas_call | solution.py:536
  43.9 0.0 copy-done.1
  43.9 0.0 copy-done.4
  43.9 0.0 copy-done.5
  43.9 60.8 %cross_project.1 = (f32[256,512]{1,0:T(8,128)S(1)}, bf16[4,256,128]{2,1,0:T(8,128)(2,1)S(1)}, bf16[4,4,256,128]{3,2,1,0:T(8,128)(2,1)S(1)}, bf16[8,16,32,256]{3,2,1,0:T(8,128)(2,1)S(1)}) custom-call(s32[3]{0:T(128)S(1)} %copy-done.4, s32[3]{0:T(128)S(1)} %copy-done.5, bf16[4,256,128]{2,1,0:T(8,128)(2,1)S(1)} %get-tuple-element.13.q_ref, ...), custom_call_target="tpu_custom_call" | custom-call | tf_op jit(solution)/shard_map/cross_project/pallas_call | solution.py:787
  104.8 32.0 %output.1 = f32[256,512]{1,0:T(8,128)S(1)} custom-call(bf16[4,256,128]{2,1,0:T(8,128)(2,1)S(1)} %get-tuple-element.17.q_ref, bf16[4,4,256,128]{3,2,1,0:T(8,128)(2,1)S(1)} %get-tuple-element.18.kv_ref, bf16[8,16,32,256]{3,2,1,0:T(8,128)(2,1)S(1)} %get-tuple-element.19.w_ref, f32[256,512]{1,0:T(8,128)S(1)} %get-tuple-element.20.rows_ref), custom_call_target="tpu_custom_call" | custom-call | tf_op jit(solution)/shard_map/output/pallas_call | solution.py:855
  136.7 0.8 copy.10
Async XLA Ops:
  0.0 0.9 copy-start
  1.0 0.8 copy-start.2
  1.7 0.7 copy-start.3
  2.4 41.5 %copy-start.1 = (bf16[1,256,512]{2,1,0:T(8,128)(2,1)S(1)}, bf16[1,256,512]{2,1,0:T(8,128)(2,1)}, u32[]{:S(2)}) copy-start(bf16[1,256,512]{2,1,0:T(8,128)(2,1)} %param.8) | copy-start | bytes 786436
  2.4 41.5 %copy-start.4 = (s32[3]{0:T(128)S(1)}, s32[3]{0:T(128)}, u32[]{:S(2)}) copy-start(s32[3]{0:T(128)} %source_ref.1) | copy-start | bytes 40
  2.4 41.5 %copy-start.5 = (s32[3]{0:T(128)S(1)}, s32[3]{0:T(128)}, u32[]{:S(2)}) copy-start(s32[3]{0:T(128)} %target_ref.1) | copy-start | bytes 40

commit v8 on v7

--- a/solution.py
+++ b/solution.py
@@ -88,6 +88,7 @@
 
 
 HALF = ROWS // 2
+STEP = ROWS // 4
 
 
 def half(h):
@@ -238,7 +239,7 @@
 class Exchange:
     def __init__(self, at, src, dst, send, recv, pieces):
         self.at, self.src, self.dst, self.send, self.recv = at, src, dst, send, recv
-        self.rows = ROWS // pieces
+        self.rows = src.shape[1] // pieces
 
     def to(self, d, k):
         at, rows = self.at, pl.ds(k * self.rows, self.rows)
@@ -373,20 +374,21 @@
                 self.hop(1, d, 2, 3).wait_send()
 
 
-def pair_heads(first, second, dst, h):
-    low = lax.broadcasted_iota(jnp.int32, (HALF, 128), 1) < 64
-    rows = half(h)
+def pair_heads(first, second, dst, rows):
+    low = lax.broadcasted_iota(jnp.int32, (first.shape[0], 128), 1) < 64
     for pair in (0, 1):
         columns = slice(pair * 128, pair * 128 + 128)
-        f = first[:, columns]
-        f_turned = pltpu.roll(f, 64, 1)
-        if second is None:
-            s = s_turned = jnp.zeros_like(f)
-        else:
-            s = second[:, columns]
-            s_turned = pltpu.roll(s, 64, 1)
-        dst[2 * pair, rows] = jnp.where(low, f, s_turned).astype(BF16)
-        dst[2 * pair + 1, rows] = jnp.where(low, f_turned, s).astype(BF16)
+        f, s = first[:, columns], second[:, columns]
+        dst[2 * pair, rows] = jnp.where(low, f, pltpu.roll(s, 64, 1)).astype(BF16)
+        dst[2 * pair + 1, rows] = jnp.where(low, pltpu.roll(f, 64, 1), s).astype(BF16)
+
+
+def packed(h):
+    return pl.ds(h * STEP, STEP)
+
+
+def pack_queries(queries, dst, h):
+    pair_heads(queries[:STEP], queries[STEP:], dst, packed(h))
 
 
 def decoded(mantissa_ref, exponent_ref):
@@ -461,9 +463,9 @@
     def heads(h):
         scale = project(h, buf, gain_ref, 0, w_vmem, acc, 3)
         rows = half(h)
-        pair_heads(acc[1, rows] * scale, acc[2, rows] * scale, kv4, h)
+        pair_heads(acc[1, rows] * scale, acc[2, rows] * scale, kv4, rows)
         kv_exchange.start(h)
-        pair_heads(acc[0, rows] * (scale * QSCALE), None, q4, h)
+        pack_queries(acc[0, rows] * (scale * QSCALE), q4, h)
         q_exchange.start(h)
 
     def start_ring(h):
@@ -536,7 +538,7 @@
     return pl.pallas_call(
         self_kernel,
         out_shape=(
-            jax.ShapeDtypeStruct((4, ROWS, 128), BF16),
+            jax.ShapeDtypeStruct((4, HALF, 128), BF16),
             jax.ShapeDtypeStruct((4, 4, ROWS, 128), BF16),
             jax.ShapeDtypeStruct((4, 8, 16, 512), BF16),
             jax.ShapeDtypeStruct((8, 32, 256), BF16),
@@ -547,7 +549,7 @@
             pltpu.VMEM((8, ROWS, 512), BF16),
             pltpu.VMEM((3, 4096, 256), BF16),
             pltpu.VMEM((3, ROWS, 256), F32),
-            pltpu.VMEM((4, ROWS, 128), BF16),
+            pltpu.VMEM((4, HALF, 128), BF16),
             pltpu.VMEM((4, ROWS, 128), BF16),
             DMA,
             *dma((2,), (10, 2), (8, 2), (2, 4), (2, 4), (2, 4), (2, 4), (2, 3, 4), (2, 3, 4)),
@@ -558,12 +560,11 @@
     )(mantissas, exponents, gains, weights, wo, wc)
 
 
-STEP = ROWS // 4
-
-
 def attention_step(at, c, q_ref, kv_ref, scores, mixed, lengths):
     rows = pl.ds(c * STEP, STEP)
-    q = q_ref[:, rows, :].reshape(ROWS, 128)
+    both = q_ref[:, packed(c // 2), :].reshape(ROWS, 128).astype(F32)
+    low = lax.broadcasted_iota(jnp.int32, (ROWS, 128), 1) < 64
+    q = jnp.where(low, pltpu.roll(both, 64, 1) if c % 2 else both, 0.0).astype(BF16)
     if lengths is not None:
         index = lax.broadcasted_iota(jnp.int32, (ROWS, 128), 0)
         lane = lax.broadcasted_iota(jnp.int32, (ROWS, 128), 1)
@@ -728,11 +729,11 @@
         return remote(ref, ref, over_send.at[h, d], over_recv.at[h, d], over_device(d))
 
     def query(d, h):
-        rows = half(h)
+        rows = packed(h)
         return remote(q4.at[(at.a + d) % 4, rows], q_out.at[at.a, rows], q_send.at[h, d], q_recv.at[h, d], far_device(d))
 
     def query_from(d, h):
-        ref = q_out.at[(at.a + 4 - d) % 4, half(h)]
+        ref = q_out.at[(at.a + 4 - d) % 4, packed(h)]
         return remote(ref, ref, q_send.at[h, d], q_recv.at[h, d], far_device(d))
 
     ring = Ring(at, kv_out, ring_send, ring_recv)
@@ -743,13 +744,13 @@
 
         @pl.when(encoder)
         def _():
-            pair_heads(acc[0, rows] * scale, acc[1, rows] * scale, kv4, h)
+            pair_heads(acc[0, rows] * scale, acc[1, rows] * scale, kv4, rows)
             for d in range(4):
                 over(d, h).start()
 
         @pl.when(decoder)
         def _():
-            pair_heads(acc[0, rows] * (scale * QSCALE), None, q4, h)
+            pack_queries(acc[0, rows] * (scale * QSCALE), q4, h)
             for d in range(4):
                 query(d, h).start()
 
@@ -788,7 +789,7 @@
         cross_kernel,
         out_shape=(
             jax.ShapeDtypeStruct((ROWS, 512), F32),
-            jax.ShapeDtypeStruct((4, ROWS, 128), BF16),
+            jax.ShapeDtypeStruct((4, HALF, 128), BF16),
             jax.ShapeDtypeStruct((4, 4, ROWS, 128), BF16),
             jax.ShapeDtypeStruct((8, 16, 32, 256), BF16),
         ),
@@ -804,7 +805,7 @@
             pltpu.VMEM((4, 8, 32, 256), BF16),
             pltpu.VMEM((2, 4096, 256), BF16),
             pltpu.VMEM((2, ROWS, 256), F32),
-            pltpu.VMEM((4, ROWS, 128), BF16),
+            pltpu.VMEM((4, HALF, 128), BF16),
             pltpu.VMEM((4, ROWS, 128), BF16),
             DMA,
             *dma((2, 4), (2, 4), (10, 2), (8, 2), (10, 2), (8, 2), (2, 4), (2, 4)),

time: 138 us -> 137 us (level)
    unnamed x13 -> x17, local copies, waits for them, and re-layouts: 3.2 us -> 3.21 us
where the time goes in v8:
time: 137 us
  Pallas kernels  134 us (98%)
  local copies, waits for them, and re-layouts  3.21 us (2%)
    pallas_call x1, Pallas kernels, cross_project(): pl.pallas_call(cross_kernel, out_shape=(jax.ShapeDtypeStruct((ROWS, 512),...  59.6 us
    pallas_call x1, Pallas kernels, self_project(): pl.pallas_call(self_kernel, out_shape=(jax.ShapeDtypeStruct((4, HALF, 128...  41.5 us
    pallas_call x1, Pallas kernels, output(): pl.pallas_call(output_kernel, out_shape=jax.ShapeDtypeStruct((ROWS, 512),...  32.5 us
    unnamed x17, local copies, waits for them, and re-layouts  3.21 us

profile of v8, /device:TPU:129, one launch (start us, length us, event | category | flops | bytes accessed | tf_op | source)
XLA Modules:
  0.0 136.9 jit_solution(558468837469163088)
XLA Ops:
  0.0 0.0 copy-start
  0.0 0.9 copy-done
  1.0 0.0 copy-start.2
  1.0 0.8 copy-done.2
  1.7 0.0 copy-start.4
  1.7 0.7 copy-done.4
  2.4 0.0 copy-start.1
  2.4 0.0 copy-start.3
  2.4 0.0 copy-start.5
  2.4 0.0 copy-start.6
  2.4 0.0 copy-start.7
  2.4 41.5 %self_project.1 = (bf16[4,128,128]{2,1,0:T(8,128)(2,1)S(1)}, bf16[4,4,256,128]{3,2,1,0:T(8,128)(2,1)S(1)}, bf16[4,8,16,512]{3,2,1,0:T(8,128)(2,1)S(1)}, bf16[8,32,256]{2,1,0:T(8,128)(2,1)S(1)}) custom-call(bf16[256,512]{1,0:T(8,128)(2,1)S(1)} %bitcast.10, s32[4,256]{1,0:T(4,128)S(1)} %bitcast.14, f32[2,4096]{1,0:T(2,128)S(1)} %bitcast.12, ...), custom_call_target="tpu_custom_call" | custom-call | tf_op jit(solution)/shard_map/self_project/pallas_call | solution.py:538
  43.9 0.0 copy-done.1
  43.9 0.0 copy-done.3
  43.9 0.0 copy-done.5
  44.0 0.0 copy-done.6
  44.0 0.0 copy-done.7
  44.0 59.6 %cross_project.1 = (f32[256,512]{1,0:T(8,128)S(1)}, bf16[4,128,128]{2,1,0:T(8,128)(2,1)S(1)}, bf16[4,4,256,128]{3,2,1,0:T(8,128)(2,1)S(1)}, bf16[8,16,32,256]{3,2,1,0:T(8,128)(2,1)S(1)}) custom-call(s32[3]{0:T(128)S(1)} %copy-done.6, s32[3]{0:T(128)S(1)} %copy-done.7, bf16[4,128,128]{2,1,0:T(8,128)(2,1)S(1)} %get-tuple-element.13.q_ref, ...), custom_call_target="tpu_custom_call" | custom-call | tf_op jit(solution)/shard_map/cross_project/pallas_call | solution.py:788
  103.6 32.5 %output.1 = f32[256,512]{1,0:T(8,128)S(1)} custom-call(bf16[4,128,128]{2,1,0:T(8,128)(2,1)S(1)} %get-tuple-element.17.q_ref, bf16[4,4,256,128]{3,2,1,0:T(8,128)(2,1)S(1)} %get-tuple-element.18.kv_ref, bf16[8,16,32,256]{3,2,1,0:T(8,128)(2,1)S(1)} %get-tuple-element.19.w_ref, f32[256,512]{1,0:T(8,128)S(1)} %get-tuple-element.20.rows_ref), custom_call_target="tpu_custom_call" | custom-call | tf_op jit(solution)/shard_map/output/pallas_call | solution.py:856
  136.1 0.8 copy.10
Async XLA Ops:
  0.0 0.9 copy-start
  1.0 0.8 copy-start.2
  1.7 0.7 copy-start.4
  2.4 41.5 %copy-start.1 = (bf16[1,256,512]{2,1,0:T(8,128)(2,1)S(1)}, bf16[1,256,512]{2,1,0:T(8,128)(2,1)}, u32[]{:S(2)}) copy-start(bf16[1,256,512]{2,1,0:T(8,128)(2,1)} %param.8) | copy-start | bytes 786436
  2.4 41.5 %copy-start.3 = (f32[1,2,4096]{2,1,0:T(2,128)S(1)}, f32[1,2,4096]{2,1,0:T(2,128)}, u32[]{:S(2)}) copy-start(f32[1,2,4096]{2,1,0:T(2,128)} %param.12) | copy-start | bytes 98308
  2.4 41.5 %copy-start.5 = (s32[1,256,4]{1,2,0:T(4,128)S(1)}, s32[1,256,4]{1,2,0:T(4,128)}, u32[]{:S(2)}) copy-start(s32[1,256,4]{1,2,0:T(4,128)} %param.9) | copy-start | bytes 12292
  2.4 41.6 %copy-start.6 = (s32[3]{0:T(128)S(1)}, s32[3]{0:T(128)}, u32[]{:S(2)}) copy-start(s32[3]{0:T(128)} %source_ref.1) | copy-start | bytes 40
  2.4 41.6 %copy-start.7 = (s32[3]{0:T(128)S(1)}, s32[3]{0:T(128)}, u32[]{:S(2)}) copy-start(s32[3]{0:T(128)} %target_ref.1) | copy-start | bytes 40

commit v9 on v8

--- a/solution.py
+++ b/solution.py
@@ -47,6 +47,8 @@
         self.sec = lax.axis_index("sec")
         self.p = self.mp // 2
         self.c = self.mp % 2
+        self.inner = (self.p == 1) | (self.p == 2)
+        self.outer = (self.p == 0) | (self.p == 3)
         y, x = self.seq // 4, self.seq % 4
         self.a = jnp.where(self.c == 0, y, x)
         self.g = jnp.where(self.c == 0, x, y)
@@ -491,9 +493,10 @@
     spread.forward()
     line.step(3, 0)
     load.wait()
+    pl.when(at.inner)(lambda: line.step(2, 1))
     line.siblings(0)
     heads(0)
-    line.step(2, 1)
+    pl.when(at.outer)(lambda: line.step(2, 1))
     start_ring(0)
     line.step(3, 1)
     line.siblings(1)
@@ -625,10 +628,11 @@
     collect(1)
     line.step(3, 0)
     line.step(1, 1)
+    pl.when(at.inner)(lambda: line.step(2, 1))
     line.siblings(0)
-    line.step(2, 1)
     after(2)
     product(0)
+    pl.when(at.outer)(lambda: line.step(2, 1))
     line.step(3, 1)
     line.siblings(1)
     product(1)
@@ -714,7 +718,7 @@
         second.start()
 
     line.step(3, 0)
-    line.step(2, 1)
+    pl.when(at.inner)(lambda: line.step(2, 1))
     load.wait()
     line.siblings(0)
 
@@ -755,6 +759,7 @@
                 query(d, h).start()
 
     send_heads(0)
+    pl.when(at.outer)(lambda: line.step(2, 1))
     line.step(3, 1)
     pl.when(decoder)(second.forward)
     line.siblings(1)

time: 137 us -> 137 us (level)
  no operation moved by 1% of the time
where the time goes in v9:
time: 137 us
  Pallas kernels  134 us (98%)
  local copies, waits for them, and re-layouts  3.21 us (2%)
    pallas_call x1, Pallas kernels, cross_project(): pl.pallas_call(cross_kernel, out_shape=(jax.ShapeDtypeStruct((ROWS, 512),...  59.9 us
    pallas_call x1, Pallas kernels, self_project(): pl.pallas_call(self_kernel, out_shape=(jax.ShapeDtypeStruct((4, HALF, 128...  41.5 us
    pallas_call x1, Pallas kernels, output(): pl.pallas_call(output_kernel, out_shape=jax.ShapeDtypeStruct((ROWS, 512),...  32.4 us
    unnamed x17, local copies, waits for them, and re-layouts  3.21 us

profile of v9, /device:TPU:129, one launch (start us, length us, event | category | flops | bytes accessed | tf_op | source)
XLA Modules:
  0.0 137.1 jit_solution(7797705954685800043)
XLA Ops:
  0.0 0.0 copy-start
  0.0 0.9 copy-done
  1.0 0.0 copy-start.2
  1.0 0.8 copy-done.2
  1.7 0.0 copy-start.4
  1.7 0.7 copy-done.4
  2.4 0.0 copy-start.1
  2.4 0.0 copy-start.3
  2.4 0.0 copy-start.5
  2.4 0.0 copy-start.6
  2.4 0.0 copy-start.7
  2.4 41.5 %self_project.1 = (bf16[4,128,128]{2,1,0:T(8,128)(2,1)S(1)}, bf16[4,4,256,128]{3,2,1,0:T(8,128)(2,1)S(1)}, bf16[4,8,16,512]{3,2,1,0:T(8,128)(2,1)S(1)}, bf16[8,32,256]{2,1,0:T(8,128)(2,1)S(1)}) custom-call(bf16[256,512]{1,0:T(8,128)(2,1)S(1)} %bitcast.10, s32[4,256]{1,0:T(4,128)S(1)} %bitcast.14, f32[2,4096]{1,0:T(2,128)S(1)} %bitcast.12, ...), custom_call_target="tpu_custom_call" | custom-call | tf_op jit(solution)/shard_map/self_project/pallas_call | solution.py:541
  43.9 0.0 copy-done.1
  43.9 0.0 copy-done.3
  44.0 0.0 copy-done.5
  44.0 0.0 copy-done.6
  44.0 0.0 copy-done.7
  44.0 59.9 %cross_project.1 = (f32[256,512]{1,0:T(8,128)S(1)}, bf16[4,128,128]{2,1,0:T(8,128)(2,1)S(1)}, bf16[4,4,256,128]{3,2,1,0:T(8,128)(2,1)S(1)}, bf16[8,16,32,256]{3,2,1,0:T(8,128)(2,1)S(1)}) custom-call(s32[3]{0:T(128)S(1)} %copy-done.6, s32[3]{0:T(128)S(1)} %copy-done.7, bf16[4,128,128]{2,1,0:T(8,128)(2,1)S(1)} %get-tuple-element.13.q_ref, ...), custom_call_target="tpu_custom_call" | custom-call | tf_op jit(solution)/shard_map/cross_project/pallas_call | solution.py:793
  103.9 32.4 %output.1 = f32[256,512]{1,0:T(8,128)S(1)} custom-call(bf16[4,128,128]{2,1,0:T(8,128)(2,1)S(1)} %get-tuple-element.17.q_ref, bf16[4,4,256,128]{3,2,1,0:T(8,128)(2,1)S(1)} %get-tuple-element.18.kv_ref, bf16[8,16,32,256]{3,2,1,0:T(8,128)(2,1)S(1)} %get-tuple-element.19.w_ref, f32[256,512]{1,0:T(8,128)S(1)} %get-tuple-element.20.rows_ref), custom_call_target="tpu_custom_call" | custom-call | tf_op jit(solution)/shard_map/output/pallas_call | solution.py:861
  136.3 0.8 copy.10
Async XLA Ops:
  0.0 0.9 copy-start
  1.0 0.8 copy-start.2
  1.7 0.7 copy-start.4
  2.4 41.5 %copy-start.1 = (bf16[1,256,512]{2,1,0:T(8,128)(2,1)S(1)}, bf16[1,256,512]{2,1,0:T(8,128)(2,1)}, u32[]{:S(2)}) copy-start(bf16[1,256,512]{2,1,0:T(8,128)(2,1)} %param.8) | copy-start | bytes 786436
  2.4 41.5 %copy-start.3 = (f32[1,2,4096]{2,1,0:T(2,128)S(1)}, f32[1,2,4096]{2,1,0:T(2,128)}, u32[]{:S(2)}) copy-start(f32[1,2,4096]{2,1,0:T(2,128)} %param.12) | copy-start | bytes 98308
  2.4 41.6 %copy-start.5 = (s32[1,256,4]{1,2,0:T(4,128)S(1)}, s32[1,256,4]{1,2,0:T(4,128)}, u32[]{:S(2)}) copy-start(s32[1,256,4]{1,2,0:T(4,128)} %param.9) | copy-start | bytes 12292
  2.4 41.6 %copy-start.6 = (s32[3]{0:T(128)S(1)}, s32[3]{0:T(128)}, u32[]{:S(2)}) copy-start(s32[3]{0:T(128)} %source_ref.1) | copy-start | bytes 40
  2.4 41.6 %copy-start.7 = (s32[3]{0:T(128)S(1)}, s32[3]{0:T(128)}, u32[]{:S(2)}) copy-start(s32[3]{0:T(128)} %target_ref.1) | copy-start | bytes 40

commit v10 on v9

--- a/solution.py
+++ b/solution.py
@@ -493,10 +493,9 @@
     spread.forward()
     line.step(3, 0)
     load.wait()
-    pl.when(at.inner)(lambda: line.step(2, 1))
     line.siblings(0)
     heads(0)
-    pl.when(at.outer)(lambda: line.step(2, 1))
+    line.step(2, 1)
     start_ring(0)
     line.step(3, 1)
     line.siblings(1)

time: 137 us -> 137 us (level)
  no operation moved by 1% of the time
where the time goes in v10:
time: 137 us; the launch traced here: 136 us
  Pallas kernels  133 us (97%)
  local copies, waits for them, and re-layouts  3.21 us (2%)
    pallas_call x1, Pallas kernels, cross_project(): pl.pallas_call(cross_kernel, out_shape=(jax.ShapeDtypeStruct((ROWS, 512),...  59.6 us
    pallas_call x1, Pallas kernels, self_project(): pl.pallas_call(self_kernel, out_shape=(jax.ShapeDtypeStruct((4, HALF, 128...  41.5 us
    pallas_call x1, Pallas kernels, output(): pl.pallas_call(output_kernel, out_shape=jax.ShapeDtypeStruct((ROWS, 512),...  31.8 us
    unnamed x17, local copies, waits for them, and re-layouts  3.21 us

profile of v10, /device:TPU:129, one launch (start us, length us, event | category | flops | bytes accessed | tf_op | source)
XLA Modules:
  0.0 136.2 jit_solution(11534850480571883312)
XLA Ops:
  0.0 0.0 copy-start
  0.0 0.9 copy-done
  1.0 0.0 copy-start.2
  1.0 0.8 copy-done.2
  1.7 0.0 copy-start.4
  1.7 0.7 copy-done.4
  2.4 0.0 copy-start.1
  2.4 0.0 copy-start.3
  2.4 0.0 copy-start.5
  2.4 0.0 copy-start.6
  2.4 0.0 copy-start.7
  2.4 41.5 %self_project.1 = (bf16[4,128,128]{2,1,0:T(8,128)(2,1)S(1)}, bf16[4,4,256,128]{3,2,1,0:T(8,128)(2,1)S(1)}, bf16[4,8,16,512]{3,2,1,0:T(8,128)(2,1)S(1)}, bf16[8,32,256]{2,1,0:T(8,128)(2,1)S(1)}) custom-call(bf16[256,512]{1,0:T(8,128)(2,1)S(1)} %bitcast.10, s32[4,256]{1,0:T(4,128)S(1)} %bitcast.14, f32[2,4096]{1,0:T(2,128)S(1)} %bitcast.12, ...), custom_call_target="tpu_custom_call" | custom-call | tf_op jit(solution)/shard_map/self_project/pallas_call | solution.py:540
  43.9 0.0 copy-done.1
  43.9 0.0 copy-done.3
  43.9 0.0 copy-done.5
  44.0 0.0 copy-done.6
  44.0 0.0 copy-done.7
  44.0 59.6 %cross_project.1 = (f32[256,512]{1,0:T(8,128)S(1)}, bf16[4,128,128]{2,1,0:T(8,128)(2,1)S(1)}, bf16[4,4,256,128]{3,2,1,0:T(8,128)(2,1)S(1)}, bf16[8,16,32,256]{3,2,1,0:T(8,128)(2,1)S(1)}) custom-call(s32[3]{0:T(128)S(1)} %copy-done.6, s32[3]{0:T(128)S(1)} %copy-done.7, bf16[4,128,128]{2,1,0:T(8,128)(2,1)S(1)} %get-tuple-element.13.q_ref, ...), custom_call_target="tpu_custom_call" | custom-call | tf_op jit(solution)/shard_map/cross_project/pallas_call | solution.py:792
  103.6 31.8 %output.1 = f32[256,512]{1,0:T(8,128)S(1)} custom-call(bf16[4,128,128]{2,1,0:T(8,128)(2,1)S(1)} %get-tuple-element.17.q_ref, bf16[4,4,256,128]{3,2,1,0:T(8,128)(2,1)S(1)} %get-tuple-element.18.kv_ref, bf16[8,16,32,256]{3,2,1,0:T(8,128)(2,1)S(1)} %get-tuple-element.19.w_ref, f32[256,512]{1,0:T(8,128)S(1)} %get-tuple-element.20.rows_ref), custom_call_target="tpu_custom_call" | custom-call | tf_op jit(solution)/shard_map/output/pallas_call | solution.py:860
  135.4 0.8 copy.10
Async XLA Ops:
  0.0 0.9 copy-start
  1.0 0.8 copy-start.2
  1.7 0.7 copy-start.4
  2.4 41.5 %copy-start.1 = (bf16[1,256,512]{2,1,0:T(8,128)(2,1)S(1)}, bf16[1,256,512]{2,1,0:T(8,128)(2,1)}, u32[]{:S(2)}) copy-start(bf16[1,256,512]{2,1,0:T(8,128)(2,1)} %param.8) | copy-start | bytes 786436
  2.4 41.5 %copy-start.3 = (f32[1,2,4096]{2,1,0:T(2,128)S(1)}, f32[1,2,4096]{2,1,0:T(2,128)}, u32[]{:S(2)}) copy-start(f32[1,2,4096]{2,1,0:T(2,128)} %param.12) | copy-start | bytes 98308
  2.4 41.5 %copy-start.5 = (s32[1,256,4]{1,2,0:T(4,128)S(1)}, s32[1,256,4]{1,2,0:T(4,128)}, u32[]{:S(2)}) copy-start(s32[1,256,4]{1,2,0:T(4,128)} %param.9) | copy-start | bytes 12292
  2.4 41.6 %copy-start.6 = (s32[3]{0:T(128)S(1)}, s32[3]{0:T(128)}, u32[]{:S(2)}) copy-start(s32[3]{0:T(128)} %source_ref.1) | copy-start | bytes 40
  2.4 41.6 %copy-start.7 = (s32[3]{0:T(128)S(1)}, s32[3]{0:T(128)}, u32[]{:S(2)}) copy-start(s32[3]{0:T(128)} %target_ref.1) | copy-start | bytes 40
